TPU v7x, 512 devices: a whole 4x4x16 slice. The times are simulated.
512 devices in a mesh: lat: 32 (over z, core), lon: 16 (over x, y).
Axes of the slice: x: 4, y: 4, z: 16, core: 2. Of those that a mesh axis runs over, the one named last changes fastest.
Arguments:
- state: float32 [6, 1, 512, 5760], P(None, None, 'lat', 'lon'), may hold values from -6 to 6
- zonal_wind: float32 [1, 512, 5760], P(None, 'lat', 'lon'), may hold values from -6 to 6
- meridional_wind: float32 [1, 512, 5760], P(None, 'lat', 'lon'), may hold values from -6 to 6
- filter_flag: int32 [512], replicated, may hold values from 0 to 1, as said below
- mode_count: int32 [512], replicated, may hold values from 0 to 360, as said below
Outputs:
- advanced: float32 [6, 1, 512, 5760], P(None, None, 'lat', 'lon')
Inputs may be any that keep to these rules, and one draw needn't show every extreme that they name: `filter_flag`: 0 outside the 128 latitudes nearest each pole; 1 at the latitude nearest each pole. `mode_count`: 0 outside the 128 latitudes nearest each pole, 1 or more inside them, 360 at the latitude nearest each pole.
All inputs are finite; a program needn't handle non-finite values.
Results may differ from a plain program's by a relative error of at most 0.00005.
Values sent between devices are 32-bit elements; how exact they have to be, the bound alone decides.
No kernel may reach another device: no remote copies, remote signals or barrier semaphores. Data moves between devices by JAX's collectives and lax.ppermute only.
A program may use at most 64 MiB of HBM per device.

v0:
```python
import math

import jax
import jax.numpy as jnp
from jax import lax
from jax.sharding import PartitionSpec as P

meridional_scale = 0.25
highest = lax.Precision.HIGHEST


def extended(block, sides, width, periodic):
    for axis, dim in sides:
        count = lax.axis_size(axis)
        forward = [(i, i + 1) for i in range(count - 1)]
        if periodic:
            forward.append((count - 1, 0))
        backward = [(target, source) for source, target in forward]
        low = lax.ppermute(
            lax.slice_in_dim(block, block.shape[dim] - width, None, axis=dim), axis, forward
        )
        high = lax.ppermute(lax.slice_in_dim(block, 0, width, axis=dim), axis, backward)
        block = jnp.concatenate([low, block, high], axis=dim)
    return block


def mode_damping(lat_flags, lat_counts, mode_start, width, kmax):
    ranks = mode_start + jnp.arange(width, dtype=jnp.int32)
    raised = jnp.maximum(ranks[None, :] - kmax + lat_counts[:, None] + 1, 0)
    scaled = raised.astype(jnp.float32) / jnp.maximum(lat_counts[:, None].astype(jnp.float32), 1.0)
    return scaled * lat_flags[:, None].astype(jnp.float32)


def mode_table(longitudes, circle, mode_start, width, kmax):
    wavenumbers = circle // 2 - kmax + mode_start + jnp.arange(width, dtype=jnp.int32)
    phase = (longitudes[:, None] * wavenumbers[None, :] % circle).astype(jnp.float32) * (
        2.0 * math.pi / circle
    )
    return jnp.concatenate([jnp.cos(phase), jnp.sin(phase)], axis=1)


def expand_back(weights, table):
    return lax.dot_general(
        weights,
        table,
        (((1,), (1,)), ((), ())),
        precision=highest,
        preferred_element_type=jnp.float32,
    )


def owner_damping(piece, lat_flags, lat_counts, circle, kmax):
    flat = piece.reshape(-1, circle)
    longitudes = jnp.arange(circle, dtype=jnp.int32)
    block_width = min(128, kmax)
    correction = jnp.zeros_like(flat)
    for mode_start in range(0, kmax, block_width):
        width = min(block_width, kmax - mode_start)
        table_block = mode_table(longitudes, circle, mode_start, width, kmax)
        weights = jnp.dot(flat, table_block, precision=highest, preferred_element_type=jnp.float32)
        damping = mode_damping(lat_flags, lat_counts, mode_start, width, kmax) * (2.0 / circle)
        damping = jnp.concatenate([damping, damping], axis=1)
        scaled = weights.reshape(piece.shape[0], piece.shape[1], 2 * width) * damping[None, :, :]
        correction = correction + expand_back(scaled.reshape(-1, 2 * width), table_block)
    return (flat - correction).reshape(piece.shape)


def run_damping(work, source_band, filter_flag, mode_count, lat_cells, circle):
    sectors = lax.axis_size("lon")
    kmax = circle // 16
    share = lat_cells // sectors
    first = source_band * lat_cells + lax.axis_index("lon") * share
    lat_flags = lax.dynamic_slice_in_dim(filter_flag, first, share)
    lat_counts = lax.dynamic_slice_in_dim(mode_count, first, share)
    finished = owner_damping(
        lax.all_to_all(work, "lon", split_axis=1, concat_axis=2, tiled=True),
        lat_flags,
        lat_counts,
        circle,
        kmax,
    )
    return lax.all_to_all(finished, "lon", split_axis=2, concat_axis=1, tiled=True)


def body(state, zonal_wind, meridional_wind, filter_flag, mode_count):
    field_count, level_count, lat_cells, lon_cells = state.shape
    item_count = field_count * level_count
    band_total = lax.axis_size("lat")
    nlat = lat_cells * band_total
    circle = lon_cells * lax.axis_size("lon")
    band_index = lax.axis_index("lat")
    fields = state.reshape(item_count, lat_cells, lon_cells)
    wide_fields, wide_wind = (
        extended(fields, (("lon", 2),), 1, True),
        extended(zonal_wind, (("lon", 2),), 1, True),
    )
    tall_fields, tall_wind = (
        extended(fields, (("lat", 1),), 1, False),
        extended(meridional_wind, (("lat", 1),), 1, False),
    )
    wide_q = wide_fields.reshape(field_count, level_count, lat_cells, lon_cells + 2)
    flux_east = wide_wind[None, :, :, :-1] * (0.5 * (wide_q[..., :-1] + wide_q[..., 1:]))
    zonal_diff = flux_east[..., 1:] - flux_east[..., :-1]
    face_ids = band_index * lat_cells - 1 + jnp.arange(lat_cells + 1, dtype=jnp.int32)
    face_metric = jnp.sin((face_ids + 1).astype(jnp.float32) * (math.pi / nlat))
    tall_q = tall_fields.reshape(field_count, level_count, lat_cells + 2, lon_cells)
    flux_north = (
        tall_wind[None, :, :-1, :]
        * face_metric[:, None]
        * (0.5 * (tall_q[..., :-1, :] + tall_q[..., 1:, :]))
    )
    merid_diff = flux_north[..., 1:, :] - flux_north[..., :-1, :]
    center_ids = band_index * lat_cells + jnp.arange(lat_cells, dtype=jnp.int32)
    center_angle = (center_ids.astype(jnp.float32) + 0.5) * (math.pi / nlat) - math.pi / 2
    center_metric = jnp.cos(center_angle)
    zonal_scale = math.sin(math.pi / (2 * nlat))
    increment = (
        -(zonal_scale / center_metric)[:, None] * zonal_diff
        - (meridional_scale / center_metric)[:, None] * merid_diff
    )
    increment = increment.reshape(item_count, lat_cells, lon_cells)
    filtered = run_damping(increment, band_index, filter_flag, mode_count, lat_cells, circle)
    advanced = fields + filtered
    return advanced.reshape(state.shape)


def solution(mesh):
    placed = (P(None, None, "lat", "lon"), P(None, "lat", "lon"), P(None, "lat", "lon"), P(), P())
    return jax.shard_map(
        body, mesh=mesh, in_specs=placed, out_specs=P(None, None, "lat", "lon"), check_vma=False
    )
```

profile of v0, /device:TPU:224, one launch (start us, length us, event | category | flops | bytes accessed | tf_op | source)
XLA Modules:
  0.0 160.8 jit_solution(17436939932593269840)
XLA Ops:
  1.0 1.9 %collective-permute-start.3 = (f32[6,1,360]{2,0,1:T(8,128)S(1)}, f32[6,1,360]{2,0,1:T(8,128)S(1)}, u32[]{:S(2)}, u32[]{:S(2)}) collective-permute-start(f32[6,1,360]{2,0,1:T(8,128)S(1)} %get-tuple-element.7), channel_id=1, source_target_pairs={{0,16},{16,32},{32,48},{48,64},{64,80},{80,96},{96,112},{112,128},... | collective-permute-start | bytes 25928 | tf_op jit(solution)/shard_map/ppermute | solution.py:19
  2.9 3.6 %collective-permute-start.4 = (f32[6,1,360]{2,0,1:T(8,128)S(1)}, f32[6,1,360]{2,0,1:T(8,128)S(1)}, u32[]{:S(2)}, u32[]{:S(2)}) collective-permute-start(f32[6,1,360]{2,0,1:T(8,128)S(1)} %get-tuple-element.8), channel_id=1, source_target_pairs={{16,0},{32,16},{48,32},{64,48},{80,64},{96,80},{112,96},{128,112},... | collective-permute-start | bytes 25928 | tf_op jit(solution)/shard_map/ppermute | solution.py:22
  7.3 3.4 %collective-permute-start.5 = (f32[1,1,360]{2,1,0:T(1,128)S(1)}, f32[1,1,360]{2,1,0:T(1,128)S(1)}, u32[]{:S(2)}, u32[]{:S(2)}) collective-permute-start(f32[1,1,360]{2,1,0:T(1,128)S(1)} %slice.55), channel_id=1, source_target_pairs={{0,16},{16,32},{32,48},{48,64},{64,80},{80,96},{96,112},{112,128},... | collective-permute-start | bytes 4328 | tf_op jit(solution)/shard_map/ppermute | solution.py:19
  10.8 3.5 %collective-permute-start = (f32[6,16,1]{2,0,1:T(8,128)S(1)}, f32[6,16,1]{2,0,1:T(8,128)S(1)}, u32[]{:S(2)}, u32[]{:S(2)}) collective-permute-start(f32[6,16,1]{2,0,1:T(8,128)S(1)} %get-tuple-element.5), channel_id=1, source_target_pairs={{0,1},{1,2},{2,3},{3,4},{4,5},{5,6},{6,7},{7,8},{8,9},{9,10},{10,1... | collective-permute-start | bytes 1160 | tf_op jit(solution)/shard_map/ppermute | solution.py:19
  15.0 3.5 %collective-permute-start.2 = (f32[1,16,1]{2,1,0:T(8,128)S(1)}, f32[1,16,1]{2,1,0:T(8,128)S(1)}, u32[]{:S(2)}, u32[]{:S(2)}) collective-permute-start(f32[1,16,1]{2,1,0:T(8,128)S(1)} %slice.48), channel_id=1, source_target_pairs={{0,1},{1,2},{2,3},{3,4},{4,5},{5,6},{6,7},{7,8},{8,9},{9,10},{10,1... | collective-permute-start | bytes 200 | tf_op jit(solution)/shard_map/ppermute | solution.py:19
  18.6 1.3 dynamic_slice.6
  23.1 13.1 %fusion.17 = (f32[5760,128]{1,0:T(8,128)S(1)}, f32[5760,128]{1,0:T(8,128)}) fusion(s32[128]{0:T(128)S(1)} %iota_add_fusion.2), kind=kLoop, calls=%fused_computation.27 | loop fusion | flops 6635520 | bytes 5898752 | tf_op jit(solution)/shard_map/cos | solution.py:39
  36.3 13.6 %fusion.13 = (f32[5760,128]{1,0:T(8,128)}, f32[5760,128]{1,0:T(8,128)}) fusion(s32[128]{0:T(128)S(1)} %iota_add_fusion.1), kind=kLoop, calls=%fused_computation.22 | loop fusion | flops 6635520 | bytes 5898752 | tf_op jit(solution)/shard_map/cos | solution.py:39
  49.8 12.0 %fusion.25 = (f32[5760,104]{0,1:T(8,128)}, f32[5760,104]{0,1:T(8,128)}) fusion(s32[104]{0:T(128)S(1)} %iota_add_fusion), kind=kLoop, calls=%fused_computation.36 | loop fusion | flops 5391360 | bytes 4792736 | tf_op jit(solution)/shard_map/cos | solution.py:39
  61.9 5.7 %collective-permute-start.1 = (f32[6,16,1]{2,0,1:T(8,128)S(1)}, f32[6,16,1]{2,0,1:T(8,128)S(1)}, u32[]{:S(2)}, u32[]{:S(2)}) collective-permute-start(f32[6,16,1]{2,0,1:T(8,128)S(1)} %get-tuple-element.6), channel_id=1, source_target_pairs={{1,0},{2,1},{3,2},{4,3},{5,4},{6,5},{7,6},{8,7},{9,8},{10,9},{11,1... | collective-permute-start | bytes 1160 | tf_op jit(solution)/shard_map/ppermute | solution.py:22
  67.7 1.8 %collective-permute-done.1 = f32[6,16,1]{2,0,1:T(8,128)S(1)} collective-permute-done((f32[6,16,1]{2,0,1:T(8,128)S(1)}, f32[6,16,1]{2,0,1:T(8,128)S(1)}, u32[]{:S(2)}, u32[]{:S(2)}) %collective-permute-start.1) | collective-permute-done | bytes 416 | tf_op jit(solution)/shard_map/ppermute | solution.py:22
  70.8 7.2 %all-to-all-start = ((f32[6,16,360]{2,0,1:T(8,128)}), f32[6,16,360]{2,0,1:T(8,128)S(1)}, u32[]{:S(2)}, u32[]{:S(2)}) async-start(f32[6,16,360]{2,0,1:T(8,128)} %fusion.33), calls=%async_computation | async-start | bytes 393216 | tf_op jit(solution)/shard_map/all_to_all | solution.py:76
  78.7 8.2 %all-to-all-done = f32[6,16,360]{2,0,1:T(8,128)S(1)} async-done(((f32[6,16,360]{2,0,1:T(8,128)}), f32[6,16,360]{2,0,1:T(8,128)S(1)}, u32[]{:S(2)}, u32[]{:S(2)}) %all-to-all-start) | async-done | bytes 138272 | tf_op jit(solution)/shard_map/all_to_all | solution.py:76
  87.1 4.4 %fusion.28 = f32[6,256]{1,0:T(8,128)S(1)} fusion(f32[6,5760]{1,0:T(8,128)S(1)} %reshape.246, f32[5760,128]{1,0:T(8,128)} %get-tuple-element.14, f32[5760,128]{1,0:T(8,128)S(1)} %get-tuple-element.13, f32[256]{0:T(256)S(1)} %bitcast.40), kind=kOutput, calls=%fused_computation.39 | convolution fusion | flops 107644416 | bytes 6043648 | tf_op jit(solution)/shard_map/dot_general | solution.py:60
  91.5 4.9 %fusion.3 = f32[6,5760]{1,0:T(8,128)S(1)} fusion(f32[6,256]{1,0:T(8,128)S(1)} %fusion.28, f32[5760,128]{1,0:T(8,128)S(1)} %copy-done, f32[5760,128]{1,0:T(8,128)S(1)} %get-tuple-element.13), kind=kOutput, calls=%fused_computation.7 | convolution fusion | flops 107642880 | bytes 6042624 | tf_op jit(solution)/shard_map/dot_general | solution.py:43
  96.5 2.4 %fusion.29 = f32[6,256]{1,0:T(8,128)S(1)} fusion(f32[6,5760]{1,0:T(8,128)S(1)} %reshape.246, f32[5760,128]{1,0:T(8,128)S(1)} %copy-done.2, f32[5760,128]{1,0:T(8,128)S(1)} %copy-done.1, f32[256]{0:T(256)S(1)} %bitcast.41), kind=kOutput, calls=%fused_computation.40 | convolution fusion | flops 107644416 | bytes 6043648 | tf_op jit(solution)/shard_map/dot_general | solution.py:60
  98.9 5.2 %convolution_add_fusion.1 = f32[6,5760]{1,0:T(8,128)S(1)} fusion(f32[6,5760]{1,0:T(8,128)S(1)} %fusion.3, f32[6,256]{1,0:T(8,128)S(1)} %fusion.29, f32[5760,128]{1,0:T(8,128)S(1)} %copy-done.2, f32[5760,128]{1,0:T(8,128)S(1)} %copy-done.1), kind=kOutput, calls=%fused_computation.1 | convolution fusion | flops 107677440 | bytes 6180864 | tf_op jit(solution)/shard_map/dot_general | solution.py:43
  104.1 3.9 %fusion.27 = f32[6,208]{1,0:T(8,128)S(1)} fusion(f32[6,5760]{1,0:T(8,128)S(1)} %reshape.246, f32[5760,104]{0,1:T(8,128)S(1)} %copy-done.4, f32[5760,104]{0,1:T(8,128)S(1)} %copy-done.3, f32[208]{0:T(256)S(1)} %bitcast.42), kind=kOutput, calls=%fused_computation.38 | convolution fusion | flops 87461088 | bytes 4936384 | tf_op jit(solution)/shard_map/dot_general | solution.py:60
  108.0 2.4 %fusion.1 = f32[6,1,5760]{2,0,1:T(8,128)S(1)} fusion(f32[6,5760]{1,0:T(8,128)S(1)} %reshape.246, f32[6,5760]{1,0:T(8,128)S(1)} %convolution_add_fusion.1, f32[6,208]{1,0:T(8,128)S(1)} %fusion.27, f32[5760,104]{0,1:T(8,128)S(1)} %copy-done.4, f32[5760,104]{0,1:T(8,128)S(1)} %copy-done.3), kind=kOutput, calls=%fused_computation.3 | convolution fusion | flops 87528960 | bytes 5212032 | tf_op jit(solution)/shard_map/dot_general | solution.py:43
  110.4 1.6 %copy.13 = f32[6,1,5760]{0,1,2:T(1,128)S(1)} copy(f32[6,1,5760]{2,0,1:T(8,128)S(1)} %fusion.1) | data formatting | bytes 276480 | tf_op jit(solution)/shard_map/reshape | solution.py:65
  112.6 26.7 %reduce = f32[5760,6]{1,0:T(8,128)} reduce(f32[5760,1,6]{2,1,0:T(1,128)S(1)} %bitcast.34, f32[]{:T(128)} %broadcast.355), dimensions={1}, to_apply=%bitcast.25.reduce_sub_computation | reduce | bytes 276484
  139.2 3.5 %reshape.248 = f32[16,1,2160]{2,1,0:T(1,128)S(1)} reshape(f32[5760,6]{1,0:T(8,128)} %reduce) | data formatting | bytes 276480
  142.7 11.4 %all_to_all.21 = f32[16,1,2160]{2,1,0:T(1,128)S(1)} all-to-all(f32[16,1,2160]{2,1,0:T(1,128)S(1)} %reshape.248), channel_id=1, replica_groups=mesh['lat'=32,'lon'=16] {'lon'}, dimensions={0} | all-to-all | bytes 276480 | tf_op jit(solution)/shard_map/all_to_all | solution.py:82
  155.1 4.1 %reshape.249 = f32[5760,1,6]{2,1,0:T(1,128)S(1)} reshape(f32[16,2160]{1,0:T(8,128)S(1)} %reduce.1) | data formatting | bytes 276480
  (50 shorter events, 9.8 us)
Async XLA Ops:
  1.0 68.9 %collective-permute-start.3 = (f32[6,1,360]{2,0,1:T(8,128)S(1)}, f32[6,1,360]{2,0,1:T(8,128)S(1)}, u32[]{:S(2)}, u32[]{:S(2)}) collective-permute-start(f32[6,1,360]{2,0,1:T(8,128)S(1)} %get-tuple-element.7), channel_id=1, source_target_pairs={{0,16},{16,32},{32,48},{48,64},{64,80},{80,96},{96,112},{112,128},... | collective-permute-start | bytes 25928 | tf_op jit(solution)/shard_map/ppermute | solution.py:19
  2.9 67.0 %collective-permute-start.4 = (f32[6,1,360]{2,0,1:T(8,128)S(1)}, f32[6,1,360]{2,0,1:T(8,128)S(1)}, u32[]{:S(2)}, u32[]{:S(2)}) collective-permute-start(f32[6,1,360]{2,0,1:T(8,128)S(1)} %get-tuple-element.8), channel_id=1, source_target_pairs={{16,0},{32,16},{48,32},{64,48},{80,64},{96,80},{112,96},{128,112},... | collective-permute-start | bytes 25928 | tf_op jit(solution)/shard_map/ppermute | solution.py:22
  7.3 62.5 %collective-permute-start.5 = (f32[1,1,360]{2,1,0:T(1,128)S(1)}, f32[1,1,360]{2,1,0:T(1,128)S(1)}, u32[]{:S(2)}, u32[]{:S(2)}) collective-permute-start(f32[1,1,360]{2,1,0:T(1,128)S(1)} %slice.55), channel_id=1, source_target_pairs={{0,16},{16,32},{32,48},{48,64},{64,80},{80,96},{96,112},{112,128},... | collective-permute-start | bytes 4328 | tf_op jit(solution)/shard_map/ppermute | solution.py:19
  10.8 57.0 %collective-permute-start = (f32[6,16,1]{2,0,1:T(8,128)S(1)}, f32[6,16,1]{2,0,1:T(8,128)S(1)}, u32[]{:S(2)}, u32[]{:S(2)}) collective-permute-start(f32[6,16,1]{2,0,1:T(8,128)S(1)} %get-tuple-element.5), channel_id=1, source_target_pairs={{0,1},{1,2},{2,3},{3,4},{4,5},{5,6},{6,7},{7,8},{8,9},{9,10},{10,1... | collective-permute-start | bytes 1160 | tf_op jit(solution)/shard_map/ppermute | solution.py:19
  15.0 46.9 %collective-permute-start.2 = (f32[1,16,1]{2,1,0:T(8,128)S(1)}, f32[1,16,1]{2,1,0:T(8,128)S(1)}, u32[]{:S(2)}, u32[]{:S(2)}) collective-permute-start(f32[1,16,1]{2,1,0:T(8,128)S(1)} %slice.48), channel_id=1, source_target_pairs={{0,1},{1,2},{2,3},{3,4},{4,5},{5,6},{6,7},{7,8},{8,9},{9,10},{10,1... | collective-permute-start | bytes 200 | tf_op jit(solution)/shard_map/ppermute | solution.py:19
  49.8 17.8 %copy-start.6 = (f32[1,16,360]{2,1,0:T(8,128)S(1)}, f32[1,16,360]{2,1,0:T(8,128)}, u32[]{:S(2)}) copy-start(f32[1,16,360]{2,1,0:T(8,128)} %param.6) | copy-start | bytes 69124
  49.8 20.0 %copy-start.7 = (f32[1,16,360]{2,1,0:T(8,128)S(1)}, f32[1,16,360]{2,1,0:T(8,128)}, u32[]{:S(2)}) copy-start(f32[1,16,360]{2,1,0:T(8,128)} %param.7) | copy-start | bytes 69124
  61.9 7.6 %collective-permute-start.1 = (f32[6,16,1]{2,0,1:T(8,128)S(1)}, f32[6,16,1]{2,0,1:T(8,128)S(1)}, u32[]{:S(2)}, u32[]{:S(2)}) collective-permute-start(f32[6,16,1]{2,0,1:T(8,128)S(1)} %get-tuple-element.6), channel_id=1, source_target_pairs={{1,0},{2,1},{3,2},{4,3},{5,4},{6,5},{7,6},{8,7},{9,8},{10,9},{11,1... | collective-permute-start | bytes 1160 | tf_op jit(solution)/shard_map/ppermute | solution.py:22
  70.8 16.2 %all-to-all-start = ((f32[6,16,360]{2,0,1:T(8,128)}), f32[6,16,360]{2,0,1:T(8,128)S(1)}, u32[]{:S(2)}, u32[]{:S(2)}) async-start(f32[6,16,360]{2,0,1:T(8,128)} %fusion.33), calls=%async_computation | async-start | bytes 393216 | tf_op jit(solution)/shard_map/all_to_all | solution.py:76
  87.1 4.4 %copy-start = (f32[5760,128]{1,0:T(8,128)S(1)}, f32[5760,128]{1,0:T(8,128)}, u32[]{:S(2)}) copy-start(f32[5760,128]{1,0:T(8,128)} %get-tuple-element.14) | copy-start | bytes 8847364
  91.5 5.0 %copy-start.1 = (f32[5760,128]{1,0:T(8,128)S(1)}, f32[5760,128]{1,0:T(8,128)}, u32[]{:S(2)}) copy-start(f32[5760,128]{1,0:T(8,128)} %get-tuple-element.11) | copy-start | bytes 8847364
  91.5 4.9 %copy-start.2 = (f32[5760,128]{1,0:T(8,128)S(1)}, f32[5760,128]{1,0:T(8,128)}, u32[]{:S(2)}) copy-start(f32[5760,128]{1,0:T(8,128)} %get-tuple-element.12) | copy-start | bytes 8847364
  98.9 5.2 %copy-start.3 = (f32[5760,104]{0,1:T(8,128)S(1)}, f32[5760,104]{0,1:T(8,128)}, u32[]{:S(2)}) copy-start(f32[5760,104]{0,1:T(8,128)} %get-tuple-element.9) | copy-start | bytes 7188484
  98.9 5.2 %copy-start.4 = (f32[5760,104]{0,1:T(8,128)S(1)}, f32[5760,104]{0,1:T(8,128)}, u32[]{:S(2)}) copy-start(f32[5760,104]{0,1:T(8,128)} %get-tuple-element.10) | copy-start | bytes 7188484
  155.1 5.0 %copy-start.5 = (f32[6,1,16,360]{3,2,1,0:T(8,128)S(1)}, f32[6,1,16,360]{3,2,1,0:T(8,128)}, u32[]{:S(2)}) copy-start(f32[6,1,16,360]{3,2,1,0:T(8,128)} %param.5) | copy-start | bytes 414724
where the time goes:
time: 161 us
  other arithmetic  69.8 us (43%)
  starting transfers between devices  28.8 us (18%)
  matrix products  23.2 us (14%)
  local copies, waits for them, and re-layouts  16 us (10%)
  blocking collectives  11.4 us (7%)
  waiting for transfers between devices  10 us (6%)
    cos x3, other arithmetic, mode_table(): return jnp.concatenate([jnp.cos(phase), jnp.sin(phase)], axis=1)  38.7 us
    unnamed x1, other arithmetic  26.7 us
    dot_general x3, matrix products, expand_back(): lax.dot_general(weights, table, (((1,), (1,)), ((), ())), precision=highe...  12.5 us
    ppermute x4, starting transfers between devices, extended(): lax.ppermute(lax.slice_in_dim(block, block.shape[dim] - width, None, axis...  12.3 us
    all_to_all x1, blocking collectives, run_damping(): lax.all_to_all(finished, 'lon', split_axis=2, concat_axis=1, tiled=True)  11.4 us
    dot_general x3, matrix products, owner_damping(): jnp.dot(flat, table_block, precision=highest, preferred_element_type=jnp....  10.7 us
    ppermute x2, starting transfers between devices, extended(): lax.ppermute(lax.slice_in_dim(block, 0, width, axis=dim), axis, backward)  9.32 us
    unnamed x20, local copies, waits for them, and re-layouts  9.12 us
  transfers between devices with their start and end apart: 7, of which 2 were waited for; matrix products, arithmetic and copies ran while one was open for 28% of the time, Pallas kernels for 0%

commit v1 on v0

v1 whole, which is shorter than its diff:
```python
import math

import jax
import jax.numpy as jnp
import ml_dtypes
import numpy as np
from jax import lax
from jax.experimental import pallas as pl
from jax.experimental.pallas import tpu as pltpu
from jax.sharding import PartitionSpec as P

meridional_scale = 0.25
SLABS = 3
SLAB = 120
POINTS = 48
ROWS = 8 * SLABS
GROUPS = 3


def mode_layout(circle, kmax):
    table = np.zeros((GROUPS, 256, 256), np.float64)
    reduced = np.full((GROUPS, 256), 1 << 20, np.int32)
    scale = np.zeros((GROUPS, 256), np.float64)
    b = np.arange(SLAB)
    sign = np.where(b % 2 == 0, 1.0, -1.0)
    for residue in range(POINTS // 2):
        group, place = divmod(residue, 8)
        if residue == 0:
            waves = [(48 * n, 0) for n in range(1, 8)] + [(24 + 48 * n, 128) for n in range(8)]
            factor = 2.0 / circle
        else:
            waves = [(residue + 48 * n, None) for n in range(-8, 8) if abs(residue + 48 * n) <= kmax]
            factor = 1.0 / circle
        for t, (k, row) in enumerate(waves):
            angle = 2.0 * np.pi * ((k * b) % circle) / circle
            cosine, sine = sign * np.cos(angle), sign * np.sin(angle)
            re, im = 32 * place + t, 32 * place + 16 + t
            if row is None:
                table[group, :SLAB, re], table[group, 128 : 128 + SLAB, re] = cosine, sine
                table[group, :SLAB, im], table[group, 128 : 128 + SLAB, im] = -sine, cosine
            else:
                table[group, row : row + SLAB, re] = cosine
                table[group, row : row + SLAB, im] = -sine
            reduced[group, [re, im]] = abs(k)
            scale[group, [re, im]] = factor
    high = table.astype(np.float32).astype(ml_dtypes.bfloat16)
    low = (table - high.astype(np.float64)).astype(np.float32).astype(ml_dtypes.bfloat16)
    return high, low, reduced, scale.astype(np.float32)


def c_add(x, y):
    return (x[0] + y[0], y[1] if x[1] is None else x[1] if y[1] is None else x[1] + y[1])


def c_sub(x, y):
    if y[1] is None:
        return (x[0] - y[0], x[1])
    return (x[0] - y[0], -y[1] if x[1] is None else x[1] - y[1])


def c_conj(x):
    return (x[0], None if x[1] is None else -x[1])


def c_turn(x, numer, denom):
    numer %= denom
    eighth = 8 * numer
    if numer == 0:
        return x
    if 2 * numer == denom:
        return (-x[0], None if x[1] is None else -x[1])
    if 4 * numer == denom:
        return (jnp.zeros_like(x[0]) if x[1] is None else -x[1], x[0])
    if 4 * numer == 3 * denom:
        return (jnp.zeros_like(x[0]) if x[1] is None else x[1], -x[0])
    angle = 2.0 * math.pi * numer / denom
    c, s = math.cos(angle), math.sin(angle)
    if x[1] is None:
        return (x[0] * c, x[0] * s)
    if eighth in (denom, 3 * denom, 5 * denom, 7 * denom):
        h = math.sqrt(0.5)
        a, b = (x[0] - x[1]) * h, (x[0] + x[1]) * h
        return {1: (a, b), 3: (-b, a), 5: (-a, -b), 7: (b, -a)}[eighth // denom]
    return (x[0] * c - x[1] * s, x[0] * s + x[1] * c)


def rfft(x):
    count = len(x)
    if count == 1:
        return [(x[0], None)]
    if count == 2:
        return [(x[0] + x[1], None), (x[0] - x[1], None)]
    even, odd = rfft(x[0::2]), rfft(x[1::2])
    result = [None] * (count // 2 + 1)
    for k in range(count // 4 + 1):
        turned = c_turn(odd[k], -k, count)
        result[k] = c_add(even[k], turned)
        if k != count // 4 or count == 2:
            result[count // 2 - k] = c_conj(c_sub(even[k], turned))
    return result


def irfft(z):
    count = 2 * (len(z) - 1)
    if count == 2:
        return [z[0][0] + z[1][0], z[0][0] - z[1][0]]
    even, odd = [], []
    for k in range(count // 4 + 1):
        mirror = c_conj(z[count // 2 - k])
        even.append(c_add(z[k], mirror))
        odd.append(c_turn(c_sub(z[k], mirror), k, count))
    result = [None] * count
    result[0::2], result[1::2] = irfft(even), irfft(odd)
    return result


def circle_forward(x):
    parts = [rfft(x[a::3]) for a in range(3)]
    result = [None] * 25
    half, root = 0.5, math.sqrt(3.0) / 2.0
    for k in range(9):
        t0 = parts[0][k]
        t1, t2 = c_turn(parts[1][k], -k, 48), c_turn(parts[2][k], -2 * k, 48)
        total, gap = c_add(t1, t2), c_sub(t1, t2)
        result[k] = c_add(t0, total)
        mid = (t0[0] - half * total[0], None if t0[1] is None and total[1] is None else
               (t0[1] if total[1] is None else (0.0 if t0[1] is None else t0[1]) - half * total[1]))
        turn = (None if gap[1] is None else root * gap[1], -root * gap[0])
        plus_re = mid[0] if turn[0] is None else mid[0] + turn[0]
        plus_im = turn[1] if mid[1] is None else mid[1] + turn[1]
        minus_re = mid[0] if turn[0] is None else mid[0] - turn[0]
        minus_im = -turn[1] if mid[1] is None else mid[1] - turn[1]
        if k + 16 <= 24:
            result[k + 16] = (plus_re, plus_im)
        if k > 0 and 16 - k != k + 16 and result[16 - k] is None:
            result[16 - k] = (minus_re, -minus_im)
    return result


def circle_backward(z):
    half, root = 0.5, math.sqrt(3.0) / 2.0
    spectra = [[], [], []]
    for k in range(9):
        t0 = z[k]
        t1 = z[k + 16] if k + 16 <= 24 else c_conj(z[32 - k])
        t2 = c_conj(z[16 - k])
        total, gap = c_add(t1, t2), c_sub(t1, t2)
        if k == 0:
            total, gap = (2.0 * t1[0], None), (None, 2.0 * t1[1])
        spectra[0].append(c_add(t0, total))
        mid = (t0[0] - half * total[0],
               t0[1] if total[1] is None else (-half * total[1] if t0[1] is None else t0[1] - half * total[1]))
        turn = (-root * gap[1], None if gap[0] is None else root * gap[0])
        plus = c_add(mid, turn)
        minus = c_sub(mid, turn)
        spectra[1].append(c_turn(plus, k, 48))
        spectra[2].append(c_turn(minus, 2 * k, 48))
    result = [None] * 48
    for a in range(3):
        result[a::3] = irfft(spectra[a])
    return result


def increment_kernel(state, zonal, merid, south, north, metric, chunks, pad):
    fields, rows, cells = state.shape
    wide = 128 * SLABS
    for f in range(fields + 2):
        pad[f, :, wide - 128 :] = jnp.zeros((rows, 128), jnp.float32)
    for f in range(fields):
        pad[f, :, :cells] = state[f]
    pad[fields, :, :cells] = zonal[...]
    pad[fields + 1, :, :cells] = merid[...]
    lane = lax.broadcasted_iota(jnp.int32, (rows, wide), 1)
    row = lax.broadcasted_iota(jnp.int32, (rows, wide), 0)
    short = lane[:, :128]

    def spread(index):
        part = metric[index]
        return jnp.concatenate([part] * SLABS, axis=1)

    zonal_factor, merid_factor, face, face_before = (spread(i) for i in range(4))
    east_wind = pad[fields]
    last_wind = pltpu.roll(east_wind, 3, 1)
    inner_wind = jnp.where(lane < cells - 1, east_wind, 0.0)
    north_wind = pad[fields + 1] * face
    south_wind = south[fields : fields + 1, :] * face_before[0:1, :]
    for f in range(fields):
        q = pad[f]
        flux_east = inner_wind * (0.5 * (q + pltpu.roll(q, wide - 1, 1)))
        zonal_diff = flux_east - pltpu.roll(flux_east, 1, 1)
        q_north = jnp.where(row == rows - 1, north[f : f + 1, :], pltpu.roll(q, rows - 1, 0))
        flux_north = north_wind * (0.5 * (q + q_north))
        flux_first = south_wind * (0.5 * (south[f : f + 1, :] + q[0:1, :]))
        merid_diff = flux_north - jnp.where(row == 0, flux_first, pltpu.roll(flux_north, 1, 0))
        part = -zonal_factor * zonal_diff - merid_factor * merid_diff
        part = jnp.where(lane == cells, pltpu.roll(q, cells, 1), part)
        part = jnp.where(lane == cells + 1, pltpu.roll(q, 2, 1), part)
        part = jnp.where(lane == cells + 2, last_wind, part)
        v0, v1, v2 = part[:, :128], part[:, 128:256], part[:, 256:]
        slabs = (
            v0,
            jnp.where(short < 8, pltpu.roll(v0, 8, 1), pltpu.roll(v1, 8, 1)),
            jnp.where(short < 16, pltpu.roll(v1, 16, 1), pltpu.roll(v2, 16, 1)),
        )
        for a in range(SLABS):
            chunks[pl.ds(8 * a + f, rows, stride=ROWS), :] = slabs[a]
    for f in range(fields, 8):
        for a in range(SLABS):
            chunks[pl.ds(8 * a + f, rows, stride=ROWS), :] = jnp.zeros((rows, 128), jnp.float32)


def split(x):
    high = x.astype(jnp.bfloat16)
    return high, (x - high.astype(jnp.float32)).astype(jnp.bfloat16)


def product(x, high, low, dims):
    def dot(p, q):
        return lax.dot_general(p, q, (dims, ((), ())), preferred_element_type=jnp.float32)

    x_high, x_low = split(x)
    return dot(x_high, high) + (dot(x_low, high) + dot(x_high, low))


def filter_kernel(chunks, own, damping, high, low, result):
    sectors = chunks.shape[0]
    lane = lax.broadcasted_iota(jnp.int32, (8, 128), 1)
    zonal_factor = own[...]
    points = [chunks[p // 3, 8 * (p % 3) : 8 * (p % 3) + 8, :] for p in range(POINTS)]
    lasts = [points[3 * s + 2] for s in range(sectors)]
    for s in range(sectors):
        after = (s + 1) % sectors
        flux = pltpu.roll(lasts[s], 125, 1) * (
            0.5 * (pltpu.roll(lasts[s], 126, 1) + pltpu.roll(lasts[after], 127, 1))
        )
        edge = jnp.where(lane == SLAB - 1, zonal_factor * flux, 0.0)
        points[3 * s + 2] = points[3 * s + 2] - edge
        points[3 * after] = points[3 * after] + pltpu.roll(edge, 128 - (SLAB - 1), 1)
    for p in range(POINTS):
        result[p // 3, 8 * (p % 3) : 8 * (p % 3) + 8, :] = points[p]
    spectrum = circle_forward(points)
    spectrum[0] = (spectrum[0][0], spectrum[24][0])
    block = lax.broadcasted_iota(jnp.int32, (64, 256), 0) // 8
    column = lax.broadcasted_iota(jnp.int32, (64, 256), 1) // 32
    back = [None] * 25
    for g in range(GROUPS):
        rows = jnp.concatenate(
            [jnp.concatenate(spectrum[8 * g + i], axis=1) for i in range(8)], axis=0
        )
        modes = product(rows, high[g], low[g], ((1,), (0,)))
        modes = jnp.where(block == column, modes * damping[g : g + 1, :], 0.0)
        rows = product(modes, high[g], low[g], ((1,), (1,)))
        for i in range(8):
            part = rows[8 * i : 8 * i + 8, :]
            back[8 * g + i] = (part[:, :128], part[:, 128:])
    back[24] = (back[0][1], None)
    back[0] = (back[0][0], None)
    correction = circle_backward(back)
    for p in range(POINTS):
        place = (p // 3, slice(8 * (p % 3), 8 * (p % 3) + 8), slice(None))
        result[place] = result[place] - correction[p]


def final_kernel(chunks, state, advanced):
    fields, rows, cells = state.shape
    lane = lax.broadcasted_iota(jnp.int32, (rows, 128), 1)
    for f in range(fields):
        s0, s1, s2 = (chunks[pl.ds(8 * a + f, rows, stride=ROWS), :] for a in range(SLABS))
        s1, s2 = pltpu.roll(s1, 120, 1), pltpu.roll(s2, 112, 1)
        advanced[f, :, :128] = state[f, :, :128] + jnp.where(lane < 120, s0, s1)
        advanced[f, :, 128:256] = state[f, :, 128:256] + jnp.where(lane < 112, s1, s2)
        advanced[f, :, 256:] = state[f, :, 256:] + s2[:, : cells - 256]


def in_vmem(count):
    return [pl.BlockSpec(memory_space=pltpu.VMEM)] * count


def body(state, zonal_wind, meridional_wind, filter_flag, mode_count):
    field_count, level_count, lat_cells, lon_cells = state.shape
    item_count = field_count * level_count
    band_total, sectors = lax.axis_size("lat"), lax.axis_size("lon")
    nlat, circle = lat_cells * band_total, lon_cells * sectors
    band_index = lax.axis_index("lat")
    wide = 128 * SLABS
    fields = state.reshape(item_count, lat_cells, lon_cells)
    zonal, merid = (w.reshape(lat_cells, lon_cells) for w in (zonal_wind, meridional_wind))

    forward = [(i, i + 1) for i in range(band_total - 1)]
    backward = [(target, source) for source, target in forward]
    top = jnp.concatenate([fields[:, -1], merid[-1:]], axis=0)
    top = jnp.pad(top, ((0, 8 - item_count - 1), (0, wide - lon_cells)))
    bottom = jnp.pad(fields[:, 0], ((0, 8 - item_count), (0, wide - lon_cells)))
    south = lax.ppermute(top, "lat", forward)
    north = lax.ppermute(bottom, "lat", backward)

    zonal_scale = math.sin(math.pi / (2 * nlat))

    def center_metric(ids):
        return jnp.cos((ids.astype(jnp.float32) + 0.5) * (math.pi / nlat) - math.pi / 2)

    def face_metric(ids):
        return jnp.sin((ids.astype(jnp.float32) + 1.0) * (math.pi / nlat))

    ids = band_index * lat_cells + jnp.arange(lat_cells, dtype=jnp.int32)
    center = center_metric(ids)
    metric = jnp.stack(
        [zonal_scale / center, meridional_scale / center, face_metric(ids), face_metric(ids - 1)]
    )
    metric = jnp.broadcast_to(metric[:, :, None], (4, lat_cells, 128))

    high, low, reduced, scale = mode_layout(circle, circle // 16)
    own_row = band_index * lat_cells + lax.axis_index("lon")
    chosen = jnp.arange(nlat, dtype=jnp.int32) == own_row
    flag = jnp.sum(jnp.where(chosen, filter_flag, 0))
    count = jnp.sum(jnp.where(chosen, mode_count, 0))
    raised = jnp.maximum(count + 1 - jnp.asarray(reduced), 0).astype(jnp.float32)
    damping = raised / jnp.maximum(count.astype(jnp.float32), 1.0) * flag.astype(jnp.float32)
    damping = damping * jnp.asarray(scale)
    own = jnp.broadcast_to(zonal_scale / center_metric(own_row), (8, 128))

    chunks = pl.pallas_call(
        increment_kernel,
        out_shape=jax.ShapeDtypeStruct((sectors * ROWS, 128), jnp.float32),
        in_specs=in_vmem(6),
        out_specs=pl.BlockSpec(memory_space=pltpu.VMEM),
        scratch_shapes=[pltpu.VMEM((8, lat_cells, wide), jnp.float32)],
        name="increments",
    )(fields, zonal, merid, south, north, metric)
    chunks = lax.all_to_all(chunks.reshape(sectors, ROWS, 128), "lon", 0, 0, tiled=True)
    chunks = pl.pallas_call(
        filter_kernel,
        out_shape=jax.ShapeDtypeStruct((sectors, ROWS, 128), jnp.float32),
        in_specs=in_vmem(5),
        out_specs=pl.BlockSpec(memory_space=pltpu.VMEM),
        name="filter_rows",
    )(chunks, own, damping, jnp.asarray(high), jnp.asarray(low))
    chunks = lax.all_to_all(chunks, "lon", 0, 0, tiled=True)
    advanced = pl.pallas_call(
        final_kernel,
        out_shape=jax.ShapeDtypeStruct((item_count, lat_cells, lon_cells), jnp.float32),
        in_specs=in_vmem(2),
        out_specs=pl.BlockSpec(memory_space=pltpu.VMEM),
        name="advance",
    )(chunks.reshape(sectors * ROWS, 128), fields)
    return advanced.reshape(state.shape)


def solution(mesh):
    placed = (P(None, None, "lat", "lon"), P(None, "lat", "lon"), P(None, "lat", "lon"), P(), P())
    return jax.shard_map(
        body, mesh=mesh, in_specs=placed, out_specs=P(None, None, "lat", "lon"), check_vma=False
    )
```

time: 161 us -> 48.2 us (0.30)
  the two profiles are of different devices: /device:TPU:224 before, /device:TPU:384 now
where the time goes in v1:
time: 48.2 us; the launch traced here: 47.6 us
  starting transfers between devices  13.9 us (29%)
  blocking collectives  12.3 us (26%)
  waiting for transfers between devices  7.45 us (15%)
  Pallas kernels  6.69 us (14%)
  local copies, waits for them, and re-layouts  3.7 us (8%)
  between operations  2.17 us (5%)
  other arithmetic  1.42 us (3%)
    all_to_all x1, blocking collectives, body(): chunks = lax.all_to_all(chunks, 'lon', 0, 0, tiled=True)  12.3 us
    all_to_all x1, waiting for transfers between devices, body(): lax.all_to_all(chunks.reshape(sectors, ROWS, 128), 'lon', 0, 0, tiled=True)  7.45 us
    all_to_all x1, starting transfers between devices, body(): lax.all_to_all(chunks.reshape(sectors, ROWS, 128), 'lon', 0, 0, tiled=True)  7.17 us
    ppermute x1, starting transfers between devices, body(): north = lax.ppermute(bottom, 'lat', backward)  4.85 us
    pallas_call x1, Pallas kernels, body(): pl.pallas_call(filter_kernel, out_shape=jax.ShapeDtypeStruct((sectors, RO...  2.97 us
    pallas_call x1, Pallas kernels, body(): pl.pallas_call(increment_kernel, out_shape=jax.ShapeDtypeStruct((sectors...  1.96 us
    ppermute x1, starting transfers between devices, body(): south = lax.ppermute(top, 'lat', forward)  1.92 us
    pallas_call x1, Pallas kernels, body(): pl.pallas_call(final_kernel, out_shape=jax.ShapeDtypeStruct((item_count,...  1.76 us
  transfers between devices with their start and end apart: 3, of which 1 were waited for; matrix products, arithmetic and copies ran while one was open for 3% of the time, Pallas kernels for 0%

profile of v1, /device:TPU:384, one launch (start us, length us, event | category | flops | bytes accessed | tf_op | source)
XLA Modules:
  0.0 47.6 jit_solution(7959234555979696246)
XLA Ops:
  0.0 0.9 %fusion.5 = (f32[6,1,360]{2,1,0:T(1,128)S(1)}, f32[6,1,360]{2,1,0:T(1,128)S(1)}) fusion(f32[6,16,360]{2,1,0:T(8,128)} %bitcast.18), kind=kLoop, calls=%fused_computation.21 | loop fusion | bytes 34560 | tf_op jit(solution)/shard_map/slice | solution.py:293
  0.9 0.7 %slice_bitcast_fusion = f32[1,360]{1,0:T(1,128)S(1)} fusion(f32[1,16,360]{2,1,0:T(8,128)} %param.11), kind=kLoop, calls=%fused_computation.14 | loop fusion | bytes 2880 | tf_op jit(solution)/shard_map/slice | solution.py:291
  1.7 1.9 %collective-permute-start = (f32[8,384]{1,0:T(8,128)S(1)}, f32[8,384]{1,0:T(8,128)S(1)}, u32[]{:S(2)}, u32[]{:S(2)}) collective-permute-start(f32[8,384]{1,0:T(8,128)S(1)} %select_maximum_fusion), channel_id=1, source_target_pairs={{0,16},{16,32},{32,48},{48,64},{64,80},{80,96},{96,112},{112,128},... | collective-permute-start | bytes 36872 | tf_op jit(solution)/shard_map/ppermute | solution.py:294
  3.6 4.9 %collective-permute-start.1 = (f32[8,384]{1,0:T(8,128)S(1)}, f32[8,384]{1,0:T(8,128)S(1)}, u32[]{:S(2)}, u32[]{:S(2)}) collective-permute-start(f32[8,384]{1,0:T(8,128)S(1)} %pad.9), channel_id=1, source_target_pairs={{16,0},{32,16},{48,32},{64,48},{80,64},{96,80},{112,96},{128,112},... | collective-permute-start | bytes 36872 | tf_op jit(solution)/shard_map/ppermute | solution.py:295
  8.5 0.1 multiply_sine_fusion
  8.6 0.0 copy-start.6
  8.6 0.0 copy-start.5
  8.6 0.7 %copy-done.6 = s32[512]{0:T(512)S(1)} copy-done((s32[512]{0:T(512)S(1)}, s32[512]{0:T(512)}, u32[]{:S(2)}) %copy-start.6) | copy-done | bytes 2072
  9.3 0.0 copy-done.5
  9.3 0.7 %select_reduce_fusion = (s32[]{:T(128)}, s32[]{:T(128)}) fusion(s32[512]{0:T(512)S(1)} %copy-done.5, s32[]{:T(128)S(6)} %add.98, s32[512]{0:T(512)S(1)} %copy-done.6), kind=kLoop, calls=%fused_computation.11 | loop fusion | flops 2558 | bytes 4108 | tf_op jit(solution)/shard_map/reduce_sum | solution.py:315
  12.0 0.0 collective-permute-done.south
  12.0 0.0 copy-start.1
  12.1 0.0 collective-permute-done.1.north
  12.1 0.7 %broadcast_in_dim.14.metric = f32[4,16,128]{2,1,0:T(8,128)} broadcast(f32[4,16]{1,0:T(4,128)S(1)} %pad_maximum_fusion), dimensions={0,1} | broadcast | bytes 33024 | tf_op jit(solution)/shard_map/broadcast_in_dim | solution.py:310
  12.8 0.0 copy-done.2
  12.8 2.0 %increments.1 = f32[384,128]{1,0:T(8,128)} custom-call(f32[6,16,360]{2,1,0:T(8,128)} %bitcast.19, f32[16,360]{1,0:T(8,128)} %bitcast.24, f32[16,360]{1,0:T(8,128)} %bitcast.23, f32[8,384]{1,0:T(8,128)} %copy-done.1, f32[8,384]{1,0:T(8,128)} %copy-done.2, f32[4,16,128]{2,1,0:T(8,128)} %broadcast_in_dim.14.metric), custom_call_target="tpu_custom_call" | custom-call | tf_op jit(solution)/shard_map/increments/pallas_call | solution.py:322
  14.7 7.2 %all-to-all-start = ((f32[16,24,128]{2,1,0:T(8,128)}), f32[16,24,128]{2,1,0:T(8,128)S(1)}, u32[]{:S(2)}, u32[]{:S(2)}) async-start(f32[16,24,128]{2,1,0:T(8,128)} %bitcast.16), calls=%async_computation | async-start | bytes 393216 | tf_op jit(solution)/shard_map/all_to_all | solution.py:330
  21.9 0.6 %fusion.3.damping = f32[3,256]{1,0:T(4,128)} fusion(f32[3,256]{1,0:T(4,128)S(1)} %copy-done.3, s32[3,256]{1,0:T(4,128)S(1)} %copy-done.4, f32[]{:T(128)S(6)} %convert_element_type.50, f32[]{:T(128)S(6)} %max.11, s32[]{:T(128)S(6)} %add.100), kind=kLoop, calls=%fused_computation.9 | loop fusion | flops 4608 | bytes 9228 | tf_op jit(solution)/shard_map/mul | solution.py:319
  22.5 7.4 %all-to-all-done.chunks = f32[16,24,128]{2,1,0:T(8,128)S(1)} async-done(((f32[16,24,128]{2,1,0:T(8,128)}), f32[16,24,128]{2,1,0:T(8,128)S(1)}, u32[]{:S(2)}, u32[]{:S(2)}) %all-to-all-start) | async-done | bytes 196640 | tf_op jit(solution)/shard_map/all_to_all | solution.py:330
  30.0 0.6 %broadcast_in_dim.15.own = f32[8,128]{1,0:T(8,128)} broadcast(f32[]{:T(128)S(6)} %div.31), dimensions={} | broadcast | bytes 4100 | tf_op jit(solution)/shard_map/broadcast_in_dim | solution.py:320
  30.6 0.0 copy-done
  30.6 3.0 %filter_rows.1 = f32[16,24,128]{2,1,0:T(8,128)} custom-call(f32[16,24,128]{2,1,0:T(8,128)} %copy-done, f32[8,128]{1,0:T(8,128)} %broadcast_in_dim.15.own, f32[3,256]{1,0:T(4,128)} %fusion.3.damping, bf16[3,256,256]{2,1,0:T(8,128)(2,1)} %constant.50.clone.high, bf16[3,256,256]{2,1,0:T(8,128)(2,1)} %constant.51.clone.low), custom_call_target="tpu_custom_call" | custom-call | tf_op jit(solution)/shard_map/filter_rows/pallas_call | solution.py:331
  33.6 12.3 %all_to_all.10 = f32[16,24,128]{2,1,0:T(8,128)} all-to-all(f32[16,24,128]{2,1,0:T(8,128)} %filter_rows.1), channel_id=1, replica_groups=mesh['lat'=32,'lon'=16] {'lon'}, dimensions={0} | all-to-all | bytes 393216 | tf_op jit(solution)/shard_map/all_to_all | solution.py:338
  45.9 1.8 %advance.1 = f32[6,16,360]{2,1,0:T(8,128)} custom-call(f32[384,128]{1,0:T(8,128)} %bitcast.17, f32[6,16,360]{2,1,0:T(8,128)} %bitcast.20), custom_call_target="tpu_custom_call" | custom-call | tf_op jit(solution)/shard_map/advance/pallas_call | solution.py:339
  (13 shorter events, 0.1 us)
Async XLA Ops:
  1.7 10.4 %collective-permute-start = (f32[8,384]{1,0:T(8,128)S(1)}, f32[8,384]{1,0:T(8,128)S(1)}, u32[]{:S(2)}, u32[]{:S(2)}) collective-permute-start(f32[8,384]{1,0:T(8,128)S(1)} %select_maximum_fusion), channel_id=1, source_target_pairs={{0,16},{16,32},{32,48},{48,64},{64,80},{80,96},{96,112},{112,128},... | collective-permute-start | bytes 36872 | tf_op jit(solution)/shard_map/ppermute | solution.py:294
  3.6 8.4 %collective-permute-start.1 = (f32[8,384]{1,0:T(8,128)S(1)}, f32[8,384]{1,0:T(8,128)S(1)}, u32[]{:S(2)}, u32[]{:S(2)}) collective-permute-start(f32[8,384]{1,0:T(8,128)S(1)} %pad.9), channel_id=1, source_target_pairs={{16,0},{32,16},{48,32},{64,48},{80,64},{96,80},{112,96},{128,112},... | collective-permute-start | bytes 36872 | tf_op jit(solution)/shard_map/ppermute | solution.py:295
  8.6 0.7 %copy-start.6 = (s32[512]{0:T(512)S(1)}, s32[512]{0:T(512)}, u32[]{:S(2)}) copy-start(s32[512]{0:T(512)} %param.13) | copy-start | bytes 6148
  8.6 0.7 %copy-start.5 = (s32[512]{0:T(512)S(1)}, s32[512]{0:T(512)}, u32[]{:S(2)}) copy-start(s32[512]{0:T(512)} %param.12) | copy-start | bytes 6148
  12.0 0.7 %copy-start.1 = (f32[8,384]{1,0:T(8,128)}, f32[8,384]{1,0:T(8,128)S(1)}, u32[]{:S(2)}) copy-start(f32[8,384]{1,0:T(8,128)S(1)} %collective-permute-done.south) | copy-start | bytes 36868
  12.1 0.7 %copy-start.2 = (f32[8,384]{1,0:T(8,128)}, f32[8,384]{1,0:T(8,128)S(1)}, u32[]{:S(2)}) copy-start(f32[8,384]{1,0:T(8,128)S(1)} %collective-permute-done.1.north) | copy-start | bytes 36868
  14.7 7.2 %copy-start.3 = (f32[3,256]{1,0:T(4,128)S(1)}, f32[3,256]{1,0:T(4,128)}, u32[]{:S(2)}) copy-start(f32[3,256]{1,0:T(4,128)} %constant.49.clone) | copy-start | bytes 9220
  14.7 7.2 %copy-start.4 = (s32[3,256]{1,0:T(4,128)S(1)}, s32[3,256]{1,0:T(4,128)}, u32[]{:S(2)}) copy-start(s32[3,256]{1,0:T(4,128)} %constant.59) | copy-start | bytes 9220
  14.7 15.3 %all-to-all-start = ((f32[16,24,128]{2,1,0:T(8,128)}), f32[16,24,128]{2,1,0:T(8,128)S(1)}, u32[]{:S(2)}, u32[]{:S(2)}) async-start(f32[16,24,128]{2,1,0:T(8,128)} %bitcast.16), calls=%async_computation | async-start | bytes 393216 | tf_op jit(solution)/shard_map/all_to_all | solution.py:330
  30.0 0.7 %copy-start = (f32[16,24,128]{2,1,0:T(8,128)}, f32[16,24,128]{2,1,0:T(8,128)S(1)}, u32[]{:S(2)}) copy-start(f32[16,24,128]{2,1,0:T(8,128)S(1)} %all-to-all-done.chunks) | copy-start | bytes 589828

commit v2 on v1

--- a/solution.py
+++ b/solution.py
@@ -161,7 +161,31 @@
     return result
 
 
-def increment_kernel(state, zonal, merid, south, north, metric, chunks, pad):
+def slabs_of(part):
+    lane = lax.broadcasted_iota(jnp.int32, (part.shape[0], 128), 1)
+    v0, v1, v2 = part[:, :128], part[:, 128:256], part[:, 256:]
+    return (
+        v0,
+        jnp.where(lane < 8, pltpu.roll(v0, 8, 1), pltpu.roll(v1, 8, 1)),
+        jnp.where(lane < 16, pltpu.roll(v1, 16, 1), pltpu.roll(v2, 16, 1)),
+    )
+
+
+def border_kernel(state, merid, top, bottom, pad):
+    fields, rows, cells = state.shape
+    pad[:, :, 128 * (SLABS - 1) :] = jnp.zeros((2, 8, 128), jnp.float32)
+    pad[1, fields:, :] = jnp.zeros((8 - fields, 128 * SLABS), jnp.float32)
+    pad[0, fields:, :] = jnp.zeros((8 - fields, 128 * SLABS), jnp.float32)
+    for f in range(fields):
+        pad[0, f : f + 1, :cells] = state[f, rows - 1 :, :]
+        pad[1, f : f + 1, :cells] = state[f, :1, :]
+    pad[0, fields : fields + 1, :cells] = merid[rows - 1 :, :]
+    for place, border in ((0, top), (1, bottom)):
+        for a, slab in enumerate(slabs_of(pad[place])):
+            border[8 * a : 8 * a + 8, :] = slab
+
+
+def increment_kernel(state, zonal, merid, metric, chunks, pad):
     fields, rows, cells = state.shape
     wide = 128 * SLABS
     for f in range(fields + 2):
@@ -172,41 +196,49 @@
     pad[fields + 1, :, :cells] = merid[...]
     lane = lax.broadcasted_iota(jnp.int32, (rows, wide), 1)
     row = lax.broadcasted_iota(jnp.int32, (rows, wide), 0)
-    short = lane[:, :128]
 
     def spread(index):
         part = metric[index]
         return jnp.concatenate([part] * SLABS, axis=1)
 
-    zonal_factor, merid_factor, face, face_before = (spread(i) for i in range(4))
+    zonal_factor, merid_factor, face = (spread(i) for i in range(3))
     east_wind = pad[fields]
     last_wind = pltpu.roll(east_wind, 3, 1)
     inner_wind = jnp.where(lane < cells - 1, east_wind, 0.0)
-    north_wind = pad[fields + 1] * face
-    south_wind = south[fields : fields + 1, :] * face_before[0:1, :]
+    north_wind = jnp.where(row < rows - 1, pad[fields + 1] * face, 0.0)
     for f in range(fields):
         q = pad[f]
         flux_east = inner_wind * (0.5 * (q + pltpu.roll(q, wide - 1, 1)))
         zonal_diff = flux_east - pltpu.roll(flux_east, 1, 1)
-        q_north = jnp.where(row == rows - 1, north[f : f + 1, :], pltpu.roll(q, rows - 1, 0))
-        flux_north = north_wind * (0.5 * (q + q_north))
-        flux_first = south_wind * (0.5 * (south[f : f + 1, :] + q[0:1, :]))
-        merid_diff = flux_north - jnp.where(row == 0, flux_first, pltpu.roll(flux_north, 1, 0))
+        flux_north = north_wind * (0.5 * (q + pltpu.roll(q, rows - 1, 0)))
+        merid_diff = flux_north - pltpu.roll(flux_north, 1, 0)
         part = -zonal_factor * zonal_diff - merid_factor * merid_diff
         part = jnp.where(lane == cells, pltpu.roll(q, cells, 1), part)
         part = jnp.where(lane == cells + 1, pltpu.roll(q, 2, 1), part)
         part = jnp.where(lane == cells + 2, last_wind, part)
-        v0, v1, v2 = part[:, :128], part[:, 128:256], part[:, 256:]
-        slabs = (
-            v0,
-            jnp.where(short < 8, pltpu.roll(v0, 8, 1), pltpu.roll(v1, 8, 1)),
-            jnp.where(short < 16, pltpu.roll(v1, 16, 1), pltpu.roll(v2, 16, 1)),
-        )
-        for a in range(SLABS):
-            chunks[pl.ds(8 * a + f, rows, stride=ROWS), :] = slabs[a]
+        for a, slab in enumerate(slabs_of(part)):
+            chunks[pl.ds(8 * a + f, rows, stride=ROWS), :] = slab
     for f in range(fields, 8):
         for a in range(SLABS):
             chunks[pl.ds(8 * a + f, rows, stride=ROWS), :] = jnp.zeros((rows, 128), jnp.float32)
+
+
+def border_fluxes_kernel(part, top, bottom, south, north, metric, chunks):
+    fields, last = 6, part.shape[0] - ROWS
+    rows = metric.shape[1]
+    inside = lax.broadcasted_iota(jnp.int32, (8, 128), 1) < SLAB
+    first_factor, last_factor = metric[1, 0:1, :], metric[1, rows - 1 :, :]
+    first_face, last_face = metric[3, 0:1, :], metric[2, rows - 1 :, :]
+    has_north = metric[4, 0:1, :]
+    chunks[...] = part[...]
+    for a in range(SLABS):
+        here = slice(8 * a, 8 * a + 8)
+        wind = slice(8 * a + fields, 8 * a + fields + 1)
+        flux = (south[wind, :] * first_face) * (0.5 * (south[here, :] + bottom[here, :]))
+        chunks[here, :] = part[here, :] + jnp.where(inside, first_factor * flux, 0.0)
+        flux = (top[wind, :] * last_face) * (0.5 * (top[here, :] + has_north * north[here, :]))
+        there = slice(last + 8 * a, last + 8 * a + 8)
+        chunks[there, :] = part[there, :] - jnp.where(inside, last_factor * flux, 0.0)
 
 
 def split(x):
@@ -272,8 +304,17 @@
         advanced[f, :, 256:] = state[f, :, 256:] + s2[:, : cells - 256]
 
 
-def in_vmem(count):
-    return [pl.BlockSpec(memory_space=pltpu.VMEM)] * count
+def call(kernel, name, outs, mebibytes, args, scratch=()):
+    vmem = pl.BlockSpec(memory_space=pltpu.VMEM)
+    return pl.pallas_call(
+        kernel,
+        out_shape=[jax.ShapeDtypeStruct(shape, jnp.float32) for shape in outs],
+        in_specs=[vmem] * len(args),
+        out_specs=[vmem] * len(outs),
+        scratch_shapes=[pltpu.VMEM(shape, jnp.float32) for shape in scratch],
+        compiler_params=pltpu.CompilerParams(vmem_limit_bytes=mebibytes << 20),
+        name=name,
+    )(*args)
 
 
 def body(state, zonal_wind, meridional_wind, filter_flag, mode_count):
@@ -286,11 +327,11 @@
     fields = state.reshape(item_count, lat_cells, lon_cells)
     zonal, merid = (w.reshape(lat_cells, lon_cells) for w in (zonal_wind, meridional_wind))
 
-    forward = [(i, i + 1) for i in range(band_total - 1)]
+    forward = [(i, (i + 1) % band_total) for i in range(band_total)]
     backward = [(target, source) for source, target in forward]
-    top = jnp.concatenate([fields[:, -1], merid[-1:]], axis=0)
-    top = jnp.pad(top, ((0, 8 - item_count - 1), (0, wide - lon_cells)))
-    bottom = jnp.pad(fields[:, 0], ((0, 8 - item_count), (0, wide - lon_cells)))
+    top, bottom = call(
+        border_kernel, "borders", [(ROWS, 128)] * 2, 2, (fields, merid), [(2, 8, wide)]
+    )
     south = lax.ppermute(top, "lat", forward)
     north = lax.ppermute(bottom, "lat", backward)
 
@@ -304,10 +345,11 @@
 
     ids = band_index * lat_cells + jnp.arange(lat_cells, dtype=jnp.int32)
     center = center_metric(ids)
+    has_north = jnp.where(band_index < band_total - 1, jnp.ones_like(center), 0.0)
     metric = jnp.stack(
-        [zonal_scale / center, meridional_scale / center, face_metric(ids), face_metric(ids - 1)]
-    )
-    metric = jnp.broadcast_to(metric[:, :, None], (4, lat_cells, 128))
+        [zonal_scale / center, meridional_scale / center, face_metric(ids), face_metric(ids - 1), has_north]
+    )
+    metric = jnp.broadcast_to(metric[:, :, None], (5, lat_cells, 128))
 
     high, low, reduced, scale = mode_layout(circle, circle // 16)
     own_row = band_index * lat_cells + lax.axis_index("lon")
@@ -319,30 +361,23 @@
     damping = damping * jnp.asarray(scale)
     own = jnp.broadcast_to(zonal_scale / center_metric(own_row), (8, 128))
 
-    chunks = pl.pallas_call(
-        increment_kernel,
-        out_shape=jax.ShapeDtypeStruct((sectors * ROWS, 128), jnp.float32),
-        in_specs=in_vmem(6),
-        out_specs=pl.BlockSpec(memory_space=pltpu.VMEM),
-        scratch_shapes=[pltpu.VMEM((8, lat_cells, wide), jnp.float32)],
-        name="increments",
-    )(fields, zonal, merid, south, north, metric)
+    packed = (sectors * ROWS, 128)
+    (part,) = call(
+        increment_kernel, "increments", [packed], 4, (fields, zonal, merid, metric), [(8, lat_cells, wide)]
+    )
+    (chunks,) = call(
+        border_fluxes_kernel, "border_fluxes", [packed], 2, (part, top, bottom, south, north, metric)
+    )
     chunks = lax.all_to_all(chunks.reshape(sectors, ROWS, 128), "lon", 0, 0, tiled=True)
-    chunks = pl.pallas_call(
+    (chunks,) = call(
         filter_kernel,
-        out_shape=jax.ShapeDtypeStruct((sectors, ROWS, 128), jnp.float32),
-        in_specs=in_vmem(5),
-        out_specs=pl.BlockSpec(memory_space=pltpu.VMEM),
-        name="filter_rows",
-    )(chunks, own, damping, jnp.asarray(high), jnp.asarray(low))
+        "filter_rows",
+        [(sectors, ROWS, 128)],
+        8,
+        (chunks, own, damping, jnp.asarray(high), jnp.asarray(low)),
+    )
     chunks = lax.all_to_all(chunks, "lon", 0, 0, tiled=True)
-    advanced = pl.pallas_call(
-        final_kernel,
-        out_shape=jax.ShapeDtypeStruct((item_count, lat_cells, lon_cells), jnp.float32),
-        in_specs=in_vmem(2),
-        out_specs=pl.BlockSpec(memory_space=pltpu.VMEM),
-        name="advance",
-    )(chunks.reshape(sectors * ROWS, 128), fields)
+    (advanced,) = call(final_kernel, "advance", [fields.shape], 4, (chunks.reshape(packed), fields))
     return advanced.reshape(state.shape)
 
 

time: 48.2 us -> 44 us (0.913)
  the two profiles are of different devices: /device:TPU:384 before, /device:TPU:2 now
where the time goes in v2:
time: 44 us; the launch traced here: 43.6 us
  starting transfers between devices  16.6 us (38%)
  blocking collectives  11.6 us (26%)
  waiting for transfers between devices  6.55 us (15%)
  local copies, waits for them, and re-layouts  3.11 us (7%)
  Pallas kernels  2.96 us (7%)
  between operations  2.04 us (5%)
  other arithmetic  0.75 us (2%)
    all_to_all x1, blocking collectives, body(): chunks = lax.all_to_all(chunks, 'lon', 0, 0, tiled=True)  11.6 us
    ppermute x1, starting transfers between devices, body(): north = lax.ppermute(bottom, 'lat', backward)  8.94 us
    all_to_all x1, starting transfers between devices, body(): lax.all_to_all(chunks.reshape(sectors, ROWS, 128), 'lon', 0, 0, tiled=True)  7.61 us
    all_to_all x1, waiting for transfers between devices, body(): lax.all_to_all(chunks.reshape(sectors, ROWS, 128), 'lon', 0, 0, tiled=True)  6.55 us
    unnamed x22, local copies, waits for them, and re-layouts  3.01 us
    pallas_call x5, Pallas kernels, call(): pl.pallas_call(kernel, out_shape=[jax.ShapeDtypeStruct(shape, jnp.float32...  2.96 us
  transfers between devices with their start and end apart: 3, of which 1 were waited for; matrix products, arithmetic and copies ran while one was open for 2% of the time, Pallas kernels for 1%

profile of v2, /device:TPU:2, one launch (start us, length us, event | category | flops | bytes accessed | tf_op | source)
XLA Modules:
  0.0 43.6 jit_solution(10992008370017439303)
XLA Ops:
  0.0 0.9 %copy-done = f32[6,1,16,360]{3,2,1,0:T(8,128)S(1)} copy-done((f32[6,1,16,360]{3,2,1,0:T(8,128)S(1)}, f32[6,1,16,360]{3,2,1,0:T(8,128)}, u32[]{:S(2)}) %copy-start) | copy-done | bytes 138264
  0.9 0.7 %copy-done.4 = f32[1,16,360]{2,1,0:T(8,128)S(1)} copy-done((f32[1,16,360]{2,1,0:T(8,128)S(1)}, f32[1,16,360]{2,1,0:T(8,128)}, u32[]{:S(2)}) %copy-start.4) | copy-done | bytes 23064
  1.7 0.1 borders.1
  1.7 0.0 collective-permute-start
  1.7 8.9 %collective-permute-start.1 = (f32[24,128]{1,0:T(8,128)S(1)}, f32[24,128]{1,0:T(8,128)S(1)}, u32[]{:S(2)}, u32[]{:S(2)}) collective-permute-start(f32[24,128]{1,0:T(8,128)S(1)} %get-tuple-element.8.bottom), channel_id=1, source_target_pairs={{16,0},{32,16},{48,32},{64,48},{80,64},{96,80},{112,96},{128,112},... | collective-permute-start | bytes 36872 | tf_op jit(solution)/shard_map/ppermute | solution.py:336
  10.7 0.1 multiply_sine_fusion
  10.7 0.0 copy-start.10
  10.7 0.0 copy-start.9
  10.8 0.7 %copy-done.10 = s32[512]{0:T(512)S(1)} copy-done((s32[512]{0:T(512)S(1)}, s32[512]{0:T(512)}, u32[]{:S(2)}) %copy-start.10) | copy-done | bytes 2072
  11.4 0.0 copy-done.9
  11.4 0.6 %select_reduce_fusion = (s32[]{:T(128)}, s32[]{:T(128)}) fusion(s32[512]{0:T(512)S(1)} %copy-done.9, s32[]{:T(128)S(6)} %add.94, s32[512]{0:T(512)S(1)} %copy-done.10), kind=kLoop, calls=%fused_computation.5 | loop fusion | flops 2558 | bytes 4108 | tf_op jit(solution)/shard_map/reduce_sum | solution.py:357
  14.0 0.0 copy-start.6
  14.0 0.1 broadcast_in_dim.16.metric
  14.1 0.6 %copy-done.6 = f32[1,16,360]{2,1,0:T(8,128)S(1)} copy-done((f32[1,16,360]{2,1,0:T(8,128)S(1)}, f32[1,16,360]{2,1,0:T(8,128)}, u32[]{:S(2)}) %copy-start.6) | copy-done | bytes 23064
  14.7 0.0 copy-done.5
  14.8 0.3 increments.1.part
  15.2 0.0 copy-start.2
  15.2 0.0 copy-start.3
  15.2 0.7 %border_fluxes.1 = f32[384,128]{1,0:T(8,128)} custom-call(f32[384,128]{1,0:T(8,128)S(1)} %increments.1.part, f32[24,128]{1,0:T(8,128)S(1)} %get-tuple-element.7.top, f32[24,128]{1,0:T(8,128)S(1)} %get-tuple-element.8.bottom, f32[24,128]{1,0:T(8,128)S(1)} %collective-permute-done.south, f32[24,128]{1,0:T(8,128)S(1)} %collective-permute-done.1.north, ...), custom_call_target="tpu_custom_call" | custom-call | tf_op jit(solution)/shard_map/border_fluxes/pallas_call | solution.py:309
  15.9 7.6 %all-to-all-start = ((f32[16,24,128]{2,1,0:T(8,128)}), f32[16,24,128]{2,1,0:T(8,128)S(1)}, u32[]{:S(2)}, u32[]{:S(2)}) async-start(f32[16,24,128]{2,1,0:T(8,128)} %bitcast.3), calls=%async_computation | async-start | bytes 393216 | tf_op jit(solution)/shard_map/all_to_all | solution.py:371
  23.6 6.5 %all-to-all-done.chunks = f32[16,24,128]{2,1,0:T(8,128)S(1)} async-done(((f32[16,24,128]{2,1,0:T(8,128)}), f32[16,24,128]{2,1,0:T(8,128)S(1)}, u32[]{:S(2)}, u32[]{:S(2)}) %all-to-all-start) | async-done | bytes 196640 | tf_op jit(solution)/shard_map/all_to_all | solution.py:371
  30.1 1.1 %filter_rows.1 = f32[16,24,128]{2,1,0:T(8,128)S(1)} custom-call(f32[16,24,128]{2,1,0:T(8,128)S(1)} %all-to-all-done.chunks, f32[8,128]{1,0:T(8,128)S(1)} %broadcast_in_dim.17.own, f32[3,256]{1,0:T(4,128)S(1)} %fusion.3.damping, bf16[3,256,256]{2,1,0:T(8,128)(2,1)S(1)} %copy-done.2, bf16[3,256,256]{2,1,0:T(8,128)(2,1)S(1)} %copy-done.3), custom_call_target="tpu_custom_call" | custom-call | tf_op jit(solution)/shard_map/filter_rows/pallas_call | solution.py:309
  31.2 11.6 %all_to_all.10 = f32[16,24,128]{2,1,0:T(8,128)S(1)} all-to-all(f32[16,24,128]{2,1,0:T(8,128)S(1)} %filter_rows.1), channel_id=1, replica_groups=mesh['lat'=32,'lon'=16] {'lon'}, dimensions={0} | all-to-all | bytes 393216 | tf_op jit(solution)/shard_map/all_to_all | solution.py:379
  42.8 0.8 %advance.1 = f32[6,16,360]{2,1,0:T(8,128)} custom-call(f32[384,128]{1,0:T(8,128)S(1)} %bitcast.11, f32[6,16,360]{2,1,0:T(8,128)S(1)} %bitcast.10), custom_call_target="tpu_custom_call" | custom-call | tf_op jit(solution)/shard_map/advance/pallas_call | solution.py:309
  (18 shorter events, 0.1 us)
Async XLA Ops:
  0.0 0.9 %copy-start = (f32[6,1,16,360]{3,2,1,0:T(8,128)S(1)}, f32[6,1,16,360]{3,2,1,0:T(8,128)}, u32[]{:S(2)}) copy-start(f32[6,1,16,360]{3,2,1,0:T(8,128)} %param.9) | copy-start | bytes 414724
  0.9 0.7 %copy-start.4 = (f32[1,16,360]{2,1,0:T(8,128)S(1)}, f32[1,16,360]{2,1,0:T(8,128)}, u32[]{:S(2)}) copy-start(f32[1,16,360]{2,1,0:T(8,128)} %param.11) | copy-start | bytes 69124
  1.6 12.5 %copy-start.1 = (f32[6,1,16,360]{3,2,1,0:T(8,128)S(1)}, f32[6,1,16,360]{3,2,1,0:T(8,128)}, u32[]{:S(2)}) copy-start(f32[6,1,16,360]{3,2,1,0:T(8,128)} %param.9) | copy-start | bytes 414724
  1.7 13.5 %collective-permute-start = (f32[24,128]{1,0:T(8,128)S(1)}, f32[24,128]{1,0:T(8,128)S(1)}, u32[]{:S(2)}, u32[]{:S(2)}) collective-permute-start(f32[24,128]{1,0:T(8,128)S(1)} %get-tuple-element.7.top), channel_id=1, source_target_pairs={{0,16},{16,32},{32,48},{48,64},{64,80},{80,96},{96,112},{112,128},... | collective-permute-start | bytes 36872 | tf_op jit(solution)/shard_map/ppermute | solution.py:335
  1.7 13.5 %collective-permute-start.1 = (f32[24,128]{1,0:T(8,128)S(1)}, f32[24,128]{1,0:T(8,128)S(1)}, u32[]{:S(2)}, u32[]{:S(2)}) collective-permute-start(f32[24,128]{1,0:T(8,128)S(1)} %get-tuple-element.8.bottom), channel_id=1, source_target_pairs={{16,0},{32,16},{48,32},{64,48},{80,64},{96,80},{112,96},{128,112},... | collective-permute-start | bytes 36872 | tf_op jit(solution)/shard_map/ppermute | solution.py:336
  10.7 0.7 %copy-start.10 = (s32[512]{0:T(512)S(1)}, s32[512]{0:T(512)}, u32[]{:S(2)}) copy-start(s32[512]{0:T(512)} %param.13) | copy-start | bytes 6148
  10.7 0.7 %copy-start.9 = (s32[512]{0:T(512)S(1)}, s32[512]{0:T(512)}, u32[]{:S(2)}) copy-start(s32[512]{0:T(512)} %param.12) | copy-start | bytes 6148
  14.0 0.7 %copy-start.6 = (f32[1,16,360]{2,1,0:T(8,128)S(1)}, f32[1,16,360]{2,1,0:T(8,128)}, u32[]{:S(2)}) copy-start(f32[1,16,360]{2,1,0:T(8,128)} %param.10) | copy-start | bytes 69124
  14.0 0.7 %copy-start.5 = (f32[1,16,360]{2,1,0:T(8,128)S(1)}, f32[1,16,360]{2,1,0:T(8,128)}, u32[]{:S(2)}) copy-start(f32[1,16,360]{2,1,0:T(8,128)} %param.11) | copy-start | bytes 69124
  15.2 15.0 %copy-start.2 = (bf16[3,256,256]{2,1,0:T(8,128)(2,1)S(1)}, bf16[3,256,256]{2,1,0:T(8,128)(2,1)}, u32[]{:S(2)}) copy-start(bf16[3,256,256]{2,1,0:T(8,128)(2,1)} %constant.52.clone.high) | copy-start | bytes 1179652
  15.2 14.9 %copy-start.3 = (bf16[3,256,256]{2,1,0:T(8,128)(2,1)S(1)}, bf16[3,256,256]{2,1,0:T(8,128)(2,1)}, u32[]{:S(2)}) copy-start(bf16[3,256,256]{2,1,0:T(8,128)(2,1)} %constant.53.clone.low) | copy-start | bytes 1179652
  15.9 7.6 %copy-start.7 = (f32[3,256]{1,0:T(4,128)S(1)}, f32[3,256]{1,0:T(4,128)}, u32[]{:S(2)}) copy-start(f32[3,256]{1,0:T(4,128)} %constant.51.clone) | copy-start | bytes 9220
  15.9 7.6 %copy-start.8 = (s32[3,256]{1,0:T(4,128)S(1)}, s32[3,256]{1,0:T(4,128)}, u32[]{:S(2)}) copy-start(s32[3,256]{1,0:T(4,128)} %constant.57) | copy-start | bytes 9220
  15.9 14.2 %all-to-all-start = ((f32[16,24,128]{2,1,0:T(8,128)}), f32[16,24,128]{2,1,0:T(8,128)S(1)}, u32[]{:S(2)}, u32[]{:S(2)}) async-start(f32[16,24,128]{2,1,0:T(8,128)} %bitcast.3), calls=%async_computation | async-start | bytes 393216 | tf_op jit(solution)/shard_map/all_to_all | solution.py:371

commit v3 on v2

--- a/solution.py
+++ b/solution.py
@@ -48,6 +48,20 @@
     return high, low, reduced, scale.astype(np.float32)
 
 
+def row_metrics(nlat, bands):
+    ids = np.arange(nlat, dtype=np.float32)
+    step = np.float32(math.pi / nlat)
+    center = (ids + np.float32(0.5)) * step - np.float32(math.pi / 2)
+    center = np.cos(center.astype(np.float64)).astype(np.float32)
+    result = np.zeros((nlat, 128), np.float32)
+    result[:, 0] = np.float32(math.sin(math.pi / (2 * nlat))) / center
+    result[:, 1] = np.float32(meridional_scale) / center
+    result[:, 2] = np.sin(((ids + np.float32(1.0)) * step).astype(np.float64))
+    result[:, 3] = np.sin((ids * step).astype(np.float64))
+    result[:, 4] = np.arange(nlat) // (nlat // bands) < bands - 1
+    return result.reshape(bands, nlat // bands, 128)
+
+
 def c_add(x, y):
     return (x[0] + y[0], y[1] if x[1] is None else x[1] if y[1] is None else x[1] + y[1])
 
@@ -171,11 +185,17 @@
     )
 
 
-def border_kernel(state, merid, top, bottom, pad):
+def border_kernel(state_in, zonal_in, merid_in, top, bottom, state, zonal, merid, pad, sems):
     fields, rows, cells = state.shape
-    pad[:, :, 128 * (SLABS - 1) :] = jnp.zeros((2, 8, 128), jnp.float32)
-    pad[1, fields:, :] = jnp.zeros((8 - fields, 128 * SLABS), jnp.float32)
-    pad[0, fields:, :] = jnp.zeros((8 - fields, 128 * SLABS), jnp.float32)
+    copies = [
+        pltpu.make_async_copy(source, target, sems.at[i])
+        for i, (source, target) in enumerate(((state_in, state), (merid_in, merid), (zonal_in, zonal)))
+    ]
+    for copy in copies:
+        copy.start()
+    pad[...] = jnp.zeros(pad.shape, jnp.float32)
+    for copy in copies:
+        copy.wait()
     for f in range(fields):
         pad[0, f : f + 1, :cells] = state[f, rows - 1 :, :]
         pad[1, f : f + 1, :cells] = state[f, :1, :]
@@ -185,9 +205,20 @@
             border[8 * a : 8 * a + 8, :] = slab
 
 
-def increment_kernel(state, zonal, merid, metric, chunks, pad):
+def increment_kernel(
+    state, zonal, merid, reduced, scale, table, flags, counts,
+    chunks, metric, own, pad, flags_here, counts_here, sems,
+):
     fields, rows, cells = state.shape
     wide = 128 * SLABS
+    band, sector = lax.axis_index("lat"), lax.axis_index("lon")
+    copies = [
+        pltpu.make_async_copy(table.at[band], metric, sems.at[0]),
+        pltpu.make_async_copy(flags, flags_here, sems.at[1]),
+        pltpu.make_async_copy(counts, counts_here, sems.at[2]),
+    ]
+    for copy in copies:
+        copy.start()
     for f in range(fields + 2):
         pad[f, :, wide - 128 :] = jnp.zeros((rows, 128), jnp.float32)
     for f in range(fields):
@@ -196,10 +227,11 @@
     pad[fields + 1, :, :cells] = merid[...]
     lane = lax.broadcasted_iota(jnp.int32, (rows, wide), 1)
     row = lax.broadcasted_iota(jnp.int32, (rows, wide), 0)
+    for copy in copies:
+        copy.wait()
 
     def spread(index):
-        part = metric[index]
-        return jnp.concatenate([part] * SLABS, axis=1)
+        return jnp.broadcast_to(metric[:, index : index + 1], (rows, wide))
 
     zonal_factor, merid_factor, face = (spread(i) for i in range(3))
     east_wind = pad[fields]
@@ -221,15 +253,24 @@
     for f in range(fields, 8):
         for a in range(SLABS):
             chunks[pl.ds(8 * a + f, rows, stride=ROWS), :] = jnp.zeros((rows, 128), jnp.float32)
+    flag = flags_here[band * rows + sector].astype(jnp.float32)
+    count = counts_here[band * rows + sector].astype(jnp.float32)
+    raised = jnp.maximum(count + 1.0 - reduced[...], 0.0)
+    own[:8, :] = raised / jnp.maximum(count, 1.0) * flag * scale[...]
+    mine = jnp.where(row == sector, zonal_factor, 0.0)[:, :256]
+    own[8:, :] = jnp.broadcast_to(jnp.sum(mine, axis=0, keepdims=True), (8, 256))
 
 
 def border_fluxes_kernel(part, top, bottom, south, north, metric, chunks):
-    fields, last = 6, part.shape[0] - ROWS
-    rows = metric.shape[1]
+    fields, last, rows = 6, part.shape[0] - ROWS, metric.shape[0]
     inside = lax.broadcasted_iota(jnp.int32, (8, 128), 1) < SLAB
-    first_factor, last_factor = metric[1, 0:1, :], metric[1, rows - 1 :, :]
-    first_face, last_face = metric[3, 0:1, :], metric[2, rows - 1 :, :]
-    has_north = metric[4, 0:1, :]
+
+    def spread(row, index):
+        return jnp.broadcast_to(metric[row : row + 1, index : index + 1], (8, 128))
+
+    first_factor, last_factor = spread(0, 1), spread(rows - 1, 1)
+    first_face, last_face = spread(0, 3), spread(rows - 1, 2)
+    has_north = spread(0, 4)
     chunks[...] = part[...]
     for a in range(SLABS):
         here = slice(8 * a, 8 * a + 8)
@@ -254,10 +295,10 @@
     return dot(x_high, high) + (dot(x_low, high) + dot(x_high, low))
 
 
-def filter_kernel(chunks, own, damping, high, low, result):
+def filter_kernel(chunks, own, high, low, result):
     sectors = chunks.shape[0]
     lane = lax.broadcasted_iota(jnp.int32, (8, 128), 1)
-    zonal_factor = own[...]
+    zonal_factor = own[8:, :128]
     points = [chunks[p // 3, 8 * (p % 3) : 8 * (p % 3) + 8, :] for p in range(POINTS)]
     lasts = [points[3 * s + 2] for s in range(sectors)]
     for s in range(sectors):
@@ -280,7 +321,7 @@
             [jnp.concatenate(spectrum[8 * g + i], axis=1) for i in range(8)], axis=0
         )
         modes = product(rows, high[g], low[g], ((1,), (0,)))
-        modes = jnp.where(block == column, modes * damping[g : g + 1, :], 0.0)
+        modes = jnp.where(block == column, modes * own[g : g + 1, :], 0.0)
         rows = product(modes, high[g], low[g], ((1,), (1,)))
         for i in range(8):
             part = rows[8 * i : 8 * i + 8, :]
@@ -304,14 +345,19 @@
         advanced[f, :, 256:] = state[f, :, 256:] + s2[:, : cells - 256]
 
 
-def call(kernel, name, outs, mebibytes, args, scratch=()):
+def call(kernel, name, outs, mebibytes, args, elsewhere=0, scratch=()):
     vmem = pl.BlockSpec(memory_space=pltpu.VMEM)
+    stay = pl.BlockSpec(memory_space=pltpu.HBM)
+    fixed = len(args) - elsewhere
+    args = args[:fixed] + tuple(
+        pltpu.with_memory_space_constraint(arg, pltpu.HBM) for arg in args[fixed:]
+    )
     return pl.pallas_call(
         kernel,
         out_shape=[jax.ShapeDtypeStruct(shape, jnp.float32) for shape in outs],
-        in_specs=[vmem] * len(args),
+        in_specs=[vmem] * fixed + [stay] * elsewhere,
         out_specs=[vmem] * len(outs),
-        scratch_shapes=[pltpu.VMEM(shape, jnp.float32) for shape in scratch],
+        scratch_shapes=list(scratch),
         compiler_params=pltpu.CompilerParams(vmem_limit_bytes=mebibytes << 20),
         name=name,
     )(*args)
@@ -322,48 +368,43 @@
     item_count = field_count * level_count
     band_total, sectors = lax.axis_size("lat"), lax.axis_size("lon")
     nlat, circle = lat_cells * band_total, lon_cells * sectors
-    band_index = lax.axis_index("lat")
     wide = 128 * SLABS
     fields = state.reshape(item_count, lat_cells, lon_cells)
     zonal, merid = (w.reshape(lat_cells, lon_cells) for w in (zonal_wind, meridional_wind))
-
-    forward = [(i, (i + 1) % band_total) for i in range(band_total)]
+    high, low, reduced, scale = mode_layout(circle, circle // 16)
+
+    def eight(rows):
+        return jnp.asarray(np.pad(rows.astype(np.float32), ((0, 8 - rows.shape[0]), (0, 0))))
+
+    top, bottom, fields, zonal, merid = call(
+        border_kernel,
+        "borders",
+        [(ROWS, 128)] * 2 + [fields.shape, zonal.shape, merid.shape],
+        3,
+        (fields, zonal, merid),
+        3,
+        [pltpu.VMEM((2, 8, wide), jnp.float32), pltpu.SemaphoreType.DMA((3,))],
+    )
+    forward = [(i, i + 1) for i in range(band_total - 1)]
     backward = [(target, source) for source, target in forward]
-    top, bottom = call(
-        border_kernel, "borders", [(ROWS, 128)] * 2, 2, (fields, merid), [(2, 8, wide)]
-    )
     south = lax.ppermute(top, "lat", forward)
     north = lax.ppermute(bottom, "lat", backward)
 
-    zonal_scale = math.sin(math.pi / (2 * nlat))
-
-    def center_metric(ids):
-        return jnp.cos((ids.astype(jnp.float32) + 0.5) * (math.pi / nlat) - math.pi / 2)
-
-    def face_metric(ids):
-        return jnp.sin((ids.astype(jnp.float32) + 1.0) * (math.pi / nlat))
-
-    ids = band_index * lat_cells + jnp.arange(lat_cells, dtype=jnp.int32)
-    center = center_metric(ids)
-    has_north = jnp.where(band_index < band_total - 1, jnp.ones_like(center), 0.0)
-    metric = jnp.stack(
-        [zonal_scale / center, meridional_scale / center, face_metric(ids), face_metric(ids - 1), has_north]
-    )
-    metric = jnp.broadcast_to(metric[:, :, None], (5, lat_cells, 128))
-
-    high, low, reduced, scale = mode_layout(circle, circle // 16)
-    own_row = band_index * lat_cells + lax.axis_index("lon")
-    chosen = jnp.arange(nlat, dtype=jnp.int32) == own_row
-    flag = jnp.sum(jnp.where(chosen, filter_flag, 0))
-    count = jnp.sum(jnp.where(chosen, mode_count, 0))
-    raised = jnp.maximum(count + 1 - jnp.asarray(reduced), 0).astype(jnp.float32)
-    damping = raised / jnp.maximum(count.astype(jnp.float32), 1.0) * flag.astype(jnp.float32)
-    damping = damping * jnp.asarray(scale)
-    own = jnp.broadcast_to(zonal_scale / center_metric(own_row), (8, 128))
-
     packed = (sectors * ROWS, 128)
-    (part,) = call(
-        increment_kernel, "increments", [packed], 4, (fields, zonal, merid, metric), [(8, lat_cells, wide)]
+    part, metric, own = call(
+        increment_kernel,
+        "increments",
+        [packed, (lat_cells, 128), (16, 256)],
+        4,
+        (fields, zonal, merid, eight(reduced), eight(scale))
+        + (jnp.asarray(row_metrics(nlat, band_total)), filter_flag, mode_count),
+        3,
+        [
+            pltpu.VMEM((8, lat_cells, wide), jnp.float32),
+            pltpu.SMEM(filter_flag.shape, jnp.int32),
+            pltpu.SMEM(mode_count.shape, jnp.int32),
+            pltpu.SemaphoreType.DMA((3,)),
+        ],
     )
     (chunks,) = call(
         border_fluxes_kernel, "border_fluxes", [packed], 2, (part, top, bottom, south, north, metric)
@@ -374,7 +415,7 @@
         "filter_rows",
         [(sectors, ROWS, 128)],
         8,
-        (chunks, own, damping, jnp.asarray(high), jnp.asarray(low)),
+        (chunks, own, jnp.asarray(high), jnp.asarray(low)),
     )
     chunks = lax.all_to_all(chunks, "lon", 0, 0, tiled=True)
     (advanced,) = call(final_kernel, "advance", [fields.shape], 4, (chunks.reshape(packed), fields))

time: 44 us -> 38.9 us (0.88)
  the two profiles are of different devices: /device:TPU:2 before, /device:TPU:225 now
where the time goes in v3:
time: 38.9 us; the launch traced here: 38.6 us
  blocking collectives  24 us (62%)
  starting transfers between devices  7.24 us (19%)
  Pallas kernels  4.27 us (11%)
  waiting for transfers between devices  2.97 us (8%)
    all_to_all x1, blocking collectives, body(): lax.all_to_all(chunks.reshape(sectors, ROWS, 128), 'lon', 0, 0, tiled=True)  13.6 us
    all_to_all x1, blocking collectives, body(): chunks = lax.all_to_all(chunks, 'lon', 0, 0, tiled=True)  10.4 us
    ppermute x1, starting transfers between devices, body(): south = lax.ppermute(top, 'lat', forward)  5.32 us
    pallas_call x5, Pallas kernels, call(): pl.pallas_call(kernel, out_shape=[jax.ShapeDtypeStruct(shape, jnp.float32...  4.27 us
    ppermute x1, waiting for transfers between devices, body(): north = lax.ppermute(bottom, 'lat', backward)  2.97 us
    ppermute x1, starting transfers between devices, body(): north = lax.ppermute(bottom, 'lat', backward)  1.92 us
  transfers between devices with their start and end apart: 2, of which 1 were waited for; matrix products, arithmetic and copies ran while one was open for 0% of the time, Pallas kernels for 3%

profile of v3, /device:TPU:225, one launch (start us, length us, event | category | flops | bytes accessed | tf_op | source)
XLA Modules:
  0.0 38.6 jit_solution(9601902768138294339)
XLA Ops:
  0.0 0.0 copy-start.3
  0.0 1.0 %borders.1 = (f32[24,128]{1,0:T(8,128)S(1)}, f32[24,128]{1,0:T(8,128)S(1)}, f32[6,16,360]{2,1,0:T(8,128)S(1)}, f32[16,360]{1,0:T(8,128)S(1)}, f32[16,360]{1,0:T(8,128)S(1)}) custom-call(f32[6,16,360]{2,1,0:T(8,128)} %bitcast.10, f32[16,360]{1,0:T(8,128)} %bitcast.11, f32[16,360]{1,0:T(8,128)} %bitcast.12), custom_call_target="tpu_custom_call" | custom-call | tf_op jit(solution)/shard_map/borders/pallas_call | solution.py:355
  1.0 0.0 copy-start.2
  1.1 5.3 %collective-permute-start = (f32[24,128]{1,0:T(8,128)S(1)}, f32[24,128]{1,0:T(8,128)S(1)}, u32[]{:S(2)}, u32[]{:S(2)}) collective-permute-start(f32[24,128]{1,0:T(8,128)S(1)} %get-tuple-element.17.top), channel_id=1, source_target_pairs={{0,16},{16,32},{32,48},{48,64},{64,80},{80,96},{96,112},{112,128},... | collective-permute-start | bytes 36872 | tf_op jit(solution)/shard_map/ppermute | solution.py:390
  6.4 1.9 %collective-permute-start.1 = (f32[24,128]{1,0:T(8,128)S(1)}, f32[24,128]{1,0:T(8,128)S(1)}, u32[]{:S(2)}, u32[]{:S(2)}) collective-permute-start(f32[24,128]{1,0:T(8,128)S(1)} %get-tuple-element.18.bottom), channel_id=1, source_target_pairs={{16,0},{32,16},{48,32},{64,48},{80,64},{96,80},{112,96},{128,112},... | collective-permute-start | bytes 36872 | tf_op jit(solution)/shard_map/ppermute | solution.py:391
  8.3 0.0 copy-done.3
  8.3 0.0 copy-done.2
  8.3 1.3 %increments.1 = (f32[384,128]{1,0:T(8,128)S(1)}, f32[16,128]{1,0:T(8,128)S(1)}, f32[16,256]{1,0:T(8,128)S(1)}) custom-call(f32[6,16,360]{2,1,0:T(8,128)S(1)} %get-tuple-element.13.state, f32[16,360]{1,0:T(8,128)S(1)} %get-tuple-element.14.zonal, f32[16,360]{1,0:T(8,128)S(1)} %get-tuple-element.15.merid, f32[8,256]{1,0:T(8,128)S(1)} %copy-done.3, ...), custom_call_target="tpu_custom_call" | custom-call | tf_op jit(solution)/shard_map/increments/pallas_call | solution.py:355
  9.6 0.0 collective-permute-done.south
  9.6 3.0 %collective-permute-done.1.north = f32[24,128]{1,0:T(8,128)S(1)} collective-permute-done((f32[24,128]{1,0:T(8,128)S(1)}, f32[24,128]{1,0:T(8,128)S(1)}, u32[]{:S(2)}, u32[]{:S(2)}) %collective-permute-start.1) | collective-permute-done | bytes 12320 | tf_op jit(solution)/shard_map/ppermute | solution.py:391
  12.6 0.0 copy-start
  12.6 0.0 copy-start.1
  12.6 0.1 border_fluxes.1
  12.7 13.6 %all_to_all.10.chunks = f32[16,24,128]{2,1,0:T(8,128)S(1)} all-to-all(f32[16,24,128]{2,1,0:T(8,128)S(1)} %bitcast.8), channel_id=1, replica_groups=mesh['lat'=32,'lon'=16] {'lon'}, dimensions={0} | all-to-all | bytes 393216 | tf_op jit(solution)/shard_map/all_to_all | solution.py:412
  26.4 0.0 copy-done
  26.4 0.0 copy-done.1
  26.4 1.1 %filter_rows.1 = f32[16,24,128]{2,1,0:T(8,128)S(1)} custom-call(f32[16,24,128]{2,1,0:T(8,128)S(1)} %all_to_all.10.chunks, f32[16,256]{1,0:T(8,128)S(1)} %get-tuple-element.20.own, bf16[3,256,256]{2,1,0:T(8,128)(2,1)S(1)} %copy-done.1, bf16[3,256,256]{2,1,0:T(8,128)(2,1)S(1)} %copy-done), custom_call_target="tpu_custom_call" | custom-call | tf_op jit(solution)/shard_map/filter_rows/pallas_call | solution.py:355
  27.4 10.4 %all_to_all.11 = f32[16,24,128]{2,1,0:T(8,128)S(1)} all-to-all(f32[16,24,128]{2,1,0:T(8,128)S(1)} %filter_rows.1), channel_id=1, replica_groups=mesh['lat'=32,'lon'=16] {'lon'}, dimensions={0} | all-to-all | bytes 393216 | tf_op jit(solution)/shard_map/all_to_all | solution.py:420
  37.8 0.8 %advance.1 = f32[6,16,360]{2,1,0:T(8,128)} custom-call(f32[384,128]{1,0:T(8,128)S(1)} %bitcast.9, f32[6,16,360]{2,1,0:T(8,128)S(1)} %get-tuple-element.13.state), custom_call_target="tpu_custom_call" | custom-call | tf_op jit(solution)/shard_map/advance/pallas_call | solution.py:355
Async XLA Ops:
  0.0 8.3 %copy-start.3 = (f32[8,256]{1,0:T(8,128)S(1)}, f32[8,256]{1,0:T(8,128)}, u32[]{:S(2)}) copy-start(f32[8,256]{1,0:T(8,128)} %constant.10.clone.reduced) | copy-start | bytes 24580
  1.0 7.3 %copy-start.2 = (f32[8,256]{1,0:T(8,128)S(1)}, f32[8,256]{1,0:T(8,128)}, u32[]{:S(2)}) copy-start(f32[8,256]{1,0:T(8,128)} %constant.11.clone.scale) | copy-start | bytes 24580
  1.1 8.6 %collective-permute-start = (f32[24,128]{1,0:T(8,128)S(1)}, f32[24,128]{1,0:T(8,128)S(1)}, u32[]{:S(2)}, u32[]{:S(2)}) collective-permute-start(f32[24,128]{1,0:T(8,128)S(1)} %get-tuple-element.17.top), channel_id=1, source_target_pairs={{0,16},{16,32},{32,48},{48,64},{64,80},{80,96},{96,112},{112,128},... | collective-permute-start | bytes 36872 | tf_op jit(solution)/shard_map/ppermute | solution.py:390
  6.4 6.2 %collective-permute-start.1 = (f32[24,128]{1,0:T(8,128)S(1)}, f32[24,128]{1,0:T(8,128)S(1)}, u32[]{:S(2)}, u32[]{:S(2)}) collective-permute-start(f32[24,128]{1,0:T(8,128)S(1)} %get-tuple-element.18.bottom), channel_id=1, source_target_pairs={{16,0},{32,16},{48,32},{64,48},{80,64},{96,80},{112,96},{128,112},... | collective-permute-start | bytes 36872 | tf_op jit(solution)/shard_map/ppermute | solution.py:391
  12.6 13.7 %copy-start = (bf16[3,256,256]{2,1,0:T(8,128)(2,1)S(1)}, bf16[3,256,256]{2,1,0:T(8,128)(2,1)}, u32[]{:S(2)}) copy-start(bf16[3,256,256]{2,1,0:T(8,128)(2,1)} %constant.14.clone.low) | copy-start | bytes 1179652
  12.6 13.7 %copy-start.1 = (bf16[3,256,256]{2,1,0:T(8,128)(2,1)S(1)}, bf16[3,256,256]{2,1,0:T(8,128)(2,1)}, u32[]{:S(2)}) copy-start(bf16[3,256,256]{2,1,0:T(8,128)(2,1)} %constant.13.clone.high) | copy-start | bytes 1179652

commit v4 on v3

--- a/solution.py
+++ b/solution.py
@@ -58,7 +58,7 @@
     result[:, 1] = np.float32(meridional_scale) / center
     result[:, 2] = np.sin(((ids + np.float32(1.0)) * step).astype(np.float64))
     result[:, 3] = np.sin((ids * step).astype(np.float64))
-    result[:, 4] = np.arange(nlat) // (nlat // bands) < bands - 1
+    result[:, 4] = np.arange(nlat) // (nlat // bands) % 2
     return result.reshape(bands, nlat // bands, 128)
 
 
@@ -185,7 +185,7 @@
     )
 
 
-def border_kernel(state_in, zonal_in, merid_in, top, bottom, state, zonal, merid, pad, sems):
+def border_kernel(state_in, zonal_in, merid_in, near, far, state, zonal, merid, pad, sems):
     fields, rows, cells = state.shape
     copies = [
         pltpu.make_async_copy(source, target, sems.at[i])
@@ -200,9 +200,10 @@
         pad[0, f : f + 1, :cells] = state[f, rows - 1 :, :]
         pad[1, f : f + 1, :cells] = state[f, :1, :]
     pad[0, fields : fields + 1, :cells] = merid[rows - 1 :, :]
-    for place, border in ((0, top), (1, bottom)):
-        for a, slab in enumerate(slabs_of(pad[place])):
-            border[8 * a : 8 * a + 8, :] = slab
+    odd = lax.axis_index("lat") % 2 == 1
+    for a, (top, bottom) in enumerate(zip(slabs_of(pad[0]), slabs_of(pad[1]))):
+        near[8 * a : 8 * a + 8, :] = jnp.where(odd, bottom, top)
+        far[8 * a : 8 * a + 8, :] = jnp.where(odd, top, bottom)
 
 
 def increment_kernel(
@@ -261,7 +262,7 @@
     own[8:, :] = jnp.broadcast_to(jnp.sum(mine, axis=0, keepdims=True), (8, 256))
 
 
-def border_fluxes_kernel(part, top, bottom, south, north, metric, chunks):
+def border_fluxes_kernel(part, near, far, from_near, from_far, metric, chunks):
     fields, last, rows = 6, part.shape[0] - ROWS, metric.shape[0]
     inside = lax.broadcasted_iota(jnp.int32, (8, 128), 1) < SLAB
 
@@ -270,14 +271,17 @@
 
     first_factor, last_factor = spread(0, 1), spread(rows - 1, 1)
     first_face, last_face = spread(0, 3), spread(rows - 1, 2)
-    has_north = spread(0, 4)
+    odd = spread(0, 4) > 0.5
     chunks[...] = part[...]
     for a in range(SLABS):
         here = slice(8 * a, 8 * a + 8)
-        wind = slice(8 * a + fields, 8 * a + fields + 1)
-        flux = (south[wind, :] * first_face) * (0.5 * (south[here, :] + bottom[here, :]))
+        mine, next_chip = near[here, :], far[here, :]
+        top, bottom = jnp.where(odd, next_chip, mine), jnp.where(odd, mine, next_chip)
+        mine, next_chip = from_near[here, :], from_far[here, :]
+        north, south = jnp.where(odd, next_chip, mine), jnp.where(odd, mine, next_chip)
+        flux = (south[fields : fields + 1, :] * first_face) * (0.5 * (south + bottom))
         chunks[here, :] = part[here, :] + jnp.where(inside, first_factor * flux, 0.0)
-        flux = (top[wind, :] * last_face) * (0.5 * (top[here, :] + has_north * north[here, :]))
+        flux = (top[fields : fields + 1, :] * last_face) * (0.5 * (top + north))
         there = slice(last + 8 * a, last + 8 * a + 8)
         chunks[there, :] = part[there, :] - jnp.where(inside, last_factor * flux, 0.0)
 
@@ -376,7 +380,7 @@
     def eight(rows):
         return jnp.asarray(np.pad(rows.astype(np.float32), ((0, 8 - rows.shape[0]), (0, 0))))
 
-    top, bottom, fields, zonal, merid = call(
+    near, far, fields, zonal, merid = call(
         border_kernel,
         "borders",
         [(ROWS, 128)] * 2 + [fields.shape, zonal.shape, merid.shape],
@@ -385,10 +389,9 @@
         3,
         [pltpu.VMEM((2, 8, wide), jnp.float32), pltpu.SemaphoreType.DMA((3,))],
     )
-    forward = [(i, i + 1) for i in range(band_total - 1)]
-    backward = [(target, source) for source, target in forward]
-    south = lax.ppermute(top, "lat", forward)
-    north = lax.ppermute(bottom, "lat", backward)
+    from_near = lax.ppermute(near, "lat", [(i, i ^ 1) for i in range(band_total)])
+    pairs = [(i, i + 1) for i in range(1, band_total - 1, 2)]
+    from_far = lax.ppermute(far, "lat", pairs + [(target, source) for source, target in pairs])
 
     packed = (sectors * ROWS, 128)
     part, metric, own = call(
@@ -407,7 +410,7 @@
         ],
     )
     (chunks,) = call(
-        border_fluxes_kernel, "border_fluxes", [packed], 2, (part, top, bottom, south, north, metric)
+        border_fluxes_kernel, "border_fluxes", [packed], 2, (part, near, far, from_near, from_far, metric)
     )
     chunks = lax.all_to_all(chunks.reshape(sectors, ROWS, 128), "lon", 0, 0, tiled=True)
     (chunks,) = call(

time: 38.9 us -> 38.1 us (0.979)
  the two profiles are of different devices: /device:TPU:225 before, /device:TPU:384 now
where the time goes in v4:
time: 38.1 us; the launch traced here: 37.8 us
  blocking collectives  26.6 us (70%)
  starting transfers between devices  6.15 us (16%)
  Pallas kernels  4.27 us (11%)
  waiting for transfers between devices  0.67 us (2%)
    all_to_all x1, blocking collectives, body(): lax.all_to_all(chunks.reshape(sectors, ROWS, 128), 'lon', 0, 0, tiled=True)  15.1 us
    all_to_all x1, blocking collectives, body(): chunks = lax.all_to_all(chunks, 'lon', 0, 0, tiled=True)  11.5 us
    pallas_call x5, Pallas kernels, call(): pl.pallas_call(kernel, out_shape=[jax.ShapeDtypeStruct(shape, jnp.float32...  4.27 us
    ppermute x1, starting transfers between devices, body(): lax.ppermute(far, 'lat', pairs + [(target, source) for source, target in...  4.23 us
    ppermute x1, starting transfers between devices, body(): lax.ppermute(near, 'lat', [(i, i ^ 1) for i in range(band_total)])  1.92 us
  transfers between devices with their start and end apart: 2, of which 1 were waited for; matrix products, arithmetic and copies ran while one was open for 0% of the time, Pallas kernels for 3%

profile of v4, /device:TPU:384, one launch (start us, length us, event | category | flops | bytes accessed | tf_op | source)
XLA Modules:
  0.0 37.8 jit_solution(3038673185970295151)
XLA Ops:
  0.0 0.0 copy-start.3
  0.0 1.0 %borders.1 = (f32[24,128]{1,0:T(8,128)S(1)}, f32[24,128]{1,0:T(8,128)S(1)}, f32[6,16,360]{2,1,0:T(8,128)S(1)}, f32[16,360]{1,0:T(8,128)S(1)}, f32[16,360]{1,0:T(8,128)S(1)}) custom-call(f32[6,16,360]{2,1,0:T(8,128)} %bitcast.10, f32[16,360]{1,0:T(8,128)} %bitcast.11, f32[16,360]{1,0:T(8,128)} %bitcast.12), custom_call_target="tpu_custom_call" | custom-call | tf_op jit(solution)/shard_map/borders/pallas_call | solution.py:359
  1.0 0.0 copy-start.2
  1.1 1.9 %collective-permute-start = (f32[24,128]{1,0:T(8,128)S(1)}, f32[24,128]{1,0:T(8,128)S(1)}, u32[]{:S(2)}, u32[]{:S(2)}) collective-permute-start(f32[24,128]{1,0:T(8,128)S(1)} %get-tuple-element.17.near), channel_id=1, source_target_pairs={{0,16},{16,0},{32,48},{48,32},{64,80},{80,64},{96,112},{112,96},{1... | collective-permute-start | bytes 36872 | tf_op jit(solution)/shard_map/ppermute | solution.py:392
  3.0 4.2 %collective-permute-start.1 = (f32[24,128]{1,0:T(8,128)S(1)}, f32[24,128]{1,0:T(8,128)S(1)}, u32[]{:S(2)}, u32[]{:S(2)}) collective-permute-start(f32[24,128]{1,0:T(8,128)S(1)} %get-tuple-element.18.far), channel_id=1, source_target_pairs={{16,32},{48,64},{80,96},{112,128},{144,160},{176,192},{208,224},{2... | collective-permute-start | bytes 36872 | tf_op jit(solution)/shard_map/ppermute | solution.py:394
  7.2 0.0 copy-done.3
  7.2 0.0 copy-done.2
  7.2 1.3 %increments.1 = (f32[384,128]{1,0:T(8,128)S(1)}, f32[16,128]{1,0:T(8,128)S(1)}, f32[16,256]{1,0:T(8,128)S(1)}) custom-call(f32[6,16,360]{2,1,0:T(8,128)S(1)} %get-tuple-element.13.state, f32[16,360]{1,0:T(8,128)S(1)} %get-tuple-element.14.zonal, f32[16,360]{1,0:T(8,128)S(1)} %get-tuple-element.15.merid, f32[8,256]{1,0:T(8,128)S(1)} %copy-done.3, ...), custom_call_target="tpu_custom_call" | custom-call | tf_op jit(solution)/shard_map/increments/pallas_call | solution.py:359
  8.5 0.0 collective-permute-done.from_near
  8.6 0.7 %collective-permute-done.1.from_far = f32[24,128]{1,0:T(8,128)S(1)} collective-permute-done((f32[24,128]{1,0:T(8,128)S(1)}, f32[24,128]{1,0:T(8,128)S(1)}, u32[]{:S(2)}, u32[]{:S(2)}) %collective-permute-start.1) | collective-permute-done | bytes 12320 | tf_op jit(solution)/shard_map/ppermute | solution.py:394
  9.2 0.0 copy-start
  9.2 0.0 copy-start.1
  9.2 0.1 border_fluxes.1
  9.3 15.1 %all_to_all.10.chunks = f32[16,24,128]{2,1,0:T(8,128)S(1)} all-to-all(f32[16,24,128]{2,1,0:T(8,128)S(1)} %bitcast.8), channel_id=1, replica_groups=mesh['lat'=32,'lon'=16] {'lon'}, dimensions={0} | all-to-all | bytes 393216 | tf_op jit(solution)/shard_map/all_to_all | solution.py:415
  24.5 0.0 copy-done
  24.5 0.0 copy-done.1
  24.5 1.1 %filter_rows.1 = f32[16,24,128]{2,1,0:T(8,128)S(1)} custom-call(f32[16,24,128]{2,1,0:T(8,128)S(1)} %all_to_all.10.chunks, f32[16,256]{1,0:T(8,128)S(1)} %get-tuple-element.20.own, bf16[3,256,256]{2,1,0:T(8,128)(2,1)S(1)} %copy-done.1, bf16[3,256,256]{2,1,0:T(8,128)(2,1)S(1)} %copy-done), custom_call_target="tpu_custom_call" | custom-call | tf_op jit(solution)/shard_map/filter_rows/pallas_call | solution.py:359
  25.6 11.5 %all_to_all.11 = f32[16,24,128]{2,1,0:T(8,128)S(1)} all-to-all(f32[16,24,128]{2,1,0:T(8,128)S(1)} %filter_rows.1), channel_id=1, replica_groups=mesh['lat'=32,'lon'=16] {'lon'}, dimensions={0} | all-to-all | bytes 393216 | tf_op jit(solution)/shard_map/all_to_all | solution.py:423
  37.1 0.8 %advance.1 = f32[6,16,360]{2,1,0:T(8,128)} custom-call(f32[384,128]{1,0:T(8,128)S(1)} %bitcast.9, f32[6,16,360]{2,1,0:T(8,128)S(1)} %get-tuple-element.13.state), custom_call_target="tpu_custom_call" | custom-call | tf_op jit(solution)/shard_map/advance/pallas_call | solution.py:359
Async XLA Ops:
  0.0 7.2 %copy-start.3 = (f32[8,256]{1,0:T(8,128)S(1)}, f32[8,256]{1,0:T(8,128)}, u32[]{:S(2)}) copy-start(f32[8,256]{1,0:T(8,128)} %constant.10.clone.reduced) | copy-start | bytes 24580
  1.0 6.2 %copy-start.2 = (f32[8,256]{1,0:T(8,128)S(1)}, f32[8,256]{1,0:T(8,128)}, u32[]{:S(2)}) copy-start(f32[8,256]{1,0:T(8,128)} %constant.11.clone.scale) | copy-start | bytes 24580
  1.1 7.5 %collective-permute-start = (f32[24,128]{1,0:T(8,128)S(1)}, f32[24,128]{1,0:T(8,128)S(1)}, u32[]{:S(2)}, u32[]{:S(2)}) collective-permute-start(f32[24,128]{1,0:T(8,128)S(1)} %get-tuple-element.17.near), channel_id=1, source_target_pairs={{0,16},{16,0},{32,48},{48,32},{64,80},{80,64},{96,112},{112,96},{1... | collective-permute-start | bytes 36872 | tf_op jit(solution)/shard_map/ppermute | solution.py:392
  3.0 6.2 %collective-permute-start.1 = (f32[24,128]{1,0:T(8,128)S(1)}, f32[24,128]{1,0:T(8,128)S(1)}, u32[]{:S(2)}, u32[]{:S(2)}) collective-permute-start(f32[24,128]{1,0:T(8,128)S(1)} %get-tuple-element.18.far), channel_id=1, source_target_pairs={{16,32},{48,64},{80,96},{112,128},{144,160},{176,192},{208,224},{2... | collective-permute-start | bytes 36872 | tf_op jit(solution)/shard_map/ppermute | solution.py:394
  9.2 15.3 %copy-start = (bf16[3,256,256]{2,1,0:T(8,128)(2,1)S(1)}, bf16[3,256,256]{2,1,0:T(8,128)(2,1)}, u32[]{:S(2)}) copy-start(bf16[3,256,256]{2,1,0:T(8,128)(2,1)} %constant.14.clone.low) | copy-start | bytes 1179652
  9.2 15.3 %copy-start.1 = (bf16[3,256,256]{2,1,0:T(8,128)(2,1)S(1)}, bf16[3,256,256]{2,1,0:T(8,128)(2,1)}, u32[]{:S(2)}) copy-start(bf16[3,256,256]{2,1,0:T(8,128)(2,1)} %constant.13.clone.high) | copy-start | bytes 1179652

commit v5 on v4

--- a/solution.py
+++ b/solution.py
@@ -185,11 +185,17 @@
     )
 
 
-def border_kernel(state_in, zonal_in, merid_in, near, far, state, zonal, merid, pad, sems):
+def border_kernel(
+    state_in, zonal_in, merid_in, table, flags_in, counts_in,
+    far, near, top, bottom, state, zonal, merid, metric, flags, counts, pad, sems,
+):
     fields, rows, cells = state.shape
+    band = lax.axis_index("lat")
+    sources = (state_in, merid_in, zonal_in, table.at[band], flags_in, counts_in)
+    targets = (state, merid, zonal, metric, flags, counts)
     copies = [
         pltpu.make_async_copy(source, target, sems.at[i])
-        for i, (source, target) in enumerate(((state_in, state), (merid_in, merid), (zonal_in, zonal)))
+        for i, (source, target) in enumerate(zip(sources, targets))
     ]
     for copy in copies:
         copy.start()
@@ -200,26 +206,20 @@
         pad[0, f : f + 1, :cells] = state[f, rows - 1 :, :]
         pad[1, f : f + 1, :cells] = state[f, :1, :]
     pad[0, fields : fields + 1, :cells] = merid[rows - 1 :, :]
-    odd = lax.axis_index("lat") % 2 == 1
-    for a, (top, bottom) in enumerate(zip(slabs_of(pad[0]), slabs_of(pad[1]))):
-        near[8 * a : 8 * a + 8, :] = jnp.where(odd, bottom, top)
-        far[8 * a : 8 * a + 8, :] = jnp.where(odd, top, bottom)
+    odd = band % 2 == 1
+    for a, (last, first) in enumerate(zip(slabs_of(pad[0]), slabs_of(pad[1]))):
+        here = slice(8 * a, 8 * a + 8)
+        top[here, :], bottom[here, :] = last, first
+        far[here, :] = jnp.where(odd, last, first)
+        near[here, :] = jnp.where(odd, first, last)
 
 
 def increment_kernel(
-    state, zonal, merid, reduced, scale, table, flags, counts,
-    chunks, metric, own, pad, flags_here, counts_here, sems,
+    state, zonal, merid, metric, flags, counts, reduced, scale, chunks, own, pad
 ):
     fields, rows, cells = state.shape
     wide = 128 * SLABS
     band, sector = lax.axis_index("lat"), lax.axis_index("lon")
-    copies = [
-        pltpu.make_async_copy(table.at[band], metric, sems.at[0]),
-        pltpu.make_async_copy(flags, flags_here, sems.at[1]),
-        pltpu.make_async_copy(counts, counts_here, sems.at[2]),
-    ]
-    for copy in copies:
-        copy.start()
     for f in range(fields + 2):
         pad[f, :, wide - 128 :] = jnp.zeros((rows, 128), jnp.float32)
     for f in range(fields):
@@ -228,8 +228,6 @@
     pad[fields + 1, :, :cells] = merid[...]
     lane = lax.broadcasted_iota(jnp.int32, (rows, wide), 1)
     row = lax.broadcasted_iota(jnp.int32, (rows, wide), 0)
-    for copy in copies:
-        copy.wait()
 
     def spread(index):
         return jnp.broadcast_to(metric[:, index : index + 1], (rows, wide))
@@ -254,15 +252,21 @@
     for f in range(fields, 8):
         for a in range(SLABS):
             chunks[pl.ds(8 * a + f, rows, stride=ROWS), :] = jnp.zeros((rows, 128), jnp.float32)
-    flag = flags_here[band * rows + sector].astype(jnp.float32)
-    count = counts_here[band * rows + sector].astype(jnp.float32)
+    place = lax.broadcasted_iota(jnp.int32, flags.shape, 0) * 128 + lax.broadcasted_iota(jnp.int32, flags.shape, 1)
+    chosen = place == band * rows + sector
+
+    def pick(values):
+        picked = jnp.where(chosen, values[...].astype(jnp.float32), 0.0)
+        return jnp.sum(jnp.sum(picked, axis=1, keepdims=True), axis=0, keepdims=True)
+
+    flag, count = pick(flags), pick(counts)
     raised = jnp.maximum(count + 1.0 - reduced[...], 0.0)
     own[:8, :] = raised / jnp.maximum(count, 1.0) * flag * scale[...]
     mine = jnp.where(row == sector, zonal_factor, 0.0)[:, :256]
     own[8:, :] = jnp.broadcast_to(jnp.sum(mine, axis=0, keepdims=True), (8, 256))
 
 
-def border_fluxes_kernel(part, near, far, from_near, from_far, metric, chunks):
+def border_fluxes_kernel(part, top_in, bottom_in, both, from_far, metric, chunks):
     fields, last, rows = 6, part.shape[0] - ROWS, metric.shape[0]
     inside = lax.broadcasted_iota(jnp.int32, (8, 128), 1) < SLAB
 
@@ -275,9 +279,8 @@
     chunks[...] = part[...]
     for a in range(SLABS):
         here = slice(8 * a, 8 * a + 8)
-        mine, next_chip = near[here, :], far[here, :]
-        top, bottom = jnp.where(odd, next_chip, mine), jnp.where(odd, mine, next_chip)
-        mine, next_chip = from_near[here, :], from_far[here, :]
+        top, bottom = top_in[here, :], bottom_in[here, :]
+        mine, next_chip = jnp.where(odd, both[here, :], both[ROWS + 8 * a : ROWS + 8 * a + 8, :]), from_far[here, :]
         north, south = jnp.where(odd, next_chip, mine), jnp.where(odd, mine, next_chip)
         flux = (south[fields : fields + 1, :] * first_face) * (0.5 * (south + bottom))
         chunks[here, :] = part[here, :] + jnp.where(inside, first_factor * flux, 0.0)
@@ -349,6 +352,10 @@
         advanced[f, :, 256:] = state[f, :, 256:] + s2[:, : cells - 256]
 
 
+def floats(*shape):
+    return jax.ShapeDtypeStruct(shape, jnp.float32)
+
+
 def call(kernel, name, outs, mebibytes, args, elsewhere=0, scratch=()):
     vmem = pl.BlockSpec(memory_space=pltpu.VMEM)
     stay = pl.BlockSpec(memory_space=pltpu.HBM)
@@ -358,7 +365,7 @@
     )
     return pl.pallas_call(
         kernel,
-        out_shape=[jax.ShapeDtypeStruct(shape, jnp.float32) for shape in outs],
+        out_shape=[jax.ShapeDtypeStruct(out.shape, out.dtype) for out in outs],
         in_specs=[vmem] * fixed + [stay] * elsewhere,
         out_specs=[vmem] * len(outs),
         scratch_shapes=list(scratch),
@@ -380,48 +387,49 @@
     def eight(rows):
         return jnp.asarray(np.pad(rows.astype(np.float32), ((0, 8 - rows.shape[0]), (0, 0))))
 
-    near, far, fields, zonal, merid = call(
+    flags, counts = filter_flag.reshape(-1, 128), mode_count.reshape(-1, 128)
+    border = floats(ROWS, 128)
+    far, near, top, bottom, fields, zonal, merid, metric, flags, counts = call(
         border_kernel,
         "borders",
-        [(ROWS, 128)] * 2 + [fields.shape, zonal.shape, merid.shape],
+        [border, border, border, border, fields, zonal, merid, floats(lat_cells, 128), flags, counts],
         3,
-        (fields, zonal, merid),
-        3,
-        [pltpu.VMEM((2, 8, wide), jnp.float32), pltpu.SemaphoreType.DMA((3,))],
-    )
-    from_near = lax.ppermute(near, "lat", [(i, i ^ 1) for i in range(band_total)])
+        (fields, zonal, merid, jnp.asarray(row_metrics(nlat, band_total)), flags, counts),
+        6,
+        [pltpu.VMEM((2, 8, wide), jnp.float32), pltpu.SemaphoreType.DMA((6,))],
+    )
     pairs = [(i, i + 1) for i in range(1, band_total - 1, 2)]
     from_far = lax.ppermute(far, "lat", pairs + [(target, source) for source, target in pairs])
+    chips = [[i, i + 1] for i in range(0, band_total, 2)]
+    both = lax.all_gather(near, "lat", axis=0, tiled=True, axis_index_groups=chips)
 
     packed = (sectors * ROWS, 128)
-    part, metric, own = call(
+    part, own = call(
         increment_kernel,
         "increments",
-        [packed, (lat_cells, 128), (16, 256)],
+        [floats(*packed), floats(16, 256)],
         4,
-        (fields, zonal, merid, eight(reduced), eight(scale))
-        + (jnp.asarray(row_metrics(nlat, band_total)), filter_flag, mode_count),
-        3,
-        [
-            pltpu.VMEM((8, lat_cells, wide), jnp.float32),
-            pltpu.SMEM(filter_flag.shape, jnp.int32),
-            pltpu.SMEM(mode_count.shape, jnp.int32),
-            pltpu.SemaphoreType.DMA((3,)),
-        ],
+        (fields, zonal, merid, metric, flags, counts, eight(reduced), eight(scale)),
+        0,
+        [pltpu.VMEM((8, lat_cells, wide), jnp.float32)],
     )
     (chunks,) = call(
-        border_fluxes_kernel, "border_fluxes", [packed], 2, (part, near, far, from_near, from_far, metric)
+        border_fluxes_kernel,
+        "border_fluxes",
+        [floats(*packed)],
+        2,
+        (part, top, bottom, both, from_far, metric),
     )
     chunks = lax.all_to_all(chunks.reshape(sectors, ROWS, 128), "lon", 0, 0, tiled=True)
     (chunks,) = call(
         filter_kernel,
         "filter_rows",
-        [(sectors, ROWS, 128)],
+        [floats(sectors, ROWS, 128)],
         8,
         (chunks, own, jnp.asarray(high), jnp.asarray(low)),
     )
     chunks = lax.all_to_all(chunks, "lon", 0, 0, tiled=True)
-    (advanced,) = call(final_kernel, "advance", [fields.shape], 4, (chunks.reshape(packed), fields))
+    (advanced,) = call(final_kernel, "advance", [fields], 4, (chunks.reshape(packed), fields))
     return advanced.reshape(state.shape)
 
 

time: 38.1 us -> 37.2 us (0.976)
  the two profiles are of different devices: /device:TPU:384 before, /device:TPU:96 now
where the time goes in v5:
time: 37.2 us; the launch traced here: 36.9 us
  blocking collectives  31.5 us (85%)
  Pallas kernels  3.43 us (9%)
  starting transfers between devices  1.92 us (5%)
    all_to_all x1, blocking collectives, body(): lax.all_to_all(chunks.reshape(sectors, ROWS, 128), 'lon', 0, 0, tiled=True)  15.3 us
    all_to_all x1, blocking collectives, body(): chunks = lax.all_to_all(chunks, 'lon', 0, 0, tiled=True)  11.5 us
    all_gather x1, blocking collectives, body(): lax.all_gather(near, 'lat', axis=0, tiled=True, axis_index_groups=chips)  4.72 us
    pallas_call x5, Pallas kernels, call(): pl.pallas_call(kernel, out_shape=[jax.ShapeDtypeStruct(out.shape, out.dty...  3.43 us
    ppermute x1, starting transfers between devices, body(): lax.ppermute(far, 'lat', pairs + [(target, source) for source, target in...  1.92 us
  transfers between devices with their start and end apart: 1, of which 0 were waited for; matrix products, arithmetic and copies ran while one was open for 0% of the time, Pallas kernels for 1%

profile of v5, /device:TPU:96, one launch (start us, length us, event | category | flops | bytes accessed | tf_op | source)
XLA Modules:
  0.0 36.9 jit_solution(4769349325313114865)
XLA Ops:
  0.0 0.0 copy-start.3
  0.0 1.1 %borders.1 = (f32[24,128]{1,0:T(8,128)S(1)}, f32[24,128]{1,0:T(8,128)S(1)}, f32[24,128]{1,0:T(8,128)S(1)}, f32[24,128]{1,0:T(8,128)S(1)}, f32[6,16,360]{2,1,0:T(...) custom-call(f32[6,16,360]{2,1,0:T(8,128)} %bitcast.12, ...), custom_call_target="tpu_custom_call" | custom-call | tf_op jit(solution)/shard_map/borders/pallas_call | solution.py:366
  1.1 0.0 copy-start.2
  1.1 1.9 %collective-permute-start = (f32[24,128]{1,0:T(8,128)S(1)}, f32[24,128]{1,0:T(8,128)S(1)}, u32[]{:S(2)}, u32[]{:S(2)}) collective-permute-start(f32[24,128]{1,0:T(8,128)S(1)} %get-tuple-element.27), channel_id=1, source_target_pairs={{16,32},{48,64},{80,96},{112,128},{144,160},{176,192},{208,224},{2... | collective-permute-start | bytes 36872 | tf_op jit(solution)/shard_map/ppermute | solution.py:402
  3.0 0.0 copy-done.3
  3.0 0.0 copy-done.2
  3.0 0.4 %increments.1 = (f32[384,128]{1,0:T(8,128)S(1)}, f32[16,256]{1,0:T(8,128)S(1)}) custom-call(f32[6,16,360]{2,1,0:T(8,128)S(1)} %get-tuple-element.17.state, f32[16,360]{1,0:T(8,128)S(1)} %get-tuple-element.18.zonal, f32[16,360]{1,0:T(8,128)S(1)} %get-tuple-element.19.merid, f32[16,128]{1,0:T(8,128)S(1)} %get-tuple-element.20.metric, ...), custom_call_target="tpu_custom_call" | custom-call | tf_op jit(solution)/shard_map/increments/pallas_call | solution.py:366
  3.5 4.7 %all_gather.3.both = f32[48,128]{1,0:T(8,128)S(1)} all-gather(f32[24,128]{1,0:T(8,128)S(1)} %get-tuple-element.26), channel_id=1, replica_groups={{0,16},{32,48},{64,80},{96,112},{128,144},{160,176},{192,208},{224,240}..., dimensions={0}, use_global_device_ids=true | all-gather | bytes 36864 | tf_op jit(solution)/shard_map/all_gather | solution.py:404
  8.2 0.0 collective-permute-done.from_far
  8.2 0.0 copy-start
  8.2 0.0 copy-start.1
  8.2 0.1 border_fluxes.1
  8.3 15.3 %all_to_all.10.chunks = f32[16,24,128]{2,1,0:T(8,128)S(1)} all-to-all(f32[16,24,128]{2,1,0:T(8,128)S(1)} %bitcast.10), channel_id=1, replica_groups=mesh['lat'=32,'lon'=16] {'lon'}, dimensions={0} | all-to-all | bytes 393216 | tf_op jit(solution)/shard_map/all_to_all | solution.py:423
  23.6 0.0 copy-done
  23.6 0.0 copy-done.1
  23.6 1.1 %filter_rows.1 = f32[16,24,128]{2,1,0:T(8,128)S(1)} custom-call(f32[16,24,128]{2,1,0:T(8,128)S(1)} %all_to_all.10.chunks, f32[16,256]{1,0:T(8,128)S(1)} %get-tuple-element.28.own, bf16[3,256,256]{2,1,0:T(8,128)(2,1)S(1)} %copy-done.1, bf16[3,256,256]{2,1,0:T(8,128)(2,1)S(1)} %copy-done), custom_call_target="tpu_custom_call" | custom-call | tf_op jit(solution)/shard_map/filter_rows/pallas_call | solution.py:366
  24.7 11.5 %all_to_all.11 = f32[16,24,128]{2,1,0:T(8,128)S(1)} all-to-all(f32[16,24,128]{2,1,0:T(8,128)S(1)} %filter_rows.1), channel_id=1, replica_groups=mesh['lat'=32,'lon'=16] {'lon'}, dimensions={0} | all-to-all | bytes 393216 | tf_op jit(solution)/shard_map/all_to_all | solution.py:431
  36.2 0.8 %advance.1 = f32[6,16,360]{2,1,0:T(8,128)} custom-call(f32[384,128]{1,0:T(8,128)S(1)} %bitcast.11, f32[6,16,360]{2,1,0:T(8,128)S(1)} %get-tuple-element.17.state), custom_call_target="tpu_custom_call" | custom-call | tf_op jit(solution)/shard_map/advance/pallas_call | solution.py:366
Async XLA Ops:
  0.0 3.0 %copy-start.3 = (f32[8,256]{1,0:T(8,128)S(1)}, f32[8,256]{1,0:T(8,128)}, u32[]{:S(2)}) copy-start(f32[8,256]{1,0:T(8,128)} %constant.11.clone.reduced) | copy-start | bytes 24580
  1.1 2.0 %copy-start.2 = (f32[8,256]{1,0:T(8,128)S(1)}, f32[8,256]{1,0:T(8,128)}, u32[]{:S(2)}) copy-start(f32[8,256]{1,0:T(8,128)} %constant.12.clone.scale) | copy-start | bytes 24580
  1.1 7.1 %collective-permute-start = (f32[24,128]{1,0:T(8,128)S(1)}, f32[24,128]{1,0:T(8,128)S(1)}, u32[]{:S(2)}, u32[]{:S(2)}) collective-permute-start(f32[24,128]{1,0:T(8,128)S(1)} %get-tuple-element.27), channel_id=1, source_target_pairs={{16,32},{48,64},{80,96},{112,128},{144,160},{176,192},{208,224},{2... | collective-permute-start | bytes 36872 | tf_op jit(solution)/shard_map/ppermute | solution.py:402
  8.2 15.5 %copy-start = (bf16[3,256,256]{2,1,0:T(8,128)(2,1)S(1)}, bf16[3,256,256]{2,1,0:T(8,128)(2,1)}, u32[]{:S(2)}) copy-start(bf16[3,256,256]{2,1,0:T(8,128)(2,1)} %constant.14.clone.low) | copy-start | bytes 1179652
  8.2 15.5 %copy-start.1 = (bf16[3,256,256]{2,1,0:T(8,128)(2,1)S(1)}, bf16[3,256,256]{2,1,0:T(8,128)(2,1)}, u32[]{:S(2)}) copy-start(bf16[3,256,256]{2,1,0:T(8,128)(2,1)} %constant.13.clone.high) | copy-start | bytes 1179652

commit v6 on v5

--- a/solution.py
+++ b/solution.py
@@ -14,6 +14,7 @@
 SLAB = 120
 POINTS = 48
 ROWS = 8 * SLABS
+CHUNK = 6 * SLABS
 GROUPS = 3
 
 
@@ -186,13 +187,13 @@
 
 
 def border_kernel(
-    state_in, zonal_in, merid_in, table, flags_in, counts_in,
-    far, near, top, bottom, state, zonal, merid, metric, flags, counts, pad, sems,
+    state_in, zonal_in, merid_in, table, flags_in, counts_in, modes_in,
+    far, near, top, bottom, state, zonal, merid, metric, flags, counts, modes, chunks, own, pad, sems,
 ):
     fields, rows, cells = state.shape
     band = lax.axis_index("lat")
-    sources = (state_in, merid_in, zonal_in, table.at[band], flags_in, counts_in)
-    targets = (state, merid, zonal, metric, flags, counts)
+    sources = (state_in, merid_in, zonal_in, table.at[band], flags_in, counts_in, modes_in)
+    targets = (state, merid, zonal, metric, flags, counts, modes)
     copies = [
         pltpu.make_async_copy(source, target, sems.at[i])
         for i, (source, target) in enumerate(zip(sources, targets))
@@ -207,19 +208,24 @@
         pad[1, f : f + 1, :cells] = state[f, :1, :]
     pad[0, fields : fields + 1, :cells] = merid[rows - 1 :, :]
     odd = band % 2 == 1
-    for a, (last, first) in enumerate(zip(slabs_of(pad[0]), slabs_of(pad[1]))):
+    for a, (last, first) in enumerate(zip(slabs_of(pad[0, :8, :]), slabs_of(pad[1, :8, :]))):
         here = slice(8 * a, 8 * a + 8)
         top[here, :], bottom[here, :] = last, first
         far[here, :] = jnp.where(odd, last, first)
         near[here, :] = jnp.where(odd, first, last)
-
-
-def increment_kernel(
-    state, zonal, merid, metric, flags, counts, reduced, scale, chunks, own, pad
-):
+    pl.when(odd)(lambda: increments(state, zonal, merid, metric, flags, counts, modes, chunks, own, pad))
+
+
+def even_kernel(*refs):
+    even = lax.axis_index("lat") % 2 == 0
+    pl.when(even)(lambda: increments(*refs))
+
+
+def increments(state, zonal, merid, metric, flags, counts, modes, chunks_out, own, pad):
     fields, rows, cells = state.shape
     wide = 128 * SLABS
     band, sector = lax.axis_index("lat"), lax.axis_index("lon")
+    chunks = chunks_out.reshape(rows * CHUNK, 128)
     for f in range(fields + 2):
         pad[f, :, wide - 128 :] = jnp.zeros((rows, 128), jnp.float32)
     for f in range(fields):
@@ -248,10 +254,7 @@
         part = jnp.where(lane == cells + 1, pltpu.roll(q, 2, 1), part)
         part = jnp.where(lane == cells + 2, last_wind, part)
         for a, slab in enumerate(slabs_of(part)):
-            chunks[pl.ds(8 * a + f, rows, stride=ROWS), :] = slab
-    for f in range(fields, 8):
-        for a in range(SLABS):
-            chunks[pl.ds(8 * a + f, rows, stride=ROWS), :] = jnp.zeros((rows, 128), jnp.float32)
+            chunks[pl.ds(fields * a + f, rows, stride=CHUNK), :] = slab
     place = lax.broadcasted_iota(jnp.int32, flags.shape, 0) * 128 + lax.broadcasted_iota(jnp.int32, flags.shape, 1)
     chosen = place == band * rows + sector
 
@@ -260,14 +263,16 @@
         return jnp.sum(jnp.sum(picked, axis=1, keepdims=True), axis=0, keepdims=True)
 
     flag, count = pick(flags), pick(counts)
-    raised = jnp.maximum(count + 1.0 - reduced[...], 0.0)
-    own[:8, :] = raised / jnp.maximum(count, 1.0) * flag * scale[...]
+    raised = jnp.maximum(count + 1.0 - modes[:8, :], 0.0)
+    own[:8, :] = raised / jnp.maximum(count, 1.0) * flag * modes[8:, :]
     mine = jnp.where(row == sector, zonal_factor, 0.0)[:, :256]
     own[8:, :] = jnp.broadcast_to(jnp.sum(mine, axis=0, keepdims=True), (8, 256))
 
 
-def border_fluxes_kernel(part, top_in, bottom_in, both, from_far, metric, chunks):
-    fields, last, rows = 6, part.shape[0] - ROWS, metric.shape[0]
+def border_fluxes_kernel(
+    odd_part, even_part, odd_own, even_own, top_in, bottom_in, both, from_far, metric, chunks_out, own
+):
+    fields, rows = 6, metric.shape[0]
     inside = lax.broadcasted_iota(jnp.int32, (8, 128), 1) < SLAB
 
     def spread(row, index):
@@ -276,17 +281,33 @@
     first_factor, last_factor = spread(0, 1), spread(rows - 1, 1)
     first_face, last_face = spread(0, 3), spread(rows - 1, 2)
     odd = spread(0, 4) > 0.5
-    chunks[...] = part[...]
+    chunks = chunks_out.reshape(rows * CHUNK, 128)
+    is_odd = lax.axis_index("lat") % 2 == 1
+
+    @pl.when(is_odd)
+    def _():
+        chunks_out[...] = odd_part[...]
+        own[...] = odd_own[...]
+
+    @pl.when(jnp.logical_not(is_odd))
+    def _():
+        chunks_out[...] = even_part[...]
+        own[...] = even_own[...]
+
     for a in range(SLABS):
         here = slice(8 * a, 8 * a + 8)
         top, bottom = top_in[here, :], bottom_in[here, :]
-        mine, next_chip = jnp.where(odd, both[here, :], both[ROWS + 8 * a : ROWS + 8 * a + 8, :]), from_far[here, :]
-        north, south = jnp.where(odd, next_chip, mine), jnp.where(odd, mine, next_chip)
+        other = jnp.where(odd, both[here, :], both[ROWS + 8 * a : ROWS + 8 * a + 8, :])
+        next_chip = from_far[here, :]
+        north, south = jnp.where(odd, next_chip, other), jnp.where(odd, other, next_chip)
         flux = (south[fields : fields + 1, :] * first_face) * (0.5 * (south + bottom))
-        chunks[here, :] = part[here, :] + jnp.where(inside, first_factor * flux, 0.0)
+        flux = jnp.where(inside, first_factor * flux, 0.0)
+        there = slice(fields * a, fields * (a + 1))
+        chunks[there, :] = chunks[there, :] + flux[:fields]
         flux = (top[fields : fields + 1, :] * last_face) * (0.5 * (top + north))
-        there = slice(last + 8 * a, last + 8 * a + 8)
-        chunks[there, :] = part[there, :] - jnp.where(inside, last_factor * flux, 0.0)
+        flux = jnp.where(inside, last_factor * flux, 0.0)
+        there = slice((rows - 1) * CHUNK + fields * a, (rows - 1) * CHUNK + fields * (a + 1))
+        chunks[there, :] = chunks[there, :] - flux[:fields]
 
 
 def split(x):
@@ -299,14 +320,18 @@
         return lax.dot_general(p, q, (dims, ((), ())), preferred_element_type=jnp.float32)
 
     x_high, x_low = split(x)
-    return dot(x_high, high) + (dot(x_low, high) + dot(x_high, low))
-
-
-def filter_kernel(chunks, own, high, low, result):
-    sectors = chunks.shape[0]
+    both = dot(jnp.concatenate([x_high, x_low], axis=0), high)
+    return both[: x.shape[0]] + (both[x.shape[0] :] + dot(x_high, low))
+
+
+def filter_kernel(chunks_in, own, high, low, result_out):
+    sectors, fields = chunks_in.shape[0], 6
+    chunks = chunks_in.reshape(sectors * CHUNK, 128)
+    result = result_out.reshape(sectors * CHUNK, 128)
     lane = lax.broadcasted_iota(jnp.int32, (8, 128), 1)
     zonal_factor = own[8:, :128]
-    points = [chunks[p // 3, 8 * (p % 3) : 8 * (p % 3) + 8, :] for p in range(POINTS)]
+    points = [chunks[fields * p : fields * p + 8, :] for p in range(POINTS - 1)]
+    points.append(pltpu.roll(chunks[sectors * CHUNK - 8 :, :], 6, 0))
     lasts = [points[3 * s + 2] for s in range(sectors)]
     for s in range(sectors):
         after = (s + 1) % sectors
@@ -317,7 +342,7 @@
         points[3 * s + 2] = points[3 * s + 2] - edge
         points[3 * after] = points[3 * after] + pltpu.roll(edge, 128 - (SLAB - 1), 1)
     for p in range(POINTS):
-        result[p // 3, 8 * (p % 3) : 8 * (p % 3) + 8, :] = points[p]
+        result[fields * p : fields * (p + 1), :] = points[p][:fields]
     spectrum = circle_forward(points)
     spectrum[0] = (spectrum[0][0], spectrum[24][0])
     block = lax.broadcasted_iota(jnp.int32, (64, 256), 0) // 8
@@ -337,15 +362,16 @@
     back[0] = (back[0][0], None)
     correction = circle_backward(back)
     for p in range(POINTS):
-        place = (p // 3, slice(8 * (p % 3), 8 * (p % 3) + 8), slice(None))
-        result[place] = result[place] - correction[p]
-
-
-def final_kernel(chunks, state, advanced):
+        place = slice(fields * p, fields * (p + 1))
+        result[place, :] = result[place, :] - correction[p][:fields]
+
+
+def final_kernel(chunks_in, state, advanced):
     fields, rows, cells = state.shape
+    chunks = chunks_in.reshape(rows * CHUNK, 128)
     lane = lax.broadcasted_iota(jnp.int32, (rows, 128), 1)
     for f in range(fields):
-        s0, s1, s2 = (chunks[pl.ds(8 * a + f, rows, stride=ROWS), :] for a in range(SLABS))
+        s0, s1, s2 = (chunks[pl.ds(fields * a + f, rows, stride=CHUNK), :] for a in range(SLABS))
         s1, s2 = pltpu.roll(s1, 120, 1), pltpu.roll(s2, 112, 1)
         advanced[f, :, :128] = state[f, :, :128] + jnp.where(lane < 120, s0, s1)
         advanced[f, :, 128:256] = state[f, :, 128:256] + jnp.where(lane < 112, s1, s2)
@@ -384,52 +410,47 @@
     zonal, merid = (w.reshape(lat_cells, lon_cells) for w in (zonal_wind, meridional_wind))
     high, low, reduced, scale = mode_layout(circle, circle // 16)
 
-    def eight(rows):
-        return jnp.asarray(np.pad(rows.astype(np.float32), ((0, 8 - rows.shape[0]), (0, 0))))
-
+    modes = np.concatenate([np.pad(rows, ((0, 8 - GROUPS), (0, 0))) for rows in (reduced, scale)])
+    modes = jnp.asarray(modes.astype(np.float32))
     flags, counts = filter_flag.reshape(-1, 128), mode_count.reshape(-1, 128)
     border = floats(ROWS, 128)
-    far, near, top, bottom, fields, zonal, merid, metric, flags, counts = call(
+    metric, own = floats(lat_cells, 128), floats(16, 256)
+    packed = floats(sectors, CHUNK // 2, 2, 128)
+    pad = pltpu.VMEM((8, lat_cells, wide), jnp.float32)
+    here = (fields, zonal, merid, jnp.asarray(row_metrics(nlat, band_total)), flags, counts, modes)
+    far, near, top, bottom, *here, odd_part, odd_own = call(
         border_kernel,
         "borders",
-        [border, border, border, border, fields, zonal, merid, floats(lat_cells, 128), flags, counts],
-        3,
-        (fields, zonal, merid, jnp.asarray(row_metrics(nlat, band_total)), flags, counts),
-        6,
-        [pltpu.VMEM((2, 8, wide), jnp.float32), pltpu.SemaphoreType.DMA((6,))],
-    )
+        [border] * 4 + [fields, zonal, merid, metric, flags, counts, modes, packed, own],
+        4,
+        here,
+        7,
+        [pad, pltpu.SemaphoreType.DMA((7,))],
+    )
+    fields, zonal, merid, metric = here[:4]
     pairs = [(i, i + 1) for i in range(1, band_total - 1, 2)]
     from_far = lax.ppermute(far, "lat", pairs + [(target, source) for source, target in pairs])
     chips = [[i, i + 1] for i in range(0, band_total, 2)]
     both = lax.all_gather(near, "lat", axis=0, tiled=True, axis_index_groups=chips)
 
-    packed = (sectors * ROWS, 128)
-    part, own = call(
-        increment_kernel,
-        "increments",
-        [floats(*packed), floats(16, 256)],
-        4,
-        (fields, zonal, merid, metric, flags, counts, eight(reduced), eight(scale)),
-        0,
-        [pltpu.VMEM((8, lat_cells, wide), jnp.float32)],
-    )
-    (chunks,) = call(
+    even_part, even_own = call(even_kernel, "even_increments", [packed, own], 4, tuple(here), 0, [pad])
+    chunks, own = call(
         border_fluxes_kernel,
         "border_fluxes",
-        [floats(*packed)],
-        2,
-        (part, top, bottom, both, from_far, metric),
-    )
-    chunks = lax.all_to_all(chunks.reshape(sectors, ROWS, 128), "lon", 0, 0, tiled=True)
+        [packed, own],
+        4,
+        (odd_part, even_part, odd_own, even_own, top, bottom, both, from_far, metric),
+    )
+    chunks = lax.all_to_all(chunks, "lon", 0, 0, tiled=True)
     (chunks,) = call(
         filter_kernel,
         "filter_rows",
-        [floats(sectors, ROWS, 128)],
+        [packed],
         8,
         (chunks, own, jnp.asarray(high), jnp.asarray(low)),
     )
     chunks = lax.all_to_all(chunks, "lon", 0, 0, tiled=True)
-    (advanced,) = call(final_kernel, "advance", [fields], 4, (chunks.reshape(packed), fields))
+    (advanced,) = call(final_kernel, "advance", [fields], 4, (chunks, fields))
     return advanced.reshape(state.shape)
 
 

time: 37.2 us -> 36 us (0.968)
  blocking collectives: 31.5 us -> 30.5 us
    all_to_all x1 -> x0, blocking collectives: 15.3 us -> none  [body(): lax.all_to_all(chunks.reshape(sectors, ROWS, 128), 'lon', 0, 0, tiled=True)]
    all_to_all x1 -> x2, blocking collectives: 11.5 us -> 26 us  [body(): chunks = lax.all_to_all(chunks, 'lon', 0, 0, tiled=True)]
where the time goes in v6:
time: 36 us; the launch traced here: 35.8 us
  blocking collectives  30.5 us (85%)
  Pallas kernels  3.31 us (9%)
  starting transfers between devices  1.92 us (5%)
    all_to_all x2, blocking collectives, body(): chunks = lax.all_to_all(chunks, 'lon', 0, 0, tiled=True)  26 us
    all_gather x1, blocking collectives, body(): lax.all_gather(near, 'lat', axis=0, tiled=True, axis_index_groups=chips)  4.45 us
    pallas_call x5, Pallas kernels, call(): pl.pallas_call(kernel, out_shape=[jax.ShapeDtypeStruct(out.shape, out.dty...  3.31 us
    ppermute x1, starting transfers between devices, body(): lax.ppermute(far, 'lat', pairs + [(target, source) for source, target in...  1.92 us
  transfers between devices with their start and end apart: 1, of which 0 were waited for; matrix products, arithmetic and copies ran while one was open for 0% of the time, Pallas kernels for 1%

profile of v6, /device:TPU:96, one launch (start us, length us, event | category | flops | bytes accessed | tf_op | source)
XLA Modules:
  0.0 35.8 jit_solution(5565685993705470887)
XLA Ops:
  0.0 1.1 %borders.1 = (f32[24,128]{1,0:T(8,128)S(1)}, f32[24,128]{1,0:T(8,128)S(1)}, f32[24,128]{1,0:T(8,128)S(1)}, f32[24,128]{1,0:T(8,128)S(1)}, f32[6,16,360]{2,1,0:T(...) custom-call(f32[6,16,360]{2,1,0:T(8,128)} %bitcast.8, ...), custom_call_target="tpu_custom_call" | custom-call | tf_op jit(solution)/shard_map/borders/pallas_call | solution.py:392
  1.1 1.9 %collective-permute-start = (f32[24,128]{1,0:T(8,128)S(1)}, f32[24,128]{1,0:T(8,128)S(1)}, u32[]{:S(2)}, u32[]{:S(2)}) collective-permute-start(f32[24,128]{1,0:T(8,128)S(1)} %get-tuple-element.36), channel_id=1, source_target_pairs={{16,32},{48,64},{80,96},{112,128},{144,160},{176,192},{208,224},{2... | collective-permute-start | bytes 36872 | tf_op jit(solution)/shard_map/ppermute | solution.py:432
  3.0 0.0 copy-start.1
  3.0 0.4 %even_increments.1 = (f32[16,9,2,128]{3,2,1,0:T(2,128)S(1)}, f32[16,256]{1,0:T(8,128)S(1)}) custom-call(f32[6,16,360]{2,1,0:T(8,128)S(1)} %get-tuple-element.23.refs_0_.state, f32[16,360]{1,0:T(8,128)S(1)} %get-tuple-element.24.refs_1_, f32[16,360]{1,0:T(8,128)S(1)} %get-tuple-element.25.refs_2_, f32[16,128]{1,0:T(8,128)S(1)} %get-tuple-element.26.refs_3_.metric, ...), custom_call_target="tpu_custom_call" | custom-call | tf_op jit(solution)/shard_map/even_increments/pallas_call | solution.py:392
  3.5 0.0 copy-start
  3.5 4.4 %all_gather.3.both = f32[48,128]{1,0:T(8,128)S(1)} all-gather(f32[24,128]{1,0:T(8,128)S(1)} %get-tuple-element.35), channel_id=1, replica_groups={{0,16},{32,48},{64,80},{96,112},{128,144},{160,176},{192,208},{224,240}..., dimensions={0}, use_global_device_ids=true | all-gather | bytes 36864 | tf_op jit(solution)/shard_map/all_gather | solution.py:434
  7.9 0.0 collective-permute-done.from_far
  7.9 0.1 border_fluxes.1
  8.1 14.8 %all_to_all.10.chunks_in = f32[16,9,2,128]{3,2,1,0:T(2,128)S(1)} all-to-all(f32[16,9,2,128]{3,2,1,0:T(2,128)S(1)} %get-tuple-element.37), channel_id=1, replica_groups=mesh['lat'=32,'lon'=16] {'lon'}, dimensions={0} | all-to-all | bytes 294912 | tf_op jit(solution)/shard_map/all_to_all | solution.py:444
  22.8 0.0 copy-done.1
  22.8 0.0 copy-done
  22.8 0.9 %filter_rows.1 = f32[16,9,2,128]{3,2,1,0:T(2,128)S(1)} custom-call(f32[16,9,2,128]{3,2,1,0:T(2,128)S(1)} %all_to_all.10.chunks_in, f32[16,256]{1,0:T(8,128)S(1)} %get-tuple-element.38.own, bf16[3,256,256]{2,1,0:T(8,128)(2,1)S(1)} %copy-done.1, bf16[3,256,256]{2,1,0:T(8,128)(2,1)S(1)} %copy-done), custom_call_target="tpu_custom_call" | custom-call | tf_op jit(solution)/shard_map/filter_rows/pallas_call | solution.py:392
  23.8 11.3 %all_to_all.11.chunks_in = f32[16,9,2,128]{3,2,1,0:T(2,128)S(1)} all-to-all(f32[16,9,2,128]{3,2,1,0:T(2,128)S(1)} %filter_rows.1), channel_id=1, replica_groups=mesh['lat'=32,'lon'=16] {'lon'}, dimensions={0} | all-to-all | bytes 294912 | tf_op jit(solution)/shard_map/all_to_all | solution.py:452
  35.0 0.8 %advance.1 = f32[6,16,360]{2,1,0:T(8,128)} custom-call(f32[16,9,2,128]{3,2,1,0:T(2,128)S(1)} %all_to_all.11.chunks_in, f32[6,16,360]{2,1,0:T(8,128)S(1)} %get-tuple-element.23.refs_0_.state), custom_call_target="tpu_custom_call" | custom-call | tf_op jit(solution)/shard_map/advance/pallas_call | solution.py:392
Async XLA Ops:
  1.1 6.8 %collective-permute-start = (f32[24,128]{1,0:T(8,128)S(1)}, f32[24,128]{1,0:T(8,128)S(1)}, u32[]{:S(2)}, u32[]{:S(2)}) collective-permute-start(f32[24,128]{1,0:T(8,128)S(1)} %get-tuple-element.36), channel_id=1, source_target_pairs={{16,32},{48,64},{80,96},{112,128},{144,160},{176,192},{208,224},{2... | collective-permute-start | bytes 36872 | tf_op jit(solution)/shard_map/ppermute | solution.py:432
  3.0 19.8 %copy-start.1 = (bf16[3,256,256]{2,1,0:T(8,128)(2,1)S(1)}, bf16[3,256,256]{2,1,0:T(8,128)(2,1)}, u32[]{:S(2)}) copy-start(bf16[3,256,256]{2,1,0:T(8,128)(2,1)} %constant.10.clone.high) | copy-start | bytes 1179652
  3.5 19.4 %copy-start = (bf16[3,256,256]{2,1,0:T(8,128)(2,1)S(1)}, bf16[3,256,256]{2,1,0:T(8,128)(2,1)}, u32[]{:S(2)}) copy-start(bf16[3,256,256]{2,1,0:T(8,128)(2,1)} %constant.11.clone.low) | copy-start | bytes 1179652

commit v7 on v6

--- a/solution.py
+++ b/solution.py
@@ -192,8 +192,10 @@
 ):
     fields, rows, cells = state.shape
     band = lax.axis_index("lat")
-    sources = (state_in, merid_in, zonal_in, table.at[band], flags_in, counts_in, modes_in)
-    targets = (state, merid, zonal, metric, flags, counts, modes)
+    sources = [state_in.at[f] for f in range(fields)]
+    targets = [state.at[f] for f in range(fields)]
+    sources += [merid_in, zonal_in, table.at[band], flags_in, counts_in, modes_in]
+    targets += [merid, zonal, metric, flags, counts, modes]
     copies = [
         pltpu.make_async_copy(source, target, sems.at[i])
         for i, (source, target) in enumerate(zip(sources, targets))
@@ -201,7 +203,7 @@
     for copy in copies:
         copy.start()
     pad[...] = jnp.zeros(pad.shape, jnp.float32)
-    for copy in copies:
+    for copy in copies[: fields + 1]:
         copy.wait()
     for f in range(fields):
         pad[0, f : f + 1, :cells] = state[f, rows - 1 :, :]
@@ -213,12 +215,20 @@
         top[here, :], bottom[here, :] = last, first
         far[here, :] = jnp.where(odd, last, first)
         near[here, :] = jnp.where(odd, first, last)
-    pl.when(odd)(lambda: increments(state, zonal, merid, metric, flags, counts, modes, chunks, own, pad))
-
-
-def even_kernel(*refs):
-    even = lax.axis_index("lat") % 2 == 0
-    pl.when(even)(lambda: increments(*refs))
+    for copy in copies[fields + 1 :]:
+        copy.wait()
+    pl.when(works_early())(
+        lambda: increments(state, zonal, merid, metric, flags, counts, modes, chunks, own, pad)
+    )
+
+
+def works_early():
+    band = lax.axis_index("lat")
+    return jnp.logical_and(band % 2 == 1, band < lax.axis_size("lat") // 2)
+
+
+def late_kernel(*refs):
+    pl.when(jnp.logical_not(works_early()))(lambda: increments(*refs))
 
 
 def increments(state, zonal, merid, metric, flags, counts, modes, chunks_out, own, pad):
@@ -270,7 +280,7 @@
 
 
 def border_fluxes_kernel(
-    odd_part, even_part, odd_own, even_own, top_in, bottom_in, both, from_far, metric, chunks_out, own
+    early_part, late_part, early_own, late_own, top_in, bottom_in, both, from_far, metric, chunks_out, own
 ):
     fields, rows = 6, metric.shape[0]
     inside = lax.broadcasted_iota(jnp.int32, (8, 128), 1) < SLAB
@@ -282,17 +292,17 @@
     first_face, last_face = spread(0, 3), spread(rows - 1, 2)
     odd = spread(0, 4) > 0.5
     chunks = chunks_out.reshape(rows * CHUNK, 128)
-    is_odd = lax.axis_index("lat") % 2 == 1
-
-    @pl.when(is_odd)
+    early = works_early()
+
+    @pl.when(early)
     def _():
-        chunks_out[...] = odd_part[...]
-        own[...] = odd_own[...]
-
-    @pl.when(jnp.logical_not(is_odd))
+        chunks_out[...] = early_part[...]
+        own[...] = early_own[...]
+
+    @pl.when(jnp.logical_not(early))
     def _():
-        chunks_out[...] = even_part[...]
-        own[...] = even_own[...]
+        chunks_out[...] = late_part[...]
+        own[...] = late_own[...]
 
     for a in range(SLABS):
         here = slice(8 * a, 8 * a + 8)
@@ -348,15 +358,17 @@
     block = lax.broadcasted_iota(jnp.int32, (64, 256), 0) // 8
     column = lax.broadcasted_iota(jnp.int32, (64, 256), 1) // 32
     back = [None] * 25
-    for g in range(GROUPS):
-        rows = jnp.concatenate(
-            [jnp.concatenate(spectrum[8 * g + i], axis=1) for i in range(8)], axis=0
-        )
-        modes = product(rows, high[g], low[g], ((1,), (0,)))
-        modes = jnp.where(block == column, modes * own[g : g + 1, :], 0.0)
-        rows = product(modes, high[g], low[g], ((1,), (1,)))
+    groups = range(GROUPS)
+    rows = [
+        jnp.concatenate([jnp.concatenate(spectrum[8 * g + i], axis=1) for i in range(8)], axis=0)
+        for g in groups
+    ]
+    modes = [product(rows[g], high[g], low[g], ((1,), (0,))) for g in groups]
+    modes = [jnp.where(block == column, modes[g] * own[g : g + 1, :], 0.0) for g in groups]
+    rows = [product(modes[g], high[g], low[g], ((1,), (1,))) for g in groups]
+    for g in groups:
         for i in range(8):
-            part = rows[8 * i : 8 * i + 8, :]
+            part = rows[g][8 * i : 8 * i + 8, :]
             back[8 * g + i] = (part[:, :128], part[:, 128:])
     back[24] = (back[0][1], None)
     back[0] = (back[0][0], None)
@@ -418,14 +430,14 @@
     packed = floats(sectors, CHUNK // 2, 2, 128)
     pad = pltpu.VMEM((8, lat_cells, wide), jnp.float32)
     here = (fields, zonal, merid, jnp.asarray(row_metrics(nlat, band_total)), flags, counts, modes)
-    far, near, top, bottom, *here, odd_part, odd_own = call(
+    far, near, top, bottom, *here, early_part, early_own = call(
         border_kernel,
         "borders",
         [border] * 4 + [fields, zonal, merid, metric, flags, counts, modes, packed, own],
         4,
         here,
         7,
-        [pad, pltpu.SemaphoreType.DMA((7,))],
+        [pad, pltpu.SemaphoreType.DMA((item_count + 6,))],
     )
     fields, zonal, merid, metric = here[:4]
     pairs = [(i, i + 1) for i in range(1, band_total - 1, 2)]
@@ -433,13 +445,13 @@
     chips = [[i, i + 1] for i in range(0, band_total, 2)]
     both = lax.all_gather(near, "lat", axis=0, tiled=True, axis_index_groups=chips)
 
-    even_part, even_own = call(even_kernel, "even_increments", [packed, own], 4, tuple(here), 0, [pad])
+    late_part, late_own = call(late_kernel, "increments", [packed, own], 4, tuple(here), 0, [pad])
     chunks, own = call(
         border_fluxes_kernel,
         "border_fluxes",
         [packed, own],
         4,
-        (odd_part, even_part, odd_own, even_own, top, bottom, both, from_far, metric),
+        (early_part, late_part, early_own, late_own, top, bottom, both, from_far, metric),
     )
     chunks = lax.all_to_all(chunks, "lon", 0, 0, tiled=True)
     (chunks,) = call(

time: 36 us -> 35.9 us (level)
  the two profiles are of different devices: /device:TPU:96 before, /device:TPU:224 now
where the time goes in v7:
time: 35.9 us; the launch traced here: 35.6 us
  blocking collectives  30.5 us (85%)
  Pallas kernels  3.15 us (9%)
  starting transfers between devices  1.92 us (5%)
    all_to_all x2, blocking collectives, body(): chunks = lax.all_to_all(chunks, 'lon', 0, 0, tiled=True)  26 us
    all_gather x1, blocking collectives, body(): lax.all_gather(near, 'lat', axis=0, tiled=True, axis_index_groups=chips)  4.45 us
    pallas_call x5, Pallas kernels, call(): pl.pallas_call(kernel, out_shape=[jax.ShapeDtypeStruct(out.shape, out.dty...  3.15 us
    ppermute x1, starting transfers between devices, body(): lax.ppermute(far, 'lat', pairs + [(target, source) for source, target in...  1.92 us
  transfers between devices with their start and end apart: 1, of which 0 were waited for; matrix products, arithmetic and copies ran while one was open for 0% of the time, Pallas kernels for 1%

profile of v7, /device:TPU:224, one launch (start us, length us, event | category | flops | bytes accessed | tf_op | source)
XLA Modules:
  0.0 35.6 jit_solution(17972818700027203311)
XLA Ops:
  0.0 1.0 %borders.1 = (f32[24,128]{1,0:T(8,128)S(1)}, f32[24,128]{1,0:T(8,128)S(1)}, f32[24,128]{1,0:T(8,128)S(1)}, f32[24,128]{1,0:T(8,128)S(1)}, f32[6,16,360]{2,1,0:T(...) custom-call(f32[6,16,360]{2,1,0:T(8,128)} %bitcast.8, ...), custom_call_target="tpu_custom_call" | custom-call | tf_op jit(solution)/shard_map/borders/pallas_call | solution.py:404
  1.1 1.9 %collective-permute-start = (f32[24,128]{1,0:T(8,128)S(1)}, f32[24,128]{1,0:T(8,128)S(1)}, u32[]{:S(2)}, u32[]{:S(2)}) collective-permute-start(f32[24,128]{1,0:T(8,128)S(1)} %get-tuple-element.36), channel_id=1, source_target_pairs={{16,32},{48,64},{80,96},{112,128},{144,160},{176,192},{208,224},{2... | collective-permute-start | bytes 36872 | tf_op jit(solution)/shard_map/ppermute | solution.py:444
  3.0 0.0 copy-start.1
  3.0 0.4 %increments.1 = (f32[16,9,2,128]{3,2,1,0:T(2,128)S(1)}, f32[16,256]{1,0:T(8,128)S(1)}) custom-call(f32[6,16,360]{2,1,0:T(8,128)S(1)} %get-tuple-element.23.refs_0_.state, f32[16,360]{1,0:T(8,128)S(1)} %get-tuple-element.24.refs_1_, f32[16,360]{1,0:T(8,128)S(1)} %get-tuple-element.25.refs_2_, f32[16,128]{1,0:T(8,128)S(1)} %get-tuple-element.26.refs_3_.metric, ...), custom_call_target="tpu_custom_call" | custom-call | tf_op jit(solution)/shard_map/increments/pallas_call | solution.py:404
  3.4 0.0 copy-start
  3.4 4.4 %all_gather.3.both = f32[48,128]{1,0:T(8,128)S(1)} all-gather(f32[24,128]{1,0:T(8,128)S(1)} %get-tuple-element.35), channel_id=1, replica_groups={{0,16},{32,48},{64,80},{96,112},{128,144},{160,176},{192,208},{224,240}..., dimensions={0}, use_global_device_ids=true | all-gather | bytes 36864 | tf_op jit(solution)/shard_map/all_gather | solution.py:446
  7.9 0.0 collective-permute-done.from_far
  7.9 0.1 border_fluxes.1
  8.0 14.8 %all_to_all.10.chunks_in = f32[16,9,2,128]{3,2,1,0:T(2,128)S(1)} all-to-all(f32[16,9,2,128]{3,2,1,0:T(2,128)S(1)} %get-tuple-element.37), channel_id=1, replica_groups=mesh['lat'=32,'lon'=16] {'lon'}, dimensions={0} | all-to-all | bytes 294912 | tf_op jit(solution)/shard_map/all_to_all | solution.py:456
  22.8 0.0 copy-done.1
  22.8 0.0 copy-done
  22.8 0.8 %filter_rows.1 = f32[16,9,2,128]{3,2,1,0:T(2,128)S(1)} custom-call(f32[16,9,2,128]{3,2,1,0:T(2,128)S(1)} %all_to_all.10.chunks_in, f32[16,256]{1,0:T(8,128)S(1)} %get-tuple-element.38.own, bf16[3,256,256]{2,1,0:T(8,128)(2,1)S(1)} %copy-done.1, bf16[3,256,256]{2,1,0:T(8,128)(2,1)S(1)} %copy-done), custom_call_target="tpu_custom_call" | custom-call | tf_op jit(solution)/shard_map/filter_rows/pallas_call | solution.py:404
  23.6 11.3 %all_to_all.11.chunks_in = f32[16,9,2,128]{3,2,1,0:T(2,128)S(1)} all-to-all(f32[16,9,2,128]{3,2,1,0:T(2,128)S(1)} %filter_rows.1), channel_id=1, replica_groups=mesh['lat'=32,'lon'=16] {'lon'}, dimensions={0} | all-to-all | bytes 294912 | tf_op jit(solution)/shard_map/all_to_all | solution.py:464
  34.9 0.8 %advance.1 = f32[6,16,360]{2,1,0:T(8,128)} custom-call(f32[16,9,2,128]{3,2,1,0:T(2,128)S(1)} %all_to_all.11.chunks_in, f32[6,16,360]{2,1,0:T(8,128)S(1)} %get-tuple-element.23.refs_0_.state), custom_call_target="tpu_custom_call" | custom-call | tf_op jit(solution)/shard_map/advance/pallas_call | solution.py:404
Async XLA Ops:
  1.1 6.8 %collective-permute-start = (f32[24,128]{1,0:T(8,128)S(1)}, f32[24,128]{1,0:T(8,128)S(1)}, u32[]{:S(2)}, u32[]{:S(2)}) collective-permute-start(f32[24,128]{1,0:T(8,128)S(1)} %get-tuple-element.36), channel_id=1, source_target_pairs={{16,32},{48,64},{80,96},{112,128},{144,160},{176,192},{208,224},{2... | collective-permute-start | bytes 36872 | tf_op jit(solution)/shard_map/ppermute | solution.py:444
  3.0 19.8 %copy-start.1 = (bf16[3,256,256]{2,1,0:T(8,128)(2,1)S(1)}, bf16[3,256,256]{2,1,0:T(8,128)(2,1)}, u32[]{:S(2)}) copy-start(bf16[3,256,256]{2,1,0:T(8,128)(2,1)} %constant.10.clone.high) | copy-start | bytes 1179652
  3.4 19.4 %copy-start = (bf16[3,256,256]{2,1,0:T(8,128)(2,1)S(1)}, bf16[3,256,256]{2,1,0:T(8,128)(2,1)}, u32[]{:S(2)}) copy-start(bf16[3,256,256]{2,1,0:T(8,128)(2,1)} %constant.11.clone.low) | copy-start | bytes 1179652

commit v8 on v7

--- a/solution.py
+++ b/solution.py
@@ -60,6 +60,7 @@
     result[:, 2] = np.sin(((ids + np.float32(1.0)) * step).astype(np.float64))
     result[:, 3] = np.sin((ids * step).astype(np.float64))
     result[:, 4] = np.arange(nlat) // (nlat // bands) % 2
+    result[:, 5] = np.arange(nlat) // (nlat // bands) < bands - 1
     return result.reshape(bands, nlat // bands, 128)
 
 
@@ -188,7 +189,7 @@
 
 def border_kernel(
     state_in, zonal_in, merid_in, table, flags_in, counts_in, modes_in,
-    far, near, top, bottom, state, zonal, merid, metric, flags, counts, modes, chunks, own, pad, sems,
+    borders, state, zonal, merid, metric, flags, counts, modes, pad, sems,
 ):
     fields, rows, cells = state.shape
     band = lax.axis_index("lat")
@@ -209,29 +210,14 @@
         pad[0, f : f + 1, :cells] = state[f, rows - 1 :, :]
         pad[1, f : f + 1, :cells] = state[f, :1, :]
     pad[0, fields : fields + 1, :cells] = merid[rows - 1 :, :]
-    odd = band % 2 == 1
-    for a, (last, first) in enumerate(zip(slabs_of(pad[0, :8, :]), slabs_of(pad[1, :8, :]))):
-        here = slice(8 * a, 8 * a + 8)
-        top[here, :], bottom[here, :] = last, first
-        far[here, :] = jnp.where(odd, last, first)
-        near[here, :] = jnp.where(odd, first, last)
+    for place in range(2):
+        for a, slab in enumerate(slabs_of(pad[place, :8, :])):
+            borders[ROWS * place + 8 * a : ROWS * place + 8 * a + 8, :] = slab
     for copy in copies[fields + 1 :]:
         copy.wait()
-    pl.when(works_early())(
-        lambda: increments(state, zonal, merid, metric, flags, counts, modes, chunks, own, pad)
-    )
-
-
-def works_early():
-    band = lax.axis_index("lat")
-    return jnp.logical_and(band % 2 == 1, band < lax.axis_size("lat") // 2)
-
-
-def late_kernel(*refs):
-    pl.when(jnp.logical_not(works_early()))(lambda: increments(*refs))
-
-
-def increments(state, zonal, merid, metric, flags, counts, modes, chunks_out, own, pad):
+
+
+def increment_kernel(state, zonal, merid, metric, flags, counts, modes, chunks_out, own, pad):
     fields, rows, cells = state.shape
     wide = 128 * SLABS
     band, sector = lax.axis_index("lat"), lax.axis_index("lon")
@@ -279,9 +265,12 @@
     own[8:, :] = jnp.broadcast_to(jnp.sum(mine, axis=0, keepdims=True), (8, 256))
 
 
-def border_fluxes_kernel(
-    early_part, late_part, early_own, late_own, top_in, bottom_in, both, from_far, metric, chunks_out, own
-):
+def passing_kernel(chip, passing):
+    odd = lax.axis_index("lat") % 2 == 1
+    passing[...] = jnp.where(odd, chip[ROWS : 2 * ROWS, :], chip[2 * ROWS : 3 * ROWS, :])
+
+
+def border_fluxes_kernel(part, borders, chip, passed, metric, chunks_out):
     fields, rows = 6, metric.shape[0]
     inside = lax.broadcasted_iota(jnp.int32, (8, 128), 1) < SLAB
 
@@ -290,34 +279,23 @@
 
     first_factor, last_factor = spread(0, 1), spread(rows - 1, 1)
     first_face, last_face = spread(0, 3), spread(rows - 1, 2)
-    odd = spread(0, 4) > 0.5
+    odd, has_north = spread(0, 4) > 0.5, spread(0, 5) > 0.5
     chunks = chunks_out.reshape(rows * CHUNK, 128)
-    early = works_early()
-
-    @pl.when(early)
-    def _():
-        chunks_out[...] = early_part[...]
-        own[...] = early_own[...]
-
-    @pl.when(jnp.logical_not(early))
-    def _():
-        chunks_out[...] = late_part[...]
-        own[...] = late_own[...]
-
+    chunks_out[...] = part[...]
     for a in range(SLABS):
         here = slice(8 * a, 8 * a + 8)
-        top, bottom = top_in[here, :], bottom_in[here, :]
-        other = jnp.where(odd, both[here, :], both[ROWS + 8 * a : ROWS + 8 * a + 8, :])
-        next_chip = from_far[here, :]
-        north, south = jnp.where(odd, next_chip, other), jnp.where(odd, other, next_chip)
+        top, bottom = borders[here, :], borders[ROWS + 8 * a : ROWS + 8 * a + 8, :]
+        south = jnp.where(odd, chip[here, :], passed[here, :])
+        above = chip[3 * ROWS + 8 * a : 3 * ROWS + 8 * a + 8, :]
+        north = jnp.where(has_north, jnp.where(odd, passed[here, :], above), 0.0)
         flux = (south[fields : fields + 1, :] * first_face) * (0.5 * (south + bottom))
         flux = jnp.where(inside, first_factor * flux, 0.0)
-        there = slice(fields * a, fields * (a + 1))
-        chunks[there, :] = chunks[there, :] + flux[:fields]
+        place = slice(fields * a, fields * (a + 1))
+        chunks[place, :] = chunks[place, :] + flux[:fields]
         flux = (top[fields : fields + 1, :] * last_face) * (0.5 * (top + north))
         flux = jnp.where(inside, last_factor * flux, 0.0)
-        there = slice((rows - 1) * CHUNK + fields * a, (rows - 1) * CHUNK + fields * (a + 1))
-        chunks[there, :] = chunks[there, :] - flux[:fields]
+        place = slice((rows - 1) * CHUNK + fields * a, (rows - 1) * CHUNK + fields * (a + 1))
+        chunks[place, :] = chunks[place, :] - flux[:fields]
 
 
 def split(x):
@@ -425,33 +403,29 @@
     modes = np.concatenate([np.pad(rows, ((0, 8 - GROUPS), (0, 0))) for rows in (reduced, scale)])
     modes = jnp.asarray(modes.astype(np.float32))
     flags, counts = filter_flag.reshape(-1, 128), mode_count.reshape(-1, 128)
-    border = floats(ROWS, 128)
     metric, own = floats(lat_cells, 128), floats(16, 256)
     packed = floats(sectors, CHUNK // 2, 2, 128)
     pad = pltpu.VMEM((8, lat_cells, wide), jnp.float32)
     here = (fields, zonal, merid, jnp.asarray(row_metrics(nlat, band_total)), flags, counts, modes)
-    far, near, top, bottom, *here, early_part, early_own = call(
+    borders, *here = call(
         border_kernel,
         "borders",
-        [border] * 4 + [fields, zonal, merid, metric, flags, counts, modes, packed, own],
+        [floats(2 * ROWS, 128), fields, zonal, merid, metric, flags, counts, modes],
         4,
         here,
         7,
         [pad, pltpu.SemaphoreType.DMA((item_count + 6,))],
     )
-    fields, zonal, merid, metric = here[:4]
-    pairs = [(i, i + 1) for i in range(1, band_total - 1, 2)]
-    from_far = lax.ppermute(far, "lat", pairs + [(target, source) for source, target in pairs])
-    chips = [[i, i + 1] for i in range(0, band_total, 2)]
-    both = lax.all_gather(near, "lat", axis=0, tiled=True, axis_index_groups=chips)
-
-    late_part, late_own = call(late_kernel, "increments", [packed, own], 4, tuple(here), 0, [pad])
-    chunks, own = call(
-        border_fluxes_kernel,
-        "border_fluxes",
-        [packed, own],
-        4,
-        (early_part, late_part, early_own, late_own, top, bottom, both, from_far, metric),
+    fields, metric = here[0], here[3]
+    cores = [[i, i + 1] for i in range(0, band_total, 2)]
+    chip = lax.all_gather(borders, "lat", axis=0, tiled=True, axis_index_groups=cores)
+    (passing,) = call(passing_kernel, "passing", [floats(ROWS, 128)], 2, (chip,))
+    ring = [(i, i + 2) for i in range(0, band_total - 2, 2)] + [(band_total - 2, band_total - 1)]
+    ring += [(i, i - 2) for i in range(3, band_total, 2)] + [(1, 0)]
+    passed = lax.ppermute(passing, "lat", ring)
+    part, own = call(increment_kernel, "increments", [packed, own], 4, tuple(here), 0, [pad])
+    (chunks,) = call(
+        border_fluxes_kernel, "border_fluxes", [packed], 4, (part, borders, chip, passed, metric)
     )
     chunks = lax.all_to_all(chunks, "lon", 0, 0, tiled=True)
     (chunks,) = call(

time: 35.9 us -> 35.8 us (level)
  the two profiles are of different devices: /device:TPU:224 before, /device:TPU:256 now
where the time goes in v8:
time: 35.8 us; the launch traced here: 35.5 us
  blocking collectives  27.9 us (78%)
  waiting for transfers between devices  3.46 us (10%)
  Pallas kernels  3.1 us (9%)
  starting transfers between devices  1.03 us (3%)
    all_to_all x2, blocking collectives, body(): chunks = lax.all_to_all(chunks, 'lon', 0, 0, tiled=True)  26 us
    ppermute x1, waiting for transfers between devices, body(): passed = lax.ppermute(passing, 'lat', ring)  3.46 us
    pallas_call x6, Pallas kernels, call(): pl.pallas_call(kernel, out_shape=[jax.ShapeDtypeStruct(out.shape, out.dty...  3.1 us
    all_gather x1, blocking collectives, body(): lax.all_gather(borders, 'lat', axis=0, tiled=True, axis_index_groups=cores)  1.84 us
    ppermute x1, starting transfers between devices, body(): passed = lax.ppermute(passing, 'lat', ring)  1.03 us
  transfers between devices with their start and end apart: 1, of which 1 were waited for; matrix products, arithmetic and copies ran while one was open for 0% of the time, Pallas kernels for 1%

profile of v8, /device:TPU:256, one launch (start us, length us, event | category | flops | bytes accessed | tf_op | source)
XLA Modules:
  0.0 35.5 jit_solution(9744135597318885776)
XLA Ops:
  0.0 1.0 %borders.1 = (f32[48,128]{1,0:T(8,128)S(1)}, f32[6,16,360]{2,1,0:T(8,128)S(1)}, f32[16,360]{1,0:T(8,128)S(1)}, f32[16,360]{1,0:T(8,128)S(1)}, f32[16,128]{1,0:T(...) custom-call(f32[6,16,360]{2,1,0:T(8,128)} %bitcast.8, f32[16,360]{1,0:T(8,128)} %bitcast.9, ...), custom_call_target="tpu_custom_call" | custom-call | tf_op jit(solution)/shard_map/borders/pallas_call | solution.py:382
  1.0 1.8 %all_gather.3.chip = f32[96,128]{1,0:T(8,128)S(1)} all-gather(f32[48,128]{1,0:T(8,128)S(1)} %get-tuple-element.23.borders), channel_id=1, replica_groups={{0,16},{32,48},{64,80},{96,112},{128,144},{160,176},{192,208},{224,240}..., dimensions={0}, use_global_device_ids=true | all-gather | bytes 73728 | tf_op jit(solution)/shard_map/all_gather | solution.py:421
  2.9 1.0 %collective-permute-start = (f32[24,128]{1,0:T(8,128)S(1)}, f32[24,128]{1,0:T(8,128)S(1)}, u32[]{:S(2)}, u32[]{:S(2)}) collective-permute-start(f32[24,128]{1,0:T(8,128)S(1)} %passing.1), channel_id=1, source_target_pairs={{0,32},{32,64},{64,96},{96,128},{128,160},{160,192},{192,224},{224... | collective-permute-start | bytes 36872 | tf_op jit(solution)/shard_map/ppermute | solution.py:425
  3.9 0.0 copy-start.1
  3.9 0.4 %increments.1 = (f32[16,9,2,128]{3,2,1,0:T(2,128)S(1)}, f32[16,256]{1,0:T(8,128)S(1)}) custom-call(f32[6,16,360]{2,1,0:T(8,128)S(1)} %get-tuple-element.15.state, f32[16,360]{1,0:T(8,128)S(1)} %get-tuple-element.16.zonal, f32[16,360]{1,0:T(8,128)S(1)} %get-tuple-element.17.merid, f32[16,128]{1,0:T(8,128)S(1)} %get-tuple-element.18.metric, ...), custom_call_target="tpu_custom_call" | custom-call | tf_op jit(solution)/shard_map/increments/pallas_call | solution.py:382
  4.3 0.0 copy-start
  4.3 3.5 %collective-permute-done.passed = f32[24,128]{1,0:T(8,128)S(1)} collective-permute-done((f32[24,128]{1,0:T(8,128)S(1)}, f32[24,128]{1,0:T(8,128)S(1)}, u32[]{:S(2)}, u32[]{:S(2)}) %collective-permute-start) | collective-permute-done | bytes 12320 | tf_op jit(solution)/shard_map/ppermute | solution.py:425
  7.8 0.1 border_fluxes.1
  7.9 14.7 %all_to_all.10.chunks_in = f32[16,9,2,128]{3,2,1,0:T(2,128)S(1)} all-to-all(f32[16,9,2,128]{3,2,1,0:T(2,128)S(1)} %border_fluxes.1), channel_id=1, replica_groups=mesh['lat'=32,'lon'=16] {'lon'}, dimensions={0} | all-to-all | bytes 294912 | tf_op jit(solution)/shard_map/all_to_all | solution.py:430
  22.7 0.0 copy-done.1
  22.7 0.0 copy-done
  22.7 0.8 %filter_rows.1 = f32[16,9,2,128]{3,2,1,0:T(2,128)S(1)} custom-call(f32[16,9,2,128]{3,2,1,0:T(2,128)S(1)} %all_to_all.10.chunks_in, f32[16,256]{1,0:T(8,128)S(1)} %get-tuple-element.24.own, bf16[3,256,256]{2,1,0:T(8,128)(2,1)S(1)} %copy-done.1, bf16[3,256,256]{2,1,0:T(8,128)(2,1)S(1)} %copy-done), custom_call_target="tpu_custom_call" | custom-call | tf_op jit(solution)/shard_map/filter_rows/pallas_call | solution.py:382
  23.5 11.3 %all_to_all.11.chunks_in = f32[16,9,2,128]{3,2,1,0:T(2,128)S(1)} all-to-all(f32[16,9,2,128]{3,2,1,0:T(2,128)S(1)} %filter_rows.1), channel_id=1, replica_groups=mesh['lat'=32,'lon'=16] {'lon'}, dimensions={0} | all-to-all | bytes 294912 | tf_op jit(solution)/shard_map/all_to_all | solution.py:438
  34.8 0.8 %advance.1 = f32[6,16,360]{2,1,0:T(8,128)} custom-call(f32[16,9,2,128]{3,2,1,0:T(2,128)S(1)} %all_to_all.11.chunks_in, f32[6,16,360]{2,1,0:T(8,128)S(1)} %get-tuple-element.15.state), custom_call_target="tpu_custom_call" | custom-call | tf_op jit(solution)/shard_map/advance/pallas_call | solution.py:382
  (1 shorter events, 0.0 us)
Async XLA Ops:
  2.9 4.9 %collective-permute-start = (f32[24,128]{1,0:T(8,128)S(1)}, f32[24,128]{1,0:T(8,128)S(1)}, u32[]{:S(2)}, u32[]{:S(2)}) collective-permute-start(f32[24,128]{1,0:T(8,128)S(1)} %passing.1), channel_id=1, source_target_pairs={{0,32},{32,64},{64,96},{96,128},{128,160},{160,192},{192,224},{224... | collective-permute-start | bytes 36872 | tf_op jit(solution)/shard_map/ppermute | solution.py:425
  3.9 18.7 %copy-start.1 = (bf16[3,256,256]{2,1,0:T(8,128)(2,1)S(1)}, bf16[3,256,256]{2,1,0:T(8,128)(2,1)}, u32[]{:S(2)}) copy-start(bf16[3,256,256]{2,1,0:T(8,128)(2,1)} %constant.10.clone.high) | copy-start | bytes 1179652
  4.3 18.3 %copy-start = (bf16[3,256,256]{2,1,0:T(8,128)(2,1)S(1)}, bf16[3,256,256]{2,1,0:T(8,128)(2,1)}, u32[]{:S(2)}) copy-start(bf16[3,256,256]{2,1,0:T(8,128)(2,1)} %constant.11.clone.low) | copy-start | bytes 1179652

commit v9 on v8

--- a/solution.py
+++ b/solution.py
@@ -187,43 +187,49 @@
     )
 
 
-def border_kernel(
+def border_kernel(state, merid, borders, last, first, wind, pad, sems):
+    fields, rows, cells = state.shape
+    copies = [
+        pltpu.make_async_copy(state.at[:, rows - 1 :, :], last, sems.at[0]),
+        pltpu.make_async_copy(state.at[:, :1, :], first, sems.at[1]),
+        pltpu.make_async_copy(merid.at[rows - 1 :, :], wind, sems.at[2]),
+    ]
+    for copy in copies:
+        copy.start()
+    pad[...] = jnp.zeros(pad.shape, jnp.float32)
+    for copy in copies:
+        copy.wait()
+    for f in range(fields):
+        pad[0, f : f + 1, :cells] = last[f]
+        pad[1, f : f + 1, :cells] = first[f]
+    pad[0, fields : fields + 1, :cells] = wind[...]
+    for place in range(2):
+        for a, slab in enumerate(slabs_of(pad[place, :8, :])):
+            borders[ROWS * place + 8 * a : ROWS * place + 8 * a + 8, :] = slab
+
+
+def increment_kernel(
     state_in, zonal_in, merid_in, table, flags_in, counts_in, modes_in,
-    borders, state, zonal, merid, metric, flags, counts, modes, pad, sems,
+    chunks_out, own, state, metric, zonal, merid, flags, counts, modes, pad, sems,
 ):
     fields, rows, cells = state.shape
-    band = lax.axis_index("lat")
+    wide = 128 * SLABS
+    band, sector = lax.axis_index("lat"), lax.axis_index("lon")
     sources = [state_in.at[f] for f in range(fields)]
     targets = [state.at[f] for f in range(fields)]
-    sources += [merid_in, zonal_in, table.at[band], flags_in, counts_in, modes_in]
-    targets += [merid, zonal, metric, flags, counts, modes]
+    sources += [zonal_in, merid_in, table.at[band], flags_in, counts_in, modes_in]
+    targets += [zonal, merid, metric, flags, counts, modes]
     copies = [
         pltpu.make_async_copy(source, target, sems.at[i])
         for i, (source, target) in enumerate(zip(sources, targets))
     ]
     for copy in copies:
         copy.start()
-    pad[...] = jnp.zeros(pad.shape, jnp.float32)
-    for copy in copies[: fields + 1]:
-        copy.wait()
-    for f in range(fields):
-        pad[0, f : f + 1, :cells] = state[f, rows - 1 :, :]
-        pad[1, f : f + 1, :cells] = state[f, :1, :]
-    pad[0, fields : fields + 1, :cells] = merid[rows - 1 :, :]
-    for place in range(2):
-        for a, slab in enumerate(slabs_of(pad[place, :8, :])):
-            borders[ROWS * place + 8 * a : ROWS * place + 8 * a + 8, :] = slab
-    for copy in copies[fields + 1 :]:
-        copy.wait()
-
-
-def increment_kernel(state, zonal, merid, metric, flags, counts, modes, chunks_out, own, pad):
-    fields, rows, cells = state.shape
-    wide = 128 * SLABS
-    band, sector = lax.axis_index("lat"), lax.axis_index("lon")
     chunks = chunks_out.reshape(rows * CHUNK, 128)
     for f in range(fields + 2):
         pad[f, :, wide - 128 :] = jnp.zeros((rows, 128), jnp.float32)
+    for copy in copies:
+        copy.wait()
     for f in range(fields):
         pad[f, :, :cells] = state[f]
     pad[fields, :, :cells] = zonal[...]
@@ -407,23 +413,33 @@
     packed = floats(sectors, CHUNK // 2, 2, 128)
     pad = pltpu.VMEM((8, lat_cells, wide), jnp.float32)
     here = (fields, zonal, merid, jnp.asarray(row_metrics(nlat, band_total)), flags, counts, modes)
-    borders, *here = call(
+    line = pltpu.VMEM((item_count, 1, lon_cells), jnp.float32)
+    (borders,) = call(
         border_kernel,
         "borders",
-        [floats(2 * ROWS, 128), fields, zonal, merid, metric, flags, counts, modes],
-        4,
-        here,
-        7,
-        [pad, pltpu.SemaphoreType.DMA((item_count + 6,))],
-    )
-    fields, metric = here[0], here[3]
+        [floats(2 * ROWS, 128)],
+        2,
+        (fields, merid),
+        2,
+        [line, line, pltpu.VMEM((1, lon_cells), jnp.float32), pltpu.VMEM((3, 8, wide), jnp.float32)]
+        + [pltpu.SemaphoreType.DMA((3,))],
+    )
     cores = [[i, i + 1] for i in range(0, band_total, 2)]
     chip = lax.all_gather(borders, "lat", axis=0, tiled=True, axis_index_groups=cores)
     (passing,) = call(passing_kernel, "passing", [floats(ROWS, 128)], 2, (chip,))
     ring = [(i, i + 2) for i in range(0, band_total - 2, 2)] + [(band_total - 2, band_total - 1)]
     ring += [(i, i - 2) for i in range(3, band_total, 2)] + [(1, 0)]
     passed = lax.ppermute(passing, "lat", ring)
-    part, own = call(increment_kernel, "increments", [packed, own], 4, tuple(here), 0, [pad])
+    part, own, fields, metric = call(
+        increment_kernel,
+        "increments",
+        [packed, own, fields, metric],
+        4,
+        here,
+        7,
+        [pltpu.VMEM(x.shape, x.dtype) for x in (zonal, merid, flags, counts, modes)]
+        + [pad, pltpu.SemaphoreType.DMA((item_count + 6,))],
+    )
     (chunks,) = call(
         border_fluxes_kernel, "border_fluxes", [packed], 4, (part, borders, chip, passed, metric)
     )

time: 35.8 us -> 35.6 us (level)
  the two profiles are of different devices: /device:TPU:256 before, /device:TPU:384 now
where the time goes in v9:
time: 35.6 us; the launch traced here: 35.3 us
  blocking collectives  27.9 us (78%)
  Pallas kernels  3.91 us (11%)
  waiting for transfers between devices  2.44 us (7%)
  starting transfers between devices  1.03 us (3%)
    all_to_all x2, blocking collectives, body(): chunks = lax.all_to_all(chunks, 'lon', 0, 0, tiled=True)  26 us
    pallas_call x6, Pallas kernels, call(): pl.pallas_call(kernel, out_shape=[jax.ShapeDtypeStruct(out.shape, out.dty...  3.91 us
    ppermute x1, waiting for transfers between devices, body(): passed = lax.ppermute(passing, 'lat', ring)  2.44 us
    all_gather x1, blocking collectives, body(): lax.all_gather(borders, 'lat', axis=0, tiled=True, axis_index_groups=cores)  1.84 us
    ppermute x1, starting transfers between devices, body(): passed = lax.ppermute(passing, 'lat', ring)  1.03 us
  transfers between devices with their start and end apart: 1, of which 1 were waited for; matrix products, arithmetic and copies ran while one was open for 0% of the time, Pallas kernels for 4%

profile of v9, /device:TPU:384, one launch (start us, length us, event | category | flops | bytes accessed | tf_op | source)
XLA Modules:
  0.0 35.3 jit_solution(530368950580924164)
XLA Ops:
  0.0 0.8 %borders.1 = f32[48,128]{1,0:T(8,128)S(1)} custom-call(f32[6,16,360]{2,1,0:T(8,128)} %bitcast.8, f32[16,360]{1,0:T(8,128)} %bitcast.10), custom_call_target="tpu_custom_call" | custom-call | tf_op jit(solution)/shard_map/borders/pallas_call | solution.py:388
  0.8 1.8 %all_gather.3.chip = f32[96,128]{1,0:T(8,128)S(1)} all-gather(f32[48,128]{1,0:T(8,128)S(1)} %borders.1), channel_id=1, replica_groups={{0,16},{32,48},{64,80},{96,112},{128,144},{160,176},{192,208},{224,240}..., dimensions={0}, use_global_device_ids=true | all-gather | bytes 73728 | tf_op jit(solution)/shard_map/all_gather | solution.py:428
  2.7 1.0 %collective-permute-start = (f32[24,128]{1,0:T(8,128)S(1)}, f32[24,128]{1,0:T(8,128)S(1)}, u32[]{:S(2)}, u32[]{:S(2)}) collective-permute-start(f32[24,128]{1,0:T(8,128)S(1)} %passing.1), channel_id=1, source_target_pairs={{0,32},{32,64},{64,96},{96,128},{128,160},{160,192},{192,224},{224... | collective-permute-start | bytes 36872 | tf_op jit(solution)/shard_map/ppermute | solution.py:432
  3.7 0.0 copy-start.1
  3.7 1.4 %increments.1 = (f32[16,9,2,128]{3,2,1,0:T(2,128)S(1)}, f32[16,256]{1,0:T(8,128)S(1)}, f32[6,16,360]{2,1,0:T(8,128)S(1)}, f32[16,128]{1,0:T(8,128)S(1)}) custom-call(f32[6,16,360]{2,1,0:T(8,128)} %bitcast.9, f32[16,360]{1,0:T(8,128)} %bitcast.12, f32[16,360]{1,0:T(8,128)} %bitcast.11, f32[32,16,128]{2,1,0:T(8,128)} %constant.9.clone.table, ...), custom_call_target="tpu_custom_call" | custom-call | tf_op jit(solution)/shard_map/increments/pallas_call | solution.py:388
  5.1 0.0 copy-start
  5.2 2.4 %collective-permute-done.passed = f32[24,128]{1,0:T(8,128)S(1)} collective-permute-done((f32[24,128]{1,0:T(8,128)S(1)}, f32[24,128]{1,0:T(8,128)S(1)}, u32[]{:S(2)}, u32[]{:S(2)}) %collective-permute-start) | collective-permute-done | bytes 12320 | tf_op jit(solution)/shard_map/ppermute | solution.py:432
  7.6 0.1 border_fluxes.1
  7.7 14.7 %all_to_all.10.chunks_in = f32[16,9,2,128]{3,2,1,0:T(2,128)S(1)} all-to-all(f32[16,9,2,128]{3,2,1,0:T(2,128)S(1)} %border_fluxes.1), channel_id=1, replica_groups=mesh['lat'=32,'lon'=16] {'lon'}, dimensions={0} | all-to-all | bytes 294912 | tf_op jit(solution)/shard_map/all_to_all | solution.py:446
  22.4 0.0 copy-done.1
  22.4 0.0 copy-done
  22.4 0.8 %filter_rows.1 = f32[16,9,2,128]{3,2,1,0:T(2,128)S(1)} custom-call(f32[16,9,2,128]{3,2,1,0:T(2,128)S(1)} %all_to_all.10.chunks_in, f32[16,256]{1,0:T(8,128)S(1)} %get-tuple-element.11.own, bf16[3,256,256]{2,1,0:T(8,128)(2,1)S(1)} %copy-done.1, bf16[3,256,256]{2,1,0:T(8,128)(2,1)S(1)} %copy-done), custom_call_target="tpu_custom_call" | custom-call | tf_op jit(solution)/shard_map/filter_rows/pallas_call | solution.py:388
  23.2 11.3 %all_to_all.11.chunks_in = f32[16,9,2,128]{3,2,1,0:T(2,128)S(1)} all-to-all(f32[16,9,2,128]{3,2,1,0:T(2,128)S(1)} %filter_rows.1), channel_id=1, replica_groups=mesh['lat'=32,'lon'=16] {'lon'}, dimensions={0} | all-to-all | bytes 294912 | tf_op jit(solution)/shard_map/all_to_all | solution.py:454
  34.6 0.8 %advance.1 = f32[6,16,360]{2,1,0:T(8,128)} custom-call(f32[16,9,2,128]{3,2,1,0:T(2,128)S(1)} %all_to_all.11.chunks_in, f32[6,16,360]{2,1,0:T(8,128)S(1)} %get-tuple-element.12.state), custom_call_target="tpu_custom_call" | custom-call | tf_op jit(solution)/shard_map/advance/pallas_call | solution.py:388
  (1 shorter events, 0.0 us)
Async XLA Ops:
  2.7 4.9 %collective-permute-start = (f32[24,128]{1,0:T(8,128)S(1)}, f32[24,128]{1,0:T(8,128)S(1)}, u32[]{:S(2)}, u32[]{:S(2)}) collective-permute-start(f32[24,128]{1,0:T(8,128)S(1)} %passing.1), channel_id=1, source_target_pairs={{0,32},{32,64},{64,96},{96,128},{128,160},{160,192},{192,224},{224... | collective-permute-start | bytes 36872 | tf_op jit(solution)/shard_map/ppermute | solution.py:432
  3.7 18.7 %copy-start.1 = (bf16[3,256,256]{2,1,0:T(8,128)(2,1)S(1)}, bf16[3,256,256]{2,1,0:T(8,128)(2,1)}, u32[]{:S(2)}) copy-start(bf16[3,256,256]{2,1,0:T(8,128)(2,1)} %constant.10.clone.high) | copy-start | bytes 1179652
  5.1 17.3 %copy-start = (bf16[3,256,256]{2,1,0:T(8,128)(2,1)S(1)}, bf16[3,256,256]{2,1,0:T(8,128)(2,1)}, u32[]{:S(2)}) copy-start(bf16[3,256,256]{2,1,0:T(8,128)(2,1)} %constant.11.clone.low) | copy-start | bytes 1179652

commit v10 on v9

--- a/solution.py
+++ b/solution.py
@@ -209,16 +209,16 @@
 
 
 def increment_kernel(
-    state_in, zonal_in, merid_in, table, flags_in, counts_in, modes_in,
-    chunks_out, own, state, metric, zonal, merid, flags, counts, modes, pad, sems,
+    state_in, zonal_in, merid_in, table, flags_in, counts_in, modes_in, waves_in,
+    chunks_out, own, state, metric, waves, zonal, merid, flags, counts, modes, pad, sems,
 ):
     fields, rows, cells = state.shape
     wide = 128 * SLABS
     band, sector = lax.axis_index("lat"), lax.axis_index("lon")
     sources = [state_in.at[f] for f in range(fields)]
     targets = [state.at[f] for f in range(fields)]
-    sources += [zonal_in, merid_in, table.at[band], flags_in, counts_in, modes_in]
-    targets += [zonal, merid, metric, flags, counts, modes]
+    sources += [zonal_in, merid_in, table.at[band], flags_in, counts_in, modes_in, waves_in]
+    targets += [zonal, merid, metric, flags, counts, modes, waves]
     copies = [
         pltpu.make_async_copy(source, target, sems.at[i])
         for i, (source, target) in enumerate(zip(sources, targets))
@@ -228,7 +228,7 @@
     chunks = chunks_out.reshape(rows * CHUNK, 128)
     for f in range(fields + 2):
         pad[f, :, wide - 128 :] = jnp.zeros((rows, 128), jnp.float32)
-    for copy in copies:
+    for copy in copies[:-1]:
         copy.wait()
     for f in range(fields):
         pad[f, :, :cells] = state[f]
@@ -269,6 +269,7 @@
     own[:8, :] = raised / jnp.maximum(count, 1.0) * flag * modes[8:, :]
     mine = jnp.where(row == sector, zonal_factor, 0.0)[:, :256]
     own[8:, :] = jnp.broadcast_to(jnp.sum(mine, axis=0, keepdims=True), (8, 256))
+    copies[-1].wait()
 
 
 def passing_kernel(chip, passing):
@@ -309,16 +310,14 @@
     return high, (x - high.astype(jnp.float32)).astype(jnp.bfloat16)
 
 
-def product(x, high, low, dims):
-    def dot(p, q):
-        return lax.dot_general(p, q, (dims, ((), ())), preferred_element_type=jnp.float32)
-
+def product(x, high, low):
     x_high, x_low = split(x)
-    both = dot(jnp.concatenate([x_high, x_low], axis=0), high)
-    return both[: x.shape[0]] + (both[x.shape[0] :] + dot(x_high, low))
-
-
-def filter_kernel(chunks_in, own, high, low, result_out):
+    both = jnp.dot(jnp.concatenate([x_high, x_low], axis=0), high, preferred_element_type=jnp.float32)
+    rest = jnp.dot(x_high, low, preferred_element_type=jnp.float32)
+    return both[: x.shape[0]] + (both[x.shape[0] :] + rest)
+
+
+def filter_kernel(chunks_in, own, waves, result_out):
     sectors, fields = chunks_in.shape[0], 6
     chunks = chunks_in.reshape(sectors * CHUNK, 128)
     result = result_out.reshape(sectors * CHUNK, 128)
@@ -347,9 +346,9 @@
         jnp.concatenate([jnp.concatenate(spectrum[8 * g + i], axis=1) for i in range(8)], axis=0)
         for g in groups
     ]
-    modes = [product(rows[g], high[g], low[g], ((1,), (0,))) for g in groups]
+    modes = [product(rows[g], waves[g], waves[3 + g]) for g in groups]
     modes = [jnp.where(block == column, modes[g] * own[g : g + 1, :], 0.0) for g in groups]
-    rows = [product(modes[g], high[g], low[g], ((1,), (1,))) for g in groups]
+    rows = [product(modes[g], waves[6 + g], waves[9 + g]) for g in groups]
     for g in groups:
         for i in range(8):
             part = rows[g][8 * i : 8 * i + 8, :]
@@ -405,6 +404,8 @@
     fields = state.reshape(item_count, lat_cells, lon_cells)
     zonal, merid = (w.reshape(lat_cells, lon_cells) for w in (zonal_wind, meridional_wind))
     high, low, reduced, scale = mode_layout(circle, circle // 16)
+    waves = [high, low, high.transpose(0, 2, 1), low.transpose(0, 2, 1)]
+    waves = jnp.asarray(np.concatenate(waves))
 
     modes = np.concatenate([np.pad(rows, ((0, 8 - GROUPS), (0, 0))) for rows in (reduced, scale)])
     modes = jnp.asarray(modes.astype(np.float32))
@@ -430,15 +431,15 @@
     ring = [(i, i + 2) for i in range(0, band_total - 2, 2)] + [(band_total - 2, band_total - 1)]
     ring += [(i, i - 2) for i in range(3, band_total, 2)] + [(1, 0)]
     passed = lax.ppermute(passing, "lat", ring)
-    part, own, fields, metric = call(
+    part, own, fields, metric, waves = call(
         increment_kernel,
         "increments",
-        [packed, own, fields, metric],
-        4,
-        here,
-        7,
+        [packed, own, fields, metric, waves],
+        6,
+        (*here, waves),
+        8,
         [pltpu.VMEM(x.shape, x.dtype) for x in (zonal, merid, flags, counts, modes)]
-        + [pad, pltpu.SemaphoreType.DMA((item_count + 6,))],
+        + [pad, pltpu.SemaphoreType.DMA((item_count + 7,))],
     )
     (chunks,) = call(
         border_fluxes_kernel, "border_fluxes", [packed], 4, (part, borders, chip, passed, metric)
@@ -449,7 +450,7 @@
         "filter_rows",
         [packed],
         8,
-        (chunks, own, jnp.asarray(high), jnp.asarray(low)),
+        (chunks, own, waves),
     )
     chunks = lax.all_to_all(chunks, "lon", 0, 0, tiled=True)
     (advanced,) = call(final_kernel, "advance", [fields], 4, (chunks, fields))

time: 35.6 us -> 35.5 us (level)
  transfers between devices with their start and end apart: 1 -> 1, of which waited for: 1 -> 1; matrix products, arithmetic and copies ran while one was open for 0% -> 0% of each run, Pallas kernels for 4% -> 5%
where the time goes in v10:
time: 35.5 us; the launch traced here: 35.2 us
  blocking collectives  27.9 us (79%)
  Pallas kernels  4.09 us (12%)
  waiting for transfers between devices  2.2 us (6%)
  starting transfers between devices  1.03 us (3%)
    all_to_all x2, blocking collectives, body(): chunks = lax.all_to_all(chunks, 'lon', 0, 0, tiled=True)  26 us
    pallas_call x6, Pallas kernels, call(): pl.pallas_call(kernel, out_shape=[jax.ShapeDtypeStruct(out.shape, out.dty...  4.09 us
    ppermute x1, waiting for transfers between devices, body(): passed = lax.ppermute(passing, 'lat', ring)  2.2 us
    all_gather x1, blocking collectives, body(): lax.all_gather(borders, 'lat', axis=0, tiled=True, axis_index_groups=cores)  1.84 us
    ppermute x1, starting transfers between devices, body(): passed = lax.ppermute(passing, 'lat', ring)  1.03 us
  transfers between devices with their start and end apart: 1, of which 1 were waited for; matrix products, arithmetic and copies ran while one was open for 0% of the time, Pallas kernels for 5%

profile of v10, /device:TPU:384, one launch (start us, length us, event | category | flops | bytes accessed | tf_op | source)
XLA Modules:
  0.0 35.2 jit_solution(679255410489959920)
XLA Ops:
  0.0 0.8 %borders.1 = f32[48,128]{1,0:T(8,128)S(1)} custom-call(f32[6,16,360]{2,1,0:T(8,128)} %bitcast.8, f32[16,360]{1,0:T(8,128)} %bitcast.10), custom_call_target="tpu_custom_call" | custom-call | tf_op jit(solution)/shard_map/borders/pallas_call | solution.py:387
  0.8 1.8 %all_gather.3.chip = f32[96,128]{1,0:T(8,128)S(1)} all-gather(f32[48,128]{1,0:T(8,128)S(1)} %borders.1), channel_id=1, replica_groups={{0,16},{32,48},{64,80},{96,112},{128,144},{160,176},{192,208},{224,240}..., dimensions={0}, use_global_device_ids=true | all-gather | bytes 73728 | tf_op jit(solution)/shard_map/all_gather | solution.py:429
  2.7 1.0 %collective-permute-start = (f32[24,128]{1,0:T(8,128)S(1)}, f32[24,128]{1,0:T(8,128)S(1)}, u32[]{:S(2)}, u32[]{:S(2)}) collective-permute-start(f32[24,128]{1,0:T(8,128)S(1)} %passing.1), channel_id=1, source_target_pairs={{0,32},{32,64},{64,96},{96,128},{128,160},{160,192},{192,224},{224... | collective-permute-start | bytes 36872 | tf_op jit(solution)/shard_map/ppermute | solution.py:433
  3.7 1.7 %increments.1 = (f32[16,9,2,128]{3,2,1,0:T(2,128)S(1)}, f32[16,256]{1,0:T(8,128)S(1)}, f32[6,16,360]{2,1,0:T(8,128)S(1)}, f32[16,128]{1,0:T(8,128)S(1)}, bf16[12,256,256]{2,1,0:T(8,128)(2,1)S(1)}) custom-call(f32[6,16,360]{2,1,0:T(8,128)} %bitcast.9, f32[16,360]{1,0:T(8,128)} %bitcast.12, f32[16,360]{1,0:T(8,128)} %bitcast.11, ...), custom_call_target="tpu_custom_call" | custom-call | tf_op jit(solution)/shard_map/increments/pallas_call | solution.py:387
  5.4 2.2 %collective-permute-done.passed = f32[24,128]{1,0:T(8,128)S(1)} collective-permute-done((f32[24,128]{1,0:T(8,128)S(1)}, f32[24,128]{1,0:T(8,128)S(1)}, u32[]{:S(2)}, u32[]{:S(2)}) %collective-permute-start) | collective-permute-done | bytes 12320 | tf_op jit(solution)/shard_map/ppermute | solution.py:433
  7.6 0.1 border_fluxes.1
  7.7 14.7 %all_to_all.10.chunks_in = f32[16,9,2,128]{3,2,1,0:T(2,128)S(1)} all-to-all(f32[16,9,2,128]{3,2,1,0:T(2,128)S(1)} %border_fluxes.1), channel_id=1, replica_groups=mesh['lat'=32,'lon'=16] {'lon'}, dimensions={0} | all-to-all | bytes 294912 | tf_op jit(solution)/shard_map/all_to_all | solution.py:447
  22.4 0.7 %filter_rows.1 = f32[16,9,2,128]{3,2,1,0:T(2,128)S(1)} custom-call(f32[16,9,2,128]{3,2,1,0:T(2,128)S(1)} %all_to_all.10.chunks_in, f32[16,256]{1,0:T(8,128)S(1)} %get-tuple-element.12.own, bf16[12,256,256]{2,1,0:T(8,128)(2,1)S(1)} %get-tuple-element.13.waves), custom_call_target="tpu_custom_call" | custom-call | tf_op jit(solution)/shard_map/filter_rows/pallas_call | solution.py:387
  23.1 11.3 %all_to_all.11.chunks_in = f32[16,9,2,128]{3,2,1,0:T(2,128)S(1)} all-to-all(f32[16,9,2,128]{3,2,1,0:T(2,128)S(1)} %filter_rows.1), channel_id=1, replica_groups=mesh['lat'=32,'lon'=16] {'lon'}, dimensions={0} | all-to-all | bytes 294912 | tf_op jit(solution)/shard_map/all_to_all | solution.py:455
  34.5 0.8 %advance.1 = f32[6,16,360]{2,1,0:T(8,128)} custom-call(f32[16,9,2,128]{3,2,1,0:T(2,128)S(1)} %all_to_all.11.chunks_in, f32[6,16,360]{2,1,0:T(8,128)S(1)} %get-tuple-element.14.state), custom_call_target="tpu_custom_call" | custom-call | tf_op jit(solution)/shard_map/advance/pallas_call | solution.py:387
  (1 shorter events, 0.0 us)
Async XLA Ops:
  2.7 4.9 %collective-permute-start = (f32[24,128]{1,0:T(8,128)S(1)}, f32[24,128]{1,0:T(8,128)S(1)}, u32[]{:S(2)}, u32[]{:S(2)}) collective-permute-start(f32[24,128]{1,0:T(8,128)S(1)} %passing.1), channel_id=1, source_target_pairs={{0,32},{32,64},{64,96},{96,128},{128,160},{160,192},{192,224},{224... | collective-permute-start | bytes 36872 | tf_op jit(solution)/shard_map/ppermute | solution.py:433

commit v11 on v10

--- a/solution.py
+++ b/solution.py
@@ -242,7 +242,8 @@
 
     zonal_factor, merid_factor, face = (spread(i) for i in range(3))
     east_wind = pad[fields]
-    last_wind = pltpu.roll(east_wind, 3, 1)
+    last_shift = SLAB - (cells - 1 - (wide - 128))
+    last_wind = 0.5 * pltpu.roll(east_wind[:, wide - 128 :], last_shift, 1)
     inner_wind = jnp.where(lane < cells - 1, east_wind, 0.0)
     north_wind = jnp.where(row < rows - 1, pad[fields + 1] * face, 0.0)
     for f in range(fields):
@@ -252,10 +253,9 @@
         flux_north = north_wind * (0.5 * (q + pltpu.roll(q, rows - 1, 0)))
         merid_diff = flux_north - pltpu.roll(flux_north, 1, 0)
         part = -zonal_factor * zonal_diff - merid_factor * merid_diff
-        part = jnp.where(lane == cells, pltpu.roll(q, cells, 1), part)
-        part = jnp.where(lane == cells + 1, pltpu.roll(q, 2, 1), part)
-        part = jnp.where(lane == cells + 2, last_wind, part)
+        edges = (last_wind, pltpu.roll(q[:, wide - 128 :], last_shift, 1), pltpu.roll(q[:, :128], SLAB, 1))
         for a, slab in enumerate(slabs_of(part)):
+            slab = jnp.where(lane[:, :128] == SLAB, edges[a], slab)
             chunks[pl.ds(fields * a + f, rows, stride=CHUNK), :] = slab
     place = lax.broadcasted_iota(jnp.int32, flags.shape, 0) * 128 + lax.broadcasted_iota(jnp.int32, flags.shape, 1)
     chosen = place == band * rows + sector
@@ -325,15 +325,13 @@
     zonal_factor = own[8:, :128]
     points = [chunks[fields * p : fields * p + 8, :] for p in range(POINTS - 1)]
     points.append(pltpu.roll(chunks[sectors * CHUNK - 8 :, :], 6, 0))
-    lasts = [points[3 * s + 2] for s in range(sectors)]
+    came = list(points)
     for s in range(sectors):
         after = (s + 1) % sectors
-        flux = pltpu.roll(lasts[s], 125, 1) * (
-            0.5 * (pltpu.roll(lasts[s], 126, 1) + pltpu.roll(lasts[after], 127, 1))
-        )
-        edge = jnp.where(lane == SLAB - 1, zonal_factor * flux, 0.0)
-        points[3 * s + 2] = points[3 * s + 2] - edge
-        points[3 * after] = points[3 * after] + pltpu.roll(edge, 128 - (SLAB - 1), 1)
+        flux = came[3 * s] * (came[3 * s + 1] + came[3 * after + 2])
+        edge = jnp.where(lane == SLAB, zonal_factor * flux, 0.0)
+        points[3 * s + 2] = points[3 * s + 2] - pltpu.roll(edge, 127, 1)
+        points[3 * after] = points[3 * after] + pltpu.roll(edge, 128 - SLAB, 1)
     for p in range(POINTS):
         result[fields * p : fields * (p + 1), :] = points[p][:fields]
     spectrum = circle_forward(points)

time: 35.5 us -> 35.4 us (level)
  no operation moved by 1% of the time
where the time goes in v11:
time: 35.4 us; the launch traced here: 35.2 us
  blocking collectives  27.9 us (79%)
  Pallas kernels  4.02 us (11%)
  waiting for transfers between devices  2.2 us (6%)
  starting transfers between devices  1.03 us (3%)
    all_to_all x2, blocking collectives, body(): chunks = lax.all_to_all(chunks, 'lon', 0, 0, tiled=True)  26 us
    pallas_call x6, Pallas kernels, call(): pl.pallas_call(kernel, out_shape=[jax.ShapeDtypeStruct(out.shape, out.dty...  4.02 us
    ppermute x1, waiting for transfers between devices, body(): passed = lax.ppermute(passing, 'lat', ring)  2.2 us
    all_gather x1, blocking collectives, body(): lax.all_gather(borders, 'lat', axis=0, tiled=True, axis_index_groups=cores)  1.84 us
    ppermute x1, starting transfers between devices, body(): passed = lax.ppermute(passing, 'lat', ring)  1.03 us
  transfers between devices with their start and end apart: 1, of which 1 were waited for; matrix products, arithmetic and copies ran while one was open for 0% of the time, Pallas kernels for 5%

profile of v11, /device:TPU:384, one launch (start us, length us, event | category | flops | bytes accessed | tf_op | source)
XLA Modules:
  0.0 35.2 jit_solution(9625072986031803782)
XLA Ops:
  0.0 0.8 %borders.1 = f32[48,128]{1,0:T(8,128)S(1)} custom-call(f32[6,16,360]{2,1,0:T(8,128)} %bitcast.8, f32[16,360]{1,0:T(8,128)} %bitcast.10), custom_call_target="tpu_custom_call" | custom-call | tf_op jit(solution)/shard_map/borders/pallas_call | solution.py:385
  0.8 1.8 %all_gather.3.chip = f32[96,128]{1,0:T(8,128)S(1)} all-gather(f32[48,128]{1,0:T(8,128)S(1)} %borders.1), channel_id=1, replica_groups={{0,16},{32,48},{64,80},{96,112},{128,144},{160,176},{192,208},{224,240}..., dimensions={0}, use_global_device_ids=true | all-gather | bytes 73728 | tf_op jit(solution)/shard_map/all_gather | solution.py:427
  2.7 1.0 %collective-permute-start = (f32[24,128]{1,0:T(8,128)S(1)}, f32[24,128]{1,0:T(8,128)S(1)}, u32[]{:S(2)}, u32[]{:S(2)}) collective-permute-start(f32[24,128]{1,0:T(8,128)S(1)} %passing.1), channel_id=1, source_target_pairs={{0,32},{32,64},{64,96},{96,128},{128,160},{160,192},{192,224},{224... | collective-permute-start | bytes 36872 | tf_op jit(solution)/shard_map/ppermute | solution.py:431
  3.7 1.7 %increments.1 = (f32[16,9,2,128]{3,2,1,0:T(2,128)S(1)}, f32[16,256]{1,0:T(8,128)S(1)}, f32[6,16,360]{2,1,0:T(8,128)S(1)}, f32[16,128]{1,0:T(8,128)S(1)}, bf16[12,256,256]{2,1,0:T(8,128)(2,1)S(1)}) custom-call(f32[6,16,360]{2,1,0:T(8,128)} %bitcast.9, f32[16,360]{1,0:T(8,128)} %bitcast.12, f32[16,360]{1,0:T(8,128)} %bitcast.11, ...), custom_call_target="tpu_custom_call" | custom-call | tf_op jit(solution)/shard_map/increments/pallas_call | solution.py:385
  5.4 2.2 %collective-permute-done.passed = f32[24,128]{1,0:T(8,128)S(1)} collective-permute-done((f32[24,128]{1,0:T(8,128)S(1)}, f32[24,128]{1,0:T(8,128)S(1)}, u32[]{:S(2)}, u32[]{:S(2)}) %collective-permute-start) | collective-permute-done | bytes 12320 | tf_op jit(solution)/shard_map/ppermute | solution.py:431
  7.6 0.1 border_fluxes.1
  7.7 14.7 %all_to_all.10.chunks_in = f32[16,9,2,128]{3,2,1,0:T(2,128)S(1)} all-to-all(f32[16,9,2,128]{3,2,1,0:T(2,128)S(1)} %border_fluxes.1), channel_id=1, replica_groups=mesh['lat'=32,'lon'=16] {'lon'}, dimensions={0} | all-to-all | bytes 294912 | tf_op jit(solution)/shard_map/all_to_all | solution.py:445
  22.4 0.6 %filter_rows.1 = f32[16,9,2,128]{3,2,1,0:T(2,128)S(1)} custom-call(f32[16,9,2,128]{3,2,1,0:T(2,128)S(1)} %all_to_all.10.chunks_in, f32[16,256]{1,0:T(8,128)S(1)} %get-tuple-element.12.own, bf16[12,256,256]{2,1,0:T(8,128)(2,1)S(1)} %get-tuple-element.13.waves), custom_call_target="tpu_custom_call" | custom-call | tf_op jit(solution)/shard_map/filter_rows/pallas_call | solution.py:385
  23.1 11.3 %all_to_all.11.chunks_in = f32[16,9,2,128]{3,2,1,0:T(2,128)S(1)} all-to-all(f32[16,9,2,128]{3,2,1,0:T(2,128)S(1)} %filter_rows.1), channel_id=1, replica_groups=mesh['lat'=32,'lon'=16] {'lon'}, dimensions={0} | all-to-all | bytes 294912 | tf_op jit(solution)/shard_map/all_to_all | solution.py:453
  34.4 0.8 %advance.1 = f32[6,16,360]{2,1,0:T(8,128)} custom-call(f32[16,9,2,128]{3,2,1,0:T(2,128)S(1)} %all_to_all.11.chunks_in, f32[6,16,360]{2,1,0:T(8,128)S(1)} %get-tuple-element.14.state), custom_call_target="tpu_custom_call" | custom-call | tf_op jit(solution)/shard_map/advance/pallas_call | solution.py:385
  (1 shorter events, 0.0 us)
Async XLA Ops:
  2.7 4.9 %collective-permute-start = (f32[24,128]{1,0:T(8,128)S(1)}, f32[24,128]{1,0:T(8,128)S(1)}, u32[]{:S(2)}, u32[]{:S(2)}) collective-permute-start(f32[24,128]{1,0:T(8,128)S(1)} %passing.1), channel_id=1, source_target_pairs={{0,32},{32,64},{64,96},{96,128},{128,160},{160,192},{192,224},{224... | collective-permute-start | bytes 36872 | tf_op jit(solution)/shard_map/ppermute | solution.py:431

commit v12 on v11

--- a/solution.py
+++ b/solution.py
@@ -317,7 +317,7 @@
     return both[: x.shape[0]] + (both[x.shape[0] :] + rest)
 
 
-def filter_kernel(chunks_in, own, waves, result_out):
+def filter_kernel(chunks_in, own, waves, high, low, result_out):
     sectors, fields = chunks_in.shape[0], 6
     chunks = chunks_in.reshape(sectors * CHUNK, 128)
     result = result_out.reshape(sectors * CHUNK, 128)
@@ -344,9 +344,9 @@
         jnp.concatenate([jnp.concatenate(spectrum[8 * g + i], axis=1) for i in range(8)], axis=0)
         for g in groups
     ]
-    modes = [product(rows[g], waves[g], waves[3 + g]) for g in groups]
+    modes = [product(rows[g], high[g], low[g]) for g in groups]
     modes = [jnp.where(block == column, modes[g] * own[g : g + 1, :], 0.0) for g in groups]
-    rows = [product(modes[g], waves[6 + g], waves[9 + g]) for g in groups]
+    rows = [product(modes[g], waves[g], waves[3 + g]) for g in groups]
     for g in groups:
         for i in range(8):
             part = rows[g][8 * i : 8 * i + 8, :]
@@ -402,7 +402,7 @@
     fields = state.reshape(item_count, lat_cells, lon_cells)
     zonal, merid = (w.reshape(lat_cells, lon_cells) for w in (zonal_wind, meridional_wind))
     high, low, reduced, scale = mode_layout(circle, circle // 16)
-    waves = [high, low, high.transpose(0, 2, 1), low.transpose(0, 2, 1)]
+    waves = [high.transpose(0, 2, 1), low.transpose(0, 2, 1)]
     waves = jnp.asarray(np.concatenate(waves))
 
     modes = np.concatenate([np.pad(rows, ((0, 8 - GROUPS), (0, 0))) for rows in (reduced, scale)])
@@ -448,7 +448,7 @@
         "filter_rows",
         [packed],
         8,
-        (chunks, own, waves),
+        (chunks, own, waves, jnp.asarray(high), jnp.asarray(low)),
     )
     chunks = lax.all_to_all(chunks, "lon", 0, 0, tiled=True)
     (advanced,) = call(final_kernel, "advance", [fields], 4, (chunks, fields))

time: 35.4 us -> 35.4 us (level)
  transfers between devices with their start and end apart: 1 -> 1, of which waited for: 1 -> 1; matrix products, arithmetic and copies ran while one was open for 0% -> 0% of each run, Pallas kernels for 5% -> 4%
where the time goes in v12:
time: 35.4 us; the launch traced here: 35.2 us
  blocking collectives  27.9 us (79%)
  Pallas kernels  3.79 us (11%)
  waiting for transfers between devices  2.41 us (7%)
  starting transfers between devices  1.03 us (3%)
    all_to_all x2, blocking collectives, body(): chunks = lax.all_to_all(chunks, 'lon', 0, 0, tiled=True)  26 us
    pallas_call x6, Pallas kernels, call(): pl.pallas_call(kernel, out_shape=[jax.ShapeDtypeStruct(out.shape, out.dty...  3.79 us
    ppermute x1, waiting for transfers between devices, body(): passed = lax.ppermute(passing, 'lat', ring)  2.41 us
    all_gather x1, blocking collectives, body(): lax.all_gather(borders, 'lat', axis=0, tiled=True, axis_index_groups=cores)  1.84 us
    ppermute x1, starting transfers between devices, body(): passed = lax.ppermute(passing, 'lat', ring)  1.03 us
  transfers between devices with their start and end apart: 1, of which 1 were waited for; matrix products, arithmetic and copies ran while one was open for 0% of the time, Pallas kernels for 4%

profile of v12, /device:TPU:384, one launch (start us, length us, event | category | flops | bytes accessed | tf_op | source)
XLA Modules:
  0.0 35.2 jit_solution(6543042917761380665)
XLA Ops:
  0.0 0.8 %borders.1 = f32[48,128]{1,0:T(8,128)S(1)} custom-call(f32[6,16,360]{2,1,0:T(8,128)} %bitcast.8, f32[16,360]{1,0:T(8,128)} %bitcast.10), custom_call_target="tpu_custom_call" | custom-call | tf_op jit(solution)/shard_map/borders/pallas_call | solution.py:385
  0.8 1.8 %all_gather.3.chip = f32[96,128]{1,0:T(8,128)S(1)} all-gather(f32[48,128]{1,0:T(8,128)S(1)} %borders.1), channel_id=1, replica_groups={{0,16},{32,48},{64,80},{96,112},{128,144},{160,176},{192,208},{224,240}..., dimensions={0}, use_global_device_ids=true | all-gather | bytes 73728 | tf_op jit(solution)/shard_map/all_gather | solution.py:427
  2.7 1.0 %collective-permute-start = (f32[24,128]{1,0:T(8,128)S(1)}, f32[24,128]{1,0:T(8,128)S(1)}, u32[]{:S(2)}, u32[]{:S(2)}) collective-permute-start(f32[24,128]{1,0:T(8,128)S(1)} %passing.1), channel_id=1, source_target_pairs={{0,32},{32,64},{64,96},{96,128},{128,160},{160,192},{192,224},{224... | collective-permute-start | bytes 36872 | tf_op jit(solution)/shard_map/ppermute | solution.py:431
  3.7 0.0 copy-start.1
  3.7 1.5 %increments.1 = (f32[16,9,2,128]{3,2,1,0:T(2,128)S(1)}, f32[16,256]{1,0:T(8,128)S(1)}, f32[6,16,360]{2,1,0:T(8,128)S(1)}, f32[16,128]{1,0:T(8,128)S(1)}, bf16[6,256,256]{2,1,0:T(8,128)(2,1)S(1)}) custom-call(f32[6,16,360]{2,1,0:T(8,128)} %bitcast.9, f32[16,360]{1,0:T(8,128)} %bitcast.12, f32[16,360]{1,0:T(8,128)} %bitcast.11, ...), custom_call_target="tpu_custom_call" | custom-call | tf_op jit(solution)/shard_map/increments/pallas_call | solution.py:385
  5.2 0.0 copy-start
  5.2 2.4 %collective-permute-done.passed = f32[24,128]{1,0:T(8,128)S(1)} collective-permute-done((f32[24,128]{1,0:T(8,128)S(1)}, f32[24,128]{1,0:T(8,128)S(1)}, u32[]{:S(2)}, u32[]{:S(2)}) %collective-permute-start) | collective-permute-done | bytes 12320 | tf_op jit(solution)/shard_map/ppermute | solution.py:431
  7.6 0.1 border_fluxes.1
  7.7 14.7 %all_to_all.10.chunks_in = f32[16,9,2,128]{3,2,1,0:T(2,128)S(1)} all-to-all(f32[16,9,2,128]{3,2,1,0:T(2,128)S(1)} %border_fluxes.1), channel_id=1, replica_groups=mesh['lat'=32,'lon'=16] {'lon'}, dimensions={0} | all-to-all | bytes 294912 | tf_op jit(solution)/shard_map/all_to_all | solution.py:445
  22.4 0.0 copy-done.1
  22.4 0.0 copy-done
  22.5 0.6 %filter_rows.1 = f32[16,9,2,128]{3,2,1,0:T(2,128)S(1)} custom-call(f32[16,9,2,128]{3,2,1,0:T(2,128)S(1)} %all_to_all.10.chunks_in, f32[16,256]{1,0:T(8,128)S(1)} %get-tuple-element.12.own, bf16[6,256,256]{2,1,0:T(8,128)(2,1)S(1)} %get-tuple-element.13.waves, bf16[3,256,256]{2,1,0:T(8,128)(2,1)S(1)} %copy-done.1, bf16[3,256,256]{2,1,0:T(8,128)(2,1)S(1)} %copy-done), custom_call_target="tpu_custom_call" | custom-call | tf_op jit(solution)/shard_map/filter_rows/pallas_call | solution.py:385
  23.1 11.3 %all_to_all.11.chunks_in = f32[16,9,2,128]{3,2,1,0:T(2,128)S(1)} all-to-all(f32[16,9,2,128]{3,2,1,0:T(2,128)S(1)} %filter_rows.1), channel_id=1, replica_groups=mesh['lat'=32,'lon'=16] {'lon'}, dimensions={0} | all-to-all | bytes 294912 | tf_op jit(solution)/shard_map/all_to_all | solution.py:453
  34.4 0.8 %advance.1 = f32[6,16,360]{2,1,0:T(8,128)} custom-call(f32[16,9,2,128]{3,2,1,0:T(2,128)S(1)} %all_to_all.11.chunks_in, f32[6,16,360]{2,1,0:T(8,128)S(1)} %get-tuple-element.14.state), custom_call_target="tpu_custom_call" | custom-call | tf_op jit(solution)/shard_map/advance/pallas_call | solution.py:385
  (1 shorter events, 0.0 us)
Async XLA Ops:
  2.7 4.9 %collective-permute-start = (f32[24,128]{1,0:T(8,128)S(1)}, f32[24,128]{1,0:T(8,128)S(1)}, u32[]{:S(2)}, u32[]{:S(2)}) collective-permute-start(f32[24,128]{1,0:T(8,128)S(1)} %passing.1), channel_id=1, source_target_pairs={{0,32},{32,64},{64,96},{96,128},{128,160},{160,192},{192,224},{224... | collective-permute-start | bytes 36872 | tf_op jit(solution)/shard_map/ppermute | solution.py:431
  3.7 18.7 %copy-start.1 = (bf16[3,256,256]{2,1,0:T(8,128)(2,1)S(1)}, bf16[3,256,256]{2,1,0:T(8,128)(2,1)}, u32[]{:S(2)}) copy-start(bf16[3,256,256]{2,1,0:T(8,128)(2,1)} %constant.13.clone.high) | copy-start | bytes 1179652
  5.2 17.3 %copy-start = (bf16[3,256,256]{2,1,0:T(8,128)(2,1)S(1)}, bf16[3,256,256]{2,1,0:T(8,128)(2,1)}, u32[]{:S(2)}) copy-start(bf16[3,256,256]{2,1,0:T(8,128)(2,1)} %constant.14.clone.low) | copy-start | bytes 1179652

commit v13 on v11

--- a/solution.py
+++ b/solution.py
@@ -78,6 +78,18 @@
     return (x[0], None if x[1] is None else -x[1])
 
 
+def c_sub_conj(x, y):
+    if x[1] is None or y[1] is None:
+        return c_conj(c_sub(x, y)) if y[1] is None else (x[0] - y[0], y[1])
+    return (x[0] - y[0], y[1] - x[1])
+
+
+def c_mirror(x, y):
+    if x[1] is None or y[1] is None:
+        return c_add(x, c_conj(y)), c_sub(x, c_conj(y))
+    return (x[0] + y[0], x[1] - y[1]), (x[0] - y[0], x[1] + y[1])
+
+
 def c_turn(x, numer, denom):
     numer %= denom
     eighth = 8 * numer
@@ -112,7 +124,7 @@
         turned = c_turn(odd[k], -k, count)
         result[k] = c_add(even[k], turned)
         if k != count // 4 or count == 2:
-            result[count // 2 - k] = c_conj(c_sub(even[k], turned))
+            result[count // 2 - k] = c_sub_conj(even[k], turned)
     return result
 
 
@@ -122,9 +134,9 @@
         return [z[0][0] + z[1][0], z[0][0] - z[1][0]]
     even, odd = [], []
     for k in range(count // 4 + 1):
-        mirror = c_conj(z[count // 2 - k])
-        even.append(c_add(z[k], mirror))
-        odd.append(c_turn(c_sub(z[k], mirror), k, count))
+        total, gap = c_mirror(z[k], z[count // 2 - k])
+        even.append(total)
+        odd.append(c_turn(gap, k, count))
     result = [None] * count
     result[0::2], result[1::2] = irfft(even), irfft(odd)
     return result

time: 35.4 us -> 35.4 us (level)
  no operation moved by 1% of the time
where the time goes in v13:
time: 35.4 us; the launch traced here: 35.2 us
  blocking collectives  27.9 us (79%)
  Pallas kernels  4.01 us (11%)
  waiting for transfers between devices  2.2 us (6%)
  starting transfers between devices  1.03 us (3%)
    all_to_all x2, blocking collectives, body(): chunks = lax.all_to_all(chunks, 'lon', 0, 0, tiled=True)  26 us
    pallas_call x6, Pallas kernels, call(): pl.pallas_call(kernel, out_shape=[jax.ShapeDtypeStruct(out.shape, out.dty...  4.01 us
    ppermute x1, waiting for transfers between devices, body(): passed = lax.ppermute(passing, 'lat', ring)  2.2 us
    all_gather x1, blocking collectives, body(): lax.all_gather(borders, 'lat', axis=0, tiled=True, axis_index_groups=cores)  1.84 us
    ppermute x1, starting transfers between devices, body(): passed = lax.ppermute(passing, 'lat', ring)  1.03 us
  transfers between devices with their start and end apart: 1, of which 1 were waited for; matrix products, arithmetic and copies ran while one was open for 0% of the time, Pallas kernels for 5%

profile of v13, /device:TPU:384, one launch (start us, length us, event | category | flops | bytes accessed | tf_op | source)
XLA Modules:
  0.0 35.2 jit_solution(10521395909716764315)
XLA Ops:
  0.0 0.8 %borders.1 = f32[48,128]{1,0:T(8,128)S(1)} custom-call(f32[6,16,360]{2,1,0:T(8,128)} %bitcast.8, f32[16,360]{1,0:T(8,128)} %bitcast.10), custom_call_target="tpu_custom_call" | custom-call | tf_op jit(solution)/shard_map/borders/pallas_call | solution.py:397
  0.8 1.8 %all_gather.3.chip = f32[96,128]{1,0:T(8,128)S(1)} all-gather(f32[48,128]{1,0:T(8,128)S(1)} %borders.1), channel_id=1, replica_groups={{0,16},{32,48},{64,80},{96,112},{128,144},{160,176},{192,208},{224,240}..., dimensions={0}, use_global_device_ids=true | all-gather | bytes 73728 | tf_op jit(solution)/shard_map/all_gather | solution.py:439
  2.7 1.0 %collective-permute-start = (f32[24,128]{1,0:T(8,128)S(1)}, f32[24,128]{1,0:T(8,128)S(1)}, u32[]{:S(2)}, u32[]{:S(2)}) collective-permute-start(f32[24,128]{1,0:T(8,128)S(1)} %passing.1), channel_id=1, source_target_pairs={{0,32},{32,64},{64,96},{96,128},{128,160},{160,192},{192,224},{224... | collective-permute-start | bytes 36872 | tf_op jit(solution)/shard_map/ppermute | solution.py:443
  3.7 1.7 %increments.1 = (f32[16,9,2,128]{3,2,1,0:T(2,128)S(1)}, f32[16,256]{1,0:T(8,128)S(1)}, f32[6,16,360]{2,1,0:T(8,128)S(1)}, f32[16,128]{1,0:T(8,128)S(1)}, bf16[12,256,256]{2,1,0:T(8,128)(2,1)S(1)}) custom-call(f32[6,16,360]{2,1,0:T(8,128)} %bitcast.9, f32[16,360]{1,0:T(8,128)} %bitcast.12, f32[16,360]{1,0:T(8,128)} %bitcast.11, ...), custom_call_target="tpu_custom_call" | custom-call | tf_op jit(solution)/shard_map/increments/pallas_call | solution.py:397
  5.4 2.2 %collective-permute-done.passed = f32[24,128]{1,0:T(8,128)S(1)} collective-permute-done((f32[24,128]{1,0:T(8,128)S(1)}, f32[24,128]{1,0:T(8,128)S(1)}, u32[]{:S(2)}, u32[]{:S(2)}) %collective-permute-start) | collective-permute-done | bytes 12320 | tf_op jit(solution)/shard_map/ppermute | solution.py:443
  7.6 0.1 border_fluxes.1
  7.7 14.7 %all_to_all.10.chunks_in = f32[16,9,2,128]{3,2,1,0:T(2,128)S(1)} all-to-all(f32[16,9,2,128]{3,2,1,0:T(2,128)S(1)} %border_fluxes.1), channel_id=1, replica_groups=mesh['lat'=32,'lon'=16] {'lon'}, dimensions={0} | all-to-all | bytes 294912 | tf_op jit(solution)/shard_map/all_to_all | solution.py:457
  22.4 0.6 %filter_rows.1 = f32[16,9,2,128]{3,2,1,0:T(2,128)S(1)} custom-call(f32[16,9,2,128]{3,2,1,0:T(2,128)S(1)} %all_to_all.10.chunks_in, f32[16,256]{1,0:T(8,128)S(1)} %get-tuple-element.12.own, bf16[12,256,256]{2,1,0:T(8,128)(2,1)S(1)} %get-tuple-element.13.waves), custom_call_target="tpu_custom_call" | custom-call | tf_op jit(solution)/shard_map/filter_rows/pallas_call | solution.py:397
  23.1 11.3 %all_to_all.11.chunks_in = f32[16,9,2,128]{3,2,1,0:T(2,128)S(1)} all-to-all(f32[16,9,2,128]{3,2,1,0:T(2,128)S(1)} %filter_rows.1), channel_id=1, replica_groups=mesh['lat'=32,'lon'=16] {'lon'}, dimensions={0} | all-to-all | bytes 294912 | tf_op jit(solution)/shard_map/all_to_all | solution.py:465
  34.4 0.8 %advance.1 = f32[6,16,360]{2,1,0:T(8,128)} custom-call(f32[16,9,2,128]{3,2,1,0:T(2,128)S(1)} %all_to_all.11.chunks_in, f32[6,16,360]{2,1,0:T(8,128)S(1)} %get-tuple-element.14.state), custom_call_target="tpu_custom_call" | custom-call | tf_op jit(solution)/shard_map/advance/pallas_call | solution.py:397
  (1 shorter events, 0.0 us)
Async XLA Ops:
  2.7 4.9 %collective-permute-start = (f32[24,128]{1,0:T(8,128)S(1)}, f32[24,128]{1,0:T(8,128)S(1)}, u32[]{:S(2)}, u32[]{:S(2)}) collective-permute-start(f32[24,128]{1,0:T(8,128)S(1)} %passing.1), channel_id=1, source_target_pairs={{0,32},{32,64},{64,96},{96,128},{128,160},{160,192},{192,224},{224... | collective-permute-start | bytes 36872 | tf_op jit(solution)/shard_map/ppermute | solution.py:443
